TPU v7x, 32 devices: a whole 2x2x4 slice. The times are simulated.
32 devices in a mesh: dp: 8 (over z, y), row: 2 (over core), col: 2 (over x).
Axes of the slice: x: 2, y: 2, z: 4, core: 2. Of those that a mesh axis runs over, the one named last changes fastest.
Arguments:
- block_input: bfloat16 [384, 32768], P(('row', 'col'), 'dp'), may hold values from -6 to 6
- condition: float32 [128, 384], P('dp', 'col'), may hold values from -6 to 6
- w_ada: bfloat16 [384, 2304], P('col', 'row'), may hold values from -0.3125 to 0.3125
- b_ada: bfloat16 [6, 384], P(None, ('row', 'col')), may hold values from -3 to 3
- w_qkv: bfloat16 [384, 1152], P('row', 'col'), may hold values from -0.3125 to 0.3125
- b_qkv: bfloat16 [2, 384], P(None, 'col'), may hold values from -3 to 3
- w_proj: bfloat16 [384, 384], P('col', 'row'), may hold values from -2.5 to 2.5
- b_proj: bfloat16 [384], P(('row', 'col')), may hold values from -3 to 3
- w_fc1: bfloat16 [384, 1536], P('row', 'col'), may hold values from -0.3125 to 0.3125
- b_fc1: bfloat16 [1536], P('col'), may hold values from -3 to 3
- w_fc2: bfloat16 [384, 1536], P('row', 'col'), may hold values from -0.15625 to 0.15625
- b_fc2: bfloat16 [384], P(('row', 'col')), may hold values from -3 to 3
- out_grad: bfloat16 [384, 32768], P(('row', 'col'), 'dp'), may hold values from -6 to 6
Outputs:
- block_output: float32 [384, 32768], P(('row', 'col'), 'dp')
- input_grad: float32 [384, 32768], P(('row', 'col'), 'dp')
- cond_grad: float32 [128, 384], P('dp', 'col')
- grad_w_ada: float32 [384, 2304], P('col', 'row')
- grad_b_ada: float32 [6, 384], P(None, ('row', 'col'))
- grad_w_qkv: float32 [384, 1152], P('row', 'col')
- grad_b_qkv: float32 [2, 384], P(None, 'col')
- grad_w_proj: float32 [384, 384], P('col', 'row')
- grad_b_proj: float32 [384], P(('row', 'col'))
- grad_w_fc1: float32 [384, 1536], P('row', 'col')
- grad_b_fc1: float32 [1536], P('col')
- grad_w_fc2: float32 [384, 1536], P('row', 'col')
- grad_b_fc2: float32 [384], P(('row', 'col'))
All inputs are finite; a program needn't handle non-finite values.
Results may differ from a plain program's by a relative error of at most 0.012.
The roundings to bfloat16 on the way count: a program that leaves them out, or rounds other values in their place, can miss the bound.
Values may be sent and summed in bfloat16 or wider, within the bound.
No kernel may reach another device: no remote copies, remote signals or barrier semaphores. Data moves between devices by JAX's collectives and lax.ppermute only.
A program may use at most 128 MiB of HBM per device.

v0:
```python
from functools import partial

import jax
import jax.numpy as jnp
from jax import lax
from jax.sharding import PartitionSpec as P

D = 384
HEADS = 6
HD = 64


EPSILON = 1e-06


def shortened(shard):
    return jax.tree.map(lambda a: a.astype(jnp.bfloat16) if a.dtype == jnp.float32 else a, shard)


def gather_features(value, dim):
    return lax.all_gather(value, "col", axis=dim, tiled=True)


def sum_features(value, dim):
    return lax.psum_scatter(value, "col", scatter_dimension=dim, tiled=True)


def gather_tokens(value):
    return lax.all_gather(shortened(value), "row", axis=1, tiled=True).astype(value.dtype)


def sum_tokens(value):
    return lax.psum_scatter(value, "row", scatter_dimension=1, tiled=True)


def norm_totals(first, second):
    return lax.psum((first, second), ("row", "col"))


def cond_totals(value):
    return lax.psum(value, "row")


def contract(left, right, left_dim, right_dim):
    return lax.dot_general(
        left, right, (((left_dim,), (right_dim,)), ((), ())), preferred_element_type=jnp.float32
    )


def layer_norm(value):
    first, second = norm_totals(jnp.sum(value, axis=0), jnp.sum(value * value, axis=0))
    center = first / D
    variance = second / D - center * center
    inverse = lax.rsqrt(variance + EPSILON)
    return ((value - center[None, :]) * inverse[None, :], inverse)


def norm_back(grad, normed, inverse):
    first, second = norm_totals(jnp.sum(grad, axis=0), jnp.sum(grad * normed, axis=0))
    return inverse[None, :] * (grad - first[None, :] / D - normed * (second[None, :] / D))


def layer(
    block_input,
    cond_low,
    w_ada,
    b_ada,
    w_qkv,
    b_qkv,
    w_proj,
    b_proj,
    w_fc1,
    b_fc1,
    w_fc2,
    b_fc2,
    out_grad,
):
    f32 = jnp.float32
    bf16 = jnp.bfloat16
    latents = cond_low.shape[0]
    token_count = block_input.shape[1]
    seq_len = token_count // latents
    col_count = lax.axis_size("col")
    row_count = lax.axis_size("row")
    heads_here = HEADS // col_count
    lat_half = latents // row_count
    scale = HD ** (-0.5)

    def modulate(value, factor):
        width = value.shape[0]
        return (value.reshape(width, latents, seq_len) * factor.T[:, :, None]).reshape(value.shape)

    def affine(value, factor, offset):
        width = value.shape[0]
        shaped = (
            value.reshape(width, latents, seq_len) * factor.T[:, :, None] + offset.T[:, :, None]
        )
        return shaped.reshape(value.shape)

    def latent_sum(value):
        width = value.shape[0]
        return jnp.sum(value.reshape(width, latents, seq_len), axis=2).T

    ada_part = jnp.dot(cond_low, w_ada, preferred_element_type=f32).reshape(latents, -1, 6)
    modulation = jnp.transpose(sum_features(ada_part, 1), (0, 2, 1)) + b_ada.astype(f32)[None]
    shift_one = modulation[:, 0]
    scale_one = modulation[:, 1]
    gate_one = modulation[:, 2]
    shift_two = modulation[:, 3]
    scale_two = modulation[:, 4]
    gate_two = modulation[:, 5]
    input_f = block_input.astype(f32)
    normed_one, inverse_one = layer_norm(input_f)
    mod_one = affine(normed_one, 1.0 + scale_one, shift_one)
    feats_one = gather_features(mod_one.astype(bf16), 0)
    qkv_all = sum_tokens(contract(w_qkv, feats_one, 0, 0))
    half_rows = qkv_all.shape[1]
    qkv_heads = qkv_all.reshape(3, heads_here, HD, half_rows)
    bias_qkv = b_qkv.astype(f32).reshape(2, heads_here, HD, 1)
    query = (qkv_heads[0] + bias_qkv[0]).astype(bf16).reshape(heads_here, HD, lat_half, seq_len)
    keys_low = qkv_heads[1].astype(bf16).reshape(heads_here, HD, lat_half, seq_len)
    values_low = (
        (qkv_heads[2] + bias_qkv[1]).astype(bf16).reshape(heads_here, HD, lat_half, seq_len)
    )
    scores = jnp.einsum("helq,helk->lhqk", query, keys_low, preferred_element_type=f32) * scale
    log_total = jax.nn.logsumexp(scores, axis=-1)
    probs = jnp.exp(scores - log_total[..., None])
    attended = jnp.einsum(
        "lhqk,helk->helq", probs.astype(bf16), values_low, preferred_element_type=f32
    )
    attended = attended.reshape(-1, half_rows).astype(bf16)
    context = gather_tokens(attended)
    attn_branch = sum_features(contract(w_proj, context, 0, 0), 0) + b_proj.astype(f32)[:, None]
    hidden_state = input_f + modulate(attn_branch, gate_one)
    normed_two, inverse_two = layer_norm(hidden_state)
    mod_two = affine(normed_two, 1.0 + scale_two, shift_two)
    feats_two = gather_features(mod_two.astype(bf16), 0)
    pre_act = sum_tokens(contract(w_fc1, feats_two, 0, 0)) + b_fc1.astype(f32)[:, None]
    activated, gelu_back = jax.vjp(partial(jax.nn.gelu, approximate=True), pre_act)
    act_full = gather_tokens(activated.astype(bf16))
    mlp_branch = (
        sum_features(jnp.dot(w_fc2, act_full, preferred_element_type=f32), 0)
        + b_fc2.astype(f32)[:, None]
    )
    block_output = hidden_state + modulate(mlp_branch, gate_two)
    out_f = out_grad.astype(f32)
    grad_gate_two = latent_sum(out_f * mlp_branch)
    mlp_grad = modulate(out_f, gate_two).astype(bf16)
    grad_b_fc2 = jnp.sum(mlp_grad.astype(f32), axis=1)
    mlp_grad_full = gather_features(mlp_grad, 0)
    grad_w_fc2 = contract(mlp_grad_full, act_full, 1, 1)
    act_grad = sum_tokens(contract(w_fc2, mlp_grad_full, 0, 0))
    pre_grad = gelu_back(act_grad)[0].astype(bf16)
    pre_full = gather_tokens(pre_grad)
    grad_w_fc1 = contract(feats_two, pre_full, 1, 1)
    grad_b_fc1 = jnp.sum(pre_full.astype(f32), axis=1)
    mod_two_grad = sum_features(jnp.dot(w_fc1, pre_full, preferred_element_type=f32), 0)
    grad_shift_two = latent_sum(mod_two_grad)
    grad_scale_two = latent_sum(mod_two_grad * normed_two)
    hidden_grad = out_f + norm_back(
        modulate(mod_two_grad, 1.0 + scale_two), normed_two, inverse_two
    )
    early = None
    grad_gate_one = latent_sum(hidden_grad * attn_branch)
    branch_grad = modulate(hidden_grad, gate_one).astype(bf16)
    grad_b_proj = jnp.sum(branch_grad.astype(f32), axis=1)
    branch_full = gather_features(branch_grad, 0)
    grad_w_proj = contract(context, branch_full, 1, 1)
    context_grad = sum_tokens(jnp.dot(w_proj, branch_full, preferred_element_type=f32))
    context_grad = context_grad.astype(bf16).reshape(heads_here, HD, lat_half, seq_len)
    scores_again = (
        jnp.einsum("helq,helk->lhqk", query, keys_low, preferred_element_type=f32) * scale
    )
    probs_again = jnp.exp(scores_again - log_total[..., None])
    prob_grad = jnp.einsum("helq,helk->lhqk", context_grad, values_low, preferred_element_type=f32)
    values_grad = jnp.einsum(
        "lhqk,helq->helk", probs_again.astype(bf16), context_grad, preferred_element_type=f32
    )
    row_dot = jnp.sum(prob_grad * probs_again, axis=-1)
    score_grad = (probs_again * (prob_grad - row_dot[..., None])).astype(bf16)
    query_grad = (
        jnp.einsum("lhqk,helk->helq", score_grad, keys_low, preferred_element_type=f32) * scale
    )
    keys_grad = jnp.einsum("lhqk,helq->helk", score_grad, query, preferred_element_type=f32) * scale
    qkv_grad = (
        jnp.stack([query_grad, keys_grad, values_grad], axis=0).reshape(-1, half_rows).astype(bf16)
    )
    qkv_full = gather_tokens(qkv_grad)
    grad_w_qkv = contract(feats_one, qkv_full, 1, 1)
    column_sums = jnp.sum(qkv_full.astype(f32), axis=1).reshape(3, -1)
    grad_b_qkv = jnp.stack([column_sums[0], column_sums[2]], axis=0)
    mod_one_grad = sum_features(jnp.dot(w_qkv, qkv_full, preferred_element_type=f32), 0)
    grad_shift_one = latent_sum(mod_one_grad)
    grad_scale_one = latent_sum(mod_one_grad * normed_one)
    input_grad = hidden_grad + norm_back(
        modulate(mod_one_grad, 1.0 + scale_one), normed_one, inverse_one
    )
    mod_grad = jnp.stack(
        [
            grad_shift_one,
            grad_scale_one,
            grad_gate_one,
            grad_shift_two,
            grad_scale_two,
            grad_gate_two,
        ],
        axis=1,
    ).astype(bf16)
    grad_b_ada = jnp.sum(mod_grad.astype(f32), axis=0)
    mod_full = gather_features(jnp.transpose(mod_grad, (0, 2, 1)), 1).reshape(latents, -1)
    grad_w_ada = jnp.dot(cond_low.T, mod_full, preferred_element_type=f32)
    cond_total = cond_totals(contract(mod_full, w_ada, 1, 1))
    grads = (
        grad_w_ada,
        grad_b_ada,
        grad_w_qkv,
        grad_b_qkv,
        grad_w_proj,
        grad_b_proj,
        grad_w_fc1,
        grad_b_fc1,
        grad_w_fc2,
        grad_b_fc2,
    )
    return (block_output, input_grad, cond_total, grads, early)


def local(
    block_input,
    condition,
    w_ada,
    b_ada,
    w_qkv,
    b_qkv,
    w_proj,
    b_proj,
    w_fc1,
    b_fc1,
    w_fc2,
    b_fc2,
    out_grad,
):
    bf16 = jnp.bfloat16
    silu_value, silu_back = jax.vjp(jax.nn.silu, condition)
    cond_local = silu_value.astype(bf16)
    results = layer(
        block_input,
        cond_local,
        w_ada,
        b_ada,
        w_qkv,
        b_qkv,
        w_proj,
        b_proj,
        w_fc1,
        b_fc1,
        w_fc2,
        b_fc2,
        out_grad,
    )
    block_output, input_grad, cond_here, grads, early = results
    cond_grad = silu_back(cond_here)[0]
    (
        grad_w_ada,
        grad_b_ada,
        grad_w_qkv,
        grad_b_qkv,
        grad_w_proj,
        grad_b_proj,
        grad_w_fc1,
        grad_b_fc1,
        grad_w_fc2,
        grad_b_fc2,
    ) = grads
    all_sums = lax.psum(
        (
            grad_w_ada,
            grad_b_ada,
            grad_w_qkv,
            grad_b_qkv,
            grad_w_proj,
            grad_b_proj,
            grad_w_fc1,
            grad_b_fc1,
            grad_w_fc2,
            grad_b_fc2,
        ),
        "dp",
    )
    (
        sums_w_ada,
        sums_b_ada,
        sums_w_qkv,
        sums_b_qkv,
        sums_w_proj,
        sums_b_proj,
        sums_w_fc1,
        sums_b_fc1,
        sums_w_fc2,
        sums_b_fc2,
    ) = all_sums
    return (
        block_output,
        input_grad,
        cond_grad,
        sums_w_ada,
        sums_b_ada,
        sums_w_qkv,
        sums_b_qkv,
        sums_w_proj,
        sums_b_proj,
        sums_w_fc1,
        sums_b_fc1,
        sums_w_fc2,
        sums_b_fc2,
    )


def solution(mesh):
    return jax.shard_map(
        local,
        mesh=mesh,
        in_specs=(
            P(("row", "col"), "dp"),
            P("dp", "col"),
            P("col", "row"),
            P(None, ("row", "col")),
            P("row", "col"),
            P(None, "col"),
            P("col", "row"),
            P(("row", "col")),
            P("row", "col"),
            P("col"),
            P("row", "col"),
            P(("row", "col")),
            P(("row", "col"), "dp"),
        ),
        out_specs=(
            P(("row", "col"), "dp"),
            P(("row", "col"), "dp"),
            P("dp", "col"),
            P("col", "row"),
            P(None, ("row", "col")),
            P("row", "col"),
            P(None, "col"),
            P("col", "row"),
            P(("row", "col")),
            P("row", "col"),
            P("col"),
            P("row", "col"),
            P(("row", "col")),
        ),
        check_vma=False,
    )
```

profile of v0, /device:TPU:0, one launch (start us, length us, event | category | flops | bytes accessed | tf_op | source)
XLA Modules:
  0.0 713.6 jit_solution(13672466653062948679)
XLA Ops:
  10.6 14.3 %all-reduce.5 = (f32[4096]{0:T(1024)S(1)}, f32[4096]{0:T(1024)S(1)}) all-reduce(f32[4096]{0:T(1024)S(1)} %get-tuple-element.20, f32[4096]{0:T(1024)S(1)} %get-tuple-element.19), channel_id=1, replica_groups=mesh['dp'=8,'row'=2,'col'=2] {'row','col'}, use_global_device_ids=true, to_apply=%region_3.4 | all-reduce | flops 8192 | bytes 65536 | tf_op jit(solution)/shard_map/psum | solution.py:37
  30.4 28.3 %all-gather.9.cloned.1.call-done = bf16[192,4096]{1,0:T(8,128)(2,1)} async-done(((bf16[96,4096]{1,0:T(8,128)(2,1)}), bf16[192,4096]{1,0:T(8,128)(2,1)}) %all-gather.9.cloned.1.call-update) | async-done | bytes 1572880 | tf_op jit(solution)/shard_map/all_gather | solution.py:21
  58.7 6.5 convolution_bitcast_fusion.2
  66.0 17.1 %reduce-scatter.12.cloned.1.call-done = f32[576,2048]{1,0:T(8,128)} async-done(((f32[576,4096]{1,0:T(8,128)}), f32[576,2048]{1,0:T(8,128)}) %reduce-scatter.12.cloned.1.call-update) | async-done | bytes 4718608 | tf_op jit(solution)/shard_map/reduce_scatter | solution.py:33
  95.5 11.2 %all-gather.11.cloned.1.call-done = bf16[192,4096]{1,0:T(8,128)(2,1)} async-done(((bf16[192,2048]{1,0:T(8,128)(2,1)}), bf16[192,4096]{1,0:T(8,128)(2,1)}) %all-gather.11.cloned.1.call-update) | async-done | bytes 1572880 | tf_op jit(solution)/shard_map/all_gather | solution.py:29
  122.3 32.8 %reduce-scatter.14.cloned.1.call-done = f32[96,4096]{1,0:T(8,128)} async-done(((f32[192,4096]{1,0:T(8,128)}), f32[96,4096]{1,0:T(8,128)}) %reduce-scatter.14.cloned.1.call-update) | async-done | bytes 1572880 | tf_op jit(solution)/shard_map/reduce_scatter | solution.py:25
  157.4 12.0 %all-reduce.4 = (f32[4096]{0:T(1024)S(1)}, f32[4096]{0:T(1024)S(1)}) all-reduce(f32[4096]{0:T(1024)S(1)} %get-tuple-element.18, f32[4096]{0:T(1024)S(1)} %get-tuple-element.17), channel_id=1, replica_groups=mesh['dp'=8,'row'=2,'col'=2] {'row','col'}, use_global_device_ids=true, to_apply=%region_12.13 | all-reduce | flops 8192 | bytes 65536 | tf_op jit(solution)/shard_map/psum | solution.py:37
  172.6 12.1 %all-gather.17.cloned.1.call-done = bf16[192,4096]{1,0:T(8,128)(2,1)} async-done(((bf16[96,4096]{1,0:T(8,128)(2,1)}), bf16[192,4096]{1,0:T(8,128)(2,1)}) %all-gather.17.cloned.1.call-update) | async-done | bytes 1572880 | tf_op jit(solution)/shard_map/all_gather | solution.py:21
  184.7 7.8 %convolution_bitcast_fusion = f32[768,4096]{0,1:T(8,128)} fusion(bf16[192,4096]{1,0:T(8,128)(2,1)} %all-gather.17.cloned.1.call-done, bf16[192,768]{1,0:T(8,128)(2,1)S(1)} %copy-done.28), kind=kOutput, calls=%fused_computation.5 | convolution fusion | flops 1207959552 | bytes 14450688 | tf_op jit(solution)/shard_map/dot_general | solution.py:45
  192.5 21.0 %all-gather.13.cloned.1.call-done = bf16[192,4096]{1,0:T(8,128)(2,1)} async-done(((bf16[96,4096]{1,0:T(8,128)(2,1)}), bf16[192,4096]{1,0:T(8,128)(2,1)}) %all-gather.13.cloned.1.call-update) | async-done | bytes 1572880 | tf_op jit(solution)/shard_map/all_gather | solution.py:21
  213.5 7.7 %convolution_bitcast_fusion.1 = f32[768,4096]{0,1:T(8,128)} fusion(bf16[192,4096]{1,0:T(8,128)(2,1)} %all-gather.13.cloned.1.call-done, bf16[192,768]{1,0:T(8,128)(2,1)S(1)} %copy-done.27), kind=kOutput, calls=%fused_computation.6 | convolution fusion | flops 1207959552 | bytes 14450688 | tf_op jit(solution)/shard_map/dot_general | solution.py:45
  222.0 15.5 %reduce-scatter.20.cloned.1.call-done = f32[768,2048]{0,1:T(8,128)} async-done(((f32[768,4096]{0,1:T(8,128)}), f32[768,2048]{0,1:T(8,128)}) %reduce-scatter.20.cloned.1.call-update) | async-done | bytes 6291472 | tf_op jit(solution)/shard_map/reduce_scatter | solution.py:33
  237.4 25.1 %reduce-scatter.16.cloned.1.call-done = f32[768,2048]{0,1:T(8,128)} async-done(((f32[768,4096]{0,1:T(8,128)}), f32[768,2048]{0,1:T(8,128)}) %reduce-scatter.16.cloned.1.call-update) | async-done | bytes 6291472 | tf_op jit(solution)/shard_map/reduce_scatter | solution.py:33
  262.5 9.5 %fusion.7 = (bf16[768,2048]{0,1:T(8,128)(2,1)}, bf16[768,2048]{0,1:T(8,128)(2,1)}) fusion(f32[768,2048]{0,1:T(8,128)} %reduce-scatter.20.cloned.1.call-done, f32[768,2048]{0,1:T(8,128)} %reduce-scatter.16.cloned.1.call-done, f32[768]{0:T(1024)S(1)} %convert_element_type.108), kind=kLoop, calls=%fused_computation.14 | loop fusion | flops 36175872 | bytes 18877440 | tf_op jit(solution)/shard_map/convert_element_type | solution.py:153
  272.8 17.3 %all-gather.19.cloned.1.call-done = bf16[768,4096]{0,1:T(8,128)(2,1)} async-done(((bf16[768,2048]{0,1:T(8,128)(2,1)}), bf16[768,4096]{0,1:T(8,128)(2,1)}) %all-gather.19.cloned.1.call-update) | async-done | bytes 6291472 | tf_op jit(solution)/shard_map/all_gather | solution.py:29
  290.1 6.6 convolution_bitcast_fusion.5
  296.8 12.9 %all-gather.15.cloned.1.call-done = bf16[768,4096]{0,1:T(8,128)(2,1)} async-done(((bf16[768,2048]{0,1:T(8,128)(2,1)}), bf16[768,4096]{0,1:T(8,128)(2,1)}) %all-gather.15.cloned.1.call-update) | async-done | bytes 6291472 | tf_op jit(solution)/shard_map/all_gather | solution.py:29
  309.7 6.6 convolution_bitcast_fusion.6
  316.9 39.5 %reduce-scatter.22.cloned.1.call-done = f32[96,4096]{1,0:T(8,128)} async-done(((f32[192,4096]{1,0:T(8,128)}), f32[96,4096]{1,0:T(8,128)}) %reduce-scatter.22.cloned.1.call-update) | async-done | bytes 1572880 | tf_op jit(solution)/shard_map/reduce_scatter | solution.py:25
  360.5 12.5 %all-reduce.3 = (f32[4096]{0:T(1024)S(1)}, f32[4096]{0:T(1024)S(1)}) all-reduce(f32[4096]{0:T(1024)S(1)} %get-tuple-element.16, f32[4096]{0:T(1024)S(1)} %get-tuple-element.15), channel_id=1, replica_groups=mesh['dp'=8,'row'=2,'col'=2] {'row','col'}, use_global_device_ids=true, to_apply=%region_20.21 | all-reduce | flops 8192 | bytes 65536 | tf_op jit(solution)/shard_map/psum | solution.py:37
  373.0 29.7 %reduce-scatter.18.cloned.1.call-done = f32[96,4096]{1,0:T(8,128)} async-done(((f32[192,4096]{1,0:T(8,128)}), f32[96,4096]{1,0:T(8,128)}) %reduce-scatter.18.cloned.1.call-update) | async-done | bytes 1572880 | tf_op jit(solution)/shard_map/reduce_scatter | solution.py:25
  402.7 6.4 convert_multiply_fusion.1
  409.2 27.3 %all-gather.21.cloned.1.call-done = bf16[192,4096]{1,0:T(8,128)(2,1)} async-done(((bf16[96,4096]{1,0:T(8,128)(2,1)}), bf16[192,4096]{1,0:T(8,128)(2,1)}) %all-gather.21.cloned.1.call-update) | async-done | bytes 1572880 | tf_op jit(solution)/shard_map/all_gather | solution.py:21
  440.4 10.8 %reduce-scatter.24.cloned.1.call-done = f32[192,2048]{1,0:T(8,128)} async-done(((f32[192,4096]{1,0:T(8,128)}), f32[192,2048]{1,0:T(8,128)}) %reduce-scatter.24.cloned.1.call-update) | async-done | bytes 1572880 | tf_op jit(solution)/shard_map/reduce_scatter | solution.py:33
  457.9 9.1 %multiply_convert_fusion = bf16[8,3,256,256]{2,3,1,0:T(8,128)(2,1)} fusion(f32[8,3,256,256]{2,3,1,0:T(8,128)} %fusion.62, f32[8,3,256,256]{2,3,1,0:T(8,128)S(1)} %bitcast.169, f32[8,3,256]{2,1,0:T(4,128)} %copy-done.33), kind=kOutput, calls=%fused_computation.15 | output fusion | flops 12589311 | bytes 15753216 | tf_op jit(solution)/shard_map/sub | solution.py:180
  476.8 15.7 %all-gather.23.cloned.1.call-done = bf16[576,4096]{1,0:T(8,128)(2,1)} async-done(((bf16[576,2048]{1,0:T(8,128)(2,1)}), bf16[576,4096]{1,0:T(8,128)(2,1)}) %all-gather.23.cloned.1.call-update) | async-done | bytes 4718608 | tf_op jit(solution)/shard_map/all_gather | solution.py:29
  503.8 6.2 fusion.85
  527.2 15.3 %reduce-scatter.26.cloned.1.call-done = f32[96,4096]{1,0:T(8,128)} async-done(((f32[192,4096]{1,0:T(8,128)}), f32[96,4096]{1,0:T(8,128)}) %reduce-scatter.26.cloned.1.call-update) | async-done | bytes 1572880 | tf_op jit(solution)/shard_map/reduce_scatter | solution.py:25
  552.6 11.9 %all-reduce.2 = (f32[4096]{0:T(1024)S(1)}, f32[4096]{0:T(1024)S(1)}) all-reduce(f32[4096]{0:T(1024)S(1)} %get-tuple-element.14, f32[4096]{0:T(1024)S(1)} %get-tuple-element.13), channel_id=1, replica_groups=mesh['dp'=8,'row'=2,'col'=2] {'row','col'}, use_global_device_ids=true, to_apply=%region_27.28 | all-reduce | flops 8192 | bytes 65536 | tf_op jit(solution)/shard_map/psum | solution.py:37
  569.2 8.3 %all_gather.35 = bf16[16,192,6]{0,2,1:T(8,128)(2,1)S(1)} all-gather(bf16[16,96,6]{0,2,1:T(8,128)(2,1)S(1)} %copy.194), channel_id=1, replica_groups=mesh['dp'=8,'row'=2,'col'=2] {'col'}, dimensions={1}, use_global_device_ids=true | all-gather | bytes 55296 | tf_op jit(solution)/shard_map/all_gather | solution.py:21
  585.8 39.0 %all-reduce = (f32[6,96]{1,0:T(8,128)}, f32[2,192]{1,0:T(2,128)}, f32[96]{0:T(128)}, f32[768]{0:T(1024)}, f32[96]{0:T(128)}) all-reduce(f32[6,96]{1,0:T(8,128)S(1)} %convert_reduce_fusion.5, f32[2,192]{1,0:T(2,128)S(1)} %pad_maximum_fusion.1, f32[96]{0:T(128)S(1)} %copy-done.41, ...), channel_id=1, replica_groups=mesh['dp'=8,'row'=2,'col'=2] {'dp'}, use_global_device_ids=true, to_apply=%region_37.38 | all-reduce | flops 1920 | bytes 15360 | tf_op jit(solution)/shard_map/psum | solution.py:275
  629.1 72.1 %all-reduce.8.cloned.1.call-done = (f32[192,1152]{1,0:T(8,128)}, f32[192,576]{1,0:T(8,128)}, f32[192,192]{1,0:T(8,128)}, f32[192,768]{1,0:T(8,128)}, f32[192,768]{1,0:T(8,128)}) async-done(((f32[192,1152]{1,0:T(8,128)}, f32[192,576]{1,0:T(8,128)}, f32[192,192]{1,0:T(8,128)}, f32[192,768]{1,0:T(8,128)}, f32[192,768]{1,0:T(8,128)}), (f32[192,1152]{1,0:T(8,128)}, f32[192,576]{1,0:T(8,128)}, ...) | async-done | bytes 2654224 | tf_op jit(solution)/shard_map/psum | solution.py:275
  (255 shorter events, 130.4 us)
Async XLA Ops:
  7.2 17.8 %reduce-scatter.28.cloned.1.call-start = ((), (), s32[]{:S(2)}) async-start(), calls=%async_computation.25 | async-start | bytes 147456
  10.2 48.4 %all-gather.9.cloned.1.call-start = ((), (), s32[]{:S(2)}) async-start(), calls=%async_computation.9 | async-start | bytes 2359296 | tf_op jit(solution)/shard_map/all_gather | solution.py:21
  29.1 29.6 %copy-start.25 = (bf16[192,576]{1,0:T(8,128)(2,1)S(1)}, bf16[192,576]{1,0:T(8,128)(2,1)}, u32[]{:S(2)}) copy-start(bf16[192,576]{1,0:T(8,128)(2,1)} %param.17) | copy-start | bytes 663556
  30.3 52.8 %reduce-scatter.12.cloned.1.call-start = ((), (), s32[]{:S(2)}) async-start(), calls=%async_computation.10 | async-start | bytes 14155776 | tf_op jit(solution)/shard_map/reduce_scatter | solution.py:33
  65.2 41.5 %all-gather.11.cloned.1.call-start = ((), (), s32[]{:S(2)}) async-start(), calls=%async_computation.11 | async-start | bytes 2359296 | tf_op jit(solution)/shard_map/all_gather | solution.py:29
  94.3 12.4 %copy-start.32 = (bf16[192,192]{1,0:T(8,128)(2,1)S(1)}, bf16[192,192]{1,0:T(8,128)(2,1)}, u32[]{:S(2)}) copy-start(bf16[192,192]{1,0:T(8,128)(2,1)} %param.19) | copy-start | bytes 221188
  95.4 59.6 %reduce-scatter.14.cloned.1.call-start = ((), (), s32[]{:S(2)}) async-start(), calls=%async_computation.12 | async-start | bytes 4718592 | tf_op jit(solution)/shard_map/reduce_scatter | solution.py:25
  110.3 74.3 %all-gather.17.cloned.1.call-start = ((), (), s32[]{:S(2)}) async-start(), calls=%async_computation.17 | async-start | bytes 2359296 | tf_op jit(solution)/shard_map/all_gather | solution.py:21
  111.0 44.0 %copy-start.42 = (f32[96]{0:T(128)}, f32[96]{0:T(128)S(1)}, u32[]{:S(2)}) copy-start(f32[96]{0:T(128)S(1)} %convert_element_type.106) | copy-start | bytes 1156
  122.2 91.3 %all-gather.13.cloned.1.call-start = ((), (), s32[]{:S(2)}) async-start(), calls=%async_computation.13 | async-start | bytes 2359296 | tf_op jit(solution)/shard_map/all_gather | solution.py:21
  169.4 15.3 %copy-start.28 = (bf16[192,768]{1,0:T(8,128)(2,1)S(1)}, bf16[192,768]{1,0:T(8,128)(2,1)}, u32[]{:S(2)}) copy-start(bf16[192,768]{1,0:T(8,128)(2,1)} %param.23) | copy-start | bytes 884740
  172.5 64.9 %reduce-scatter.20.cloned.1.call-start = ((), (), s32[]{:S(2)}) async-start(), calls=%async_computation.18 | async-start | bytes 18874368 | tf_op jit(solution)/shard_map/reduce_scatter | solution.py:33
  192.5 21.1 %copy-start.27 = (bf16[192,768]{1,0:T(8,128)(2,1)S(1)}, bf16[192,768]{1,0:T(8,128)(2,1)}, u32[]{:S(2)}) copy-start(bf16[192,768]{1,0:T(8,128)(2,1)} %param.21) | copy-start | bytes 884740
  192.5 70.0 %reduce-scatter.16.cloned.1.call-start = ((), (), s32[]{:S(2)}) async-start(), calls=%async_computation.14 | async-start | bytes 18874368 | tf_op jit(solution)/shard_map/reduce_scatter | solution.py:33
  221.3 68.8 %all-gather.19.cloned.1.call-start = ((), (), s32[]{:S(2)}) async-start(), calls=%async_computation.19 | async-start | bytes 9437184 | tf_op jit(solution)/shard_map/all_gather | solution.py:29
  272.0 37.7 %all-gather.15.cloned.1.call-start = ((), (), s32[]{:S(2)}) async-start(), calls=%async_computation.15 | async-start | bytes 9437184 | tf_op jit(solution)/shard_map/all_gather | solution.py:29
  272.8 83.7 %reduce-scatter.22.cloned.1.call-start = ((), (), s32[]{:S(2)}) async-start(), calls=%async_computation.20 | async-start | bytes 4718592 | tf_op jit(solution)/shard_map/reduce_scatter | solution.py:25
  296.7 106.0 %reduce-scatter.18.cloned.1.call-start = ((), (), s32[]{:S(2)}) async-start(), calls=%async_computation.16 | async-start | bytes 4718592 | tf_op jit(solution)/shard_map/reduce_scatter | solution.py:25
  316.3 120.2 %all-gather.21.cloned.1.call-start = ((), (), s32[]{:S(2)}) async-start(), calls=%async_computation.21 | async-start | bytes 2359296 | tf_op jit(solution)/shard_map/all_gather | solution.py:21
  316.9 85.8 %copy-start.19 = (bf16[96,4096]{1,0:T(8,128)(2,1)S(1)}, bf16[96,4096]{1,0:T(8,128)(2,1)}, u32[]{:S(2)}) copy-start(bf16[96,4096]{1,0:T(8,128)(2,1)} %param.25) | copy-start | bytes 2359300
  409.1 42.1 %reduce-scatter.24.cloned.1.call-start = ((), (), s32[]{:S(2)}) async-start(), calls=%async_computation.22 | async-start | bytes 4718592 | tf_op jit(solution)/shard_map/reduce_scatter | solution.py:33
  440.1 13.8 %copy-start.3 = (f32[24,8,8,256]{3,2,1,0:T(8,128)S(1)}, f32[24,8,8,256]{3,2,1,0:T(8,128)}, u32[]{:S(2)}) copy-start(f32[24,8,8,256]{3,2,1,0:T(8,128)} %copy-done.2) | copy-start | bytes 4718596
  440.2 52.3 %all-gather.23.cloned.1.call-start = ((), (), s32[]{:S(2)}) async-start(), calls=%async_computation.23 | async-start | bytes 7077888 | tf_op jit(solution)/shard_map/all_gather | solution.py:29
  476.7 15.8 %copy-start.26 = (bf16[192,576]{1,0:T(8,128)(2,1)S(1)}, bf16[192,576]{1,0:T(8,128)(2,1)}, u32[]{:S(2)}) copy-start(bf16[192,576]{1,0:T(8,128)(2,1)} %param.17) | copy-start | bytes 663556
  476.7 65.8 %reduce-scatter.26.cloned.1.call-start = ((), (), s32[]{:S(2)}) async-start(), calls=%async_computation.24 | async-start | bytes 4718592 | tf_op jit(solution)/shard_map/reduce_scatter | solution.py:25
  497.9 203.3 %all-reduce.8.cloned.1.call-start = ((), (), s32[]{:S(2)}) async-start(), calls=%async_computation.26 | async-start | bytes 5505024 | tf_op jit(solution)/shard_map/psum | solution.py:275
  522.1 20.5 %copy-start.5 = (bf16[96,4096]{1,0:T(8,128)(2,1)S(1)}, bf16[96,4096]{1,0:T(8,128)(2,1)}, u32[]{:S(2)}) copy-start(bf16[96,4096]{1,0:T(8,128)(2,1)} %param.13) | copy-start | bytes 2359300
  522.1 20.5 %copy-start.7 = (f32[12,8,16,256]{3,1,2,0:T(8,128)S(1)}, f32[12,8,16,256]{3,1,2,0:T(8,128)}, u32[]{:S(2)}) copy-start(f32[12,8,16,256]{3,1,2,0:T(8,128)} %copy-done.6) | copy-start | bytes 4718596
  522.1 20.5 %copy-start.36 = (f32[4096]{0:T(1024)S(1)}, f32[4096]{0:T(1024)}, u32[]{:S(2)}) copy-start(f32[4096]{0:T(1024)} %copy-done.35) | copy-start | bytes 49156
  522.1 20.5 %copy-start.38 = (f32[4096]{0:T(1024)S(1)}, f32[4096]{0:T(1024)}, u32[]{:S(2)}) copy-start(f32[4096]{0:T(1024)} %copy-done.37) | copy-start | bytes 49156
  550.7 13.8 %copy-start.16 = (f32[96,4096]{1,0:T(8,128)S(1)}, f32[96,4096]{1,0:T(8,128)}, u32[]{:S(2)}) copy-start(f32[96,4096]{1,0:T(8,128)} %get-tuple-element.59) | copy-start | bytes 4718596
  550.7 13.8 %copy-start.43 = (f32[96]{0:T(128)S(1)}, f32[96]{0:T(128)}, u32[]{:S(2)}) copy-start(f32[96]{0:T(128)} %copy-done.42) | copy-start | bytes 1156
  (38 other events, 107.4 us)
Sparse Core Ops, SparseCore 0:
  10.8 12.8 reduce-scatter.27
  30.4 28.1 all-gather.8
  65.3 17.7 reduce-scatter.11
  95.5 11.0 all-gather.10
  110.5 44.5 reduce-scatter.13
  157.1 27.5 all-gather.16
  186.3 27.1 all-gather.12
  215.9 21.4 reduce-scatter.19
  239.8 22.6 reduce-scatter.15
  272.1 17.8 all-gather.18
  291.7 17.9 all-gather.14
  311.9 44.5 reduce-scatter.21
  358.7 44.0 reduce-scatter.17
  409.3 27.2 all-gather.20
  440.3 10.9 reduce-scatter.23
  476.9 15.5 all-gather.22
  498.0 44.4 reduce-scatter.25
  579.1 122.0 all-reduce.7
where the time goes:
time: 719 us; the launch traced here: 714 us
  waiting for transfers between devices  405 us (56%)
  blocking collectives  101 us (14%)
  matrix products  82.1 us (11%)
  other arithmetic  62.7 us (9%)
  local copies, waits for them, and re-layouts  45.6 us (6%)
  between operations  15.3 us (2%)
    reduce_scatter x4, waiting for transfers between devices, sum_features(): return lax.psum_scatter(value, 'col', scatter_dimension=dim, tiled=True)  117 us
    all_gather x4, waiting for transfers between devices, gather_features(): return lax.all_gather(value, 'col', axis=dim, tiled=True)  88.7 us
    psum x1, waiting for transfers between devices, local(): lax.psum((grad_w_ada, grad_b_ada, grad_w_qkv, grad_b_qkv, grad_w_proj, gr...  72.1 us
    reduce_scatter x4, waiting for transfers between devices, sum_tokens(): return lax.psum_scatter(value, 'row', scatter_dimension=1, tiled=True)  68.5 us
    all_gather x4, waiting for transfers between devices, gather_tokens(): lax.all_gather(shortened(value), 'row', axis=1, tiled=True)  57.1 us
    psum x4, blocking collectives, norm_totals(): return lax.psum((first, second), ('row', 'col'))  50.7 us
    dot_general x9, matrix products, contract(): lax.dot_general(left, right, (((left_dim,), (right_dim,)), ((), ())), pre...  45.6 us
    psum x1, blocking collectives, local(): lax.psum((grad_w_ada, grad_b_ada, grad_w_qkv, grad_b_qkv, grad_w_proj, gr...  39 us
  transfers between devices with their start and end apart: 18, of which 17 were waited for; matrix products, arithmetic and copies ran while one was open for 12% of the time, Pallas kernels for 0%

commit v1 on v0

v1 whole, which is shorter than its diff:
```python
import jax
import jax.numpy as jnp
from jax import lax
from jax.experimental import pallas as pl
from jax.experimental.pallas import tpu as pltpu
from jax.sharding import PartitionSpec as P

D = 384
HEADS = 6
HD = 64
FF = 1536
GROUPS = 2
EPSILON = 1e-06
BF16 = jnp.bfloat16
F32 = jnp.float32
GROUP = ("row", "col")
VMEM_BYTES = 56 * 1024 * 1024


def dot_nn(left, right):
    return lax.dot_general(left, right, (((1,), (0,)), ((), ())), preferred_element_type=F32)


def dot_nt(left, right):
    return lax.dot_general(left, right, (((1,), (1,)), ((), ())), preferred_element_type=F32)


def dot_tn(left, right):
    return lax.dot_general(left, right, (((0,), (0,)), ((), ())), preferred_element_type=F32)


def lane_sum(value):
    return jnp.sum(value, axis=1, keepdims=True)


def lane_fold(value):
    parts = [value[:, at : at + 128] for at in range(0, value.shape[1], 128)]
    return sum(parts[1:], parts[0])


def norm_stats(value):
    center = jnp.sum(value, axis=0, keepdims=True) * (1.0 / D)
    square = jnp.sum(value * value, axis=0, keepdims=True) * (1.0 / D)
    inverse = lax.rsqrt(square - center * center + EPSILON)
    return (value - center) * inverse, inverse


def norm_back(grad, normed, inverse):
    first = jnp.sum(grad, axis=0, keepdims=True) * (1.0 / D)
    second = jnp.sum(grad * normed, axis=0, keepdims=True) * (1.0 / D)
    return inverse * (grad - first - normed * second)


PIECES = ((0, 0), (0, 1), (1, 0), (1, 1))


def place_split(pieces, target, pos):
    row, col = pos[0], pos[1]
    for piece, (step_row, step_col) in zip(pieces, PIECES):
        height = piece.shape[0]
        at = pl.multiple_of((row ^ step_row) * height, height)
        target[col ^ step_col, pl.ds(at, height), :] = piece[...]


def place_proj(pieces, target, pos):
    row, col = pos[0], pos[1]
    for piece, (step_row, step_col) in zip(pieces, PIECES):
        height = piece.shape[0]
        at = pl.multiple_of((col ^ step_col) * height, height)
        target[row ^ step_row, pl.ds(at, height), :] = piece[...]


def place_features(pieces, target, pos):
    own = pos[0] * 2 + pos[1]
    for step, piece in enumerate(pieces):
        height = piece.shape[0]
        at = pl.multiple_of((own ^ step) * height, height)
        target[pl.ds(at, height), :] = piece[...].astype(target.dtype)


def split_features(source, pieces, pos):
    own = pos[0] * 2 + pos[1]
    for step, piece in enumerate(pieces):
        height = piece.shape[0]
        at = pl.multiple_of((own ^ step) * height, height)
        piece[...] = source[pl.ds(at, height), :].astype(piece.dtype)


def attention_forward(
    pos, x0, x1, x2, x3, mod, wq0, wq1, wq2, wq3, wp0, wp1, wp2, wp3, bias_q, bias_v, bias_p,
    x_out, mod_one_out, qkv_out, probs_out, attended_out, branch_out,
    x_s, wq_s, wq_t, wp_s, wp_t,
):
    @pl.when(pl.program_id(0) == 0)
    def _():
        place_split((wq0, wq1, wq2, wq3), wq_s, pos)
        place_proj((wp0, wp1, wp2, wp3), wp_s, pos)
        for part in range(GROUPS):
            wq_t[part] = wq_s[part].T
            wp_t[part] = wp_s[part].T

    place_features((x0, x1, x2, x3), x_s, pos)
    x = x_s[...]
    x_out[...] = x.astype(BF16)
    normed, _ = norm_stats(x)
    mod_one = (normed * (1.0 + mod[0, :, 1:2]) + mod[0, :, 0:1]).astype(BF16)
    mod_one_out[...] = mod_one
    third = D // GROUPS
    for part in range(GROUPS):
        qkv = dot_nn(wq_t[part], mod_one)
        base = part * third
        query = (qkv[:third] + bias_q[base : base + third]).astype(BF16)
        keys = qkv[third : 2 * third].astype(BF16)
        values = (qkv[2 * third :] + bias_v[base : base + third]).astype(BF16)
        qkv_out[part, :third] = query
        qkv_out[part, third : 2 * third] = keys
        qkv_out[part, 2 * third :] = values
        scaled = query * jnp.asarray(HD ** (-0.5), BF16)
        for head in range(HEADS // GROUPS):
            rows = slice(head * HD, (head + 1) * HD)
            scores = dot_tn(keys[rows], scaled[rows])
            top = jnp.max(scores, axis=0, keepdims=True)
            raised = jnp.exp(scores - top)
            total = jnp.sum(raised, axis=0, keepdims=True)
            probs = (raised * (1.0 / total)).astype(BF16)
            probs_out[0, part * (HEADS // GROUPS) + head] = probs
            attended_out[base + head * HD : base + (head + 1) * HD] = dot_nn(
                values[rows], probs
            ).astype(BF16)
    attended = attended_out[...]
    for part in range(2):
        rows = slice(part * third, (part + 1) * third)
        branch_out[rows] = dot_nn(wp_t[part], attended) + bias_p[rows]


def mlp_forward(
    pos, x, branch, mod, w10, w11, w12, w13, w20, w21, w22, w23, bias_1, bias_2,
    out0, out1, out2, out3, mod_two_out, act_out, slope_out, mlp_out,
    w1_s, w1_t, w2_s, block_s,
):
    @pl.when(pl.program_id(0) == 0)
    def _():
        place_split((w10, w11, w12, w13), w1_s, pos)
        place_split((w20, w21, w22, w23), w2_s, pos)
        for part in range(GROUPS):
            w1_t[part] = w1_s[part].T

    hidden = x[...].astype(F32) + mod[0, :, 2:3] * branch[...]
    normed, _ = norm_stats(hidden)
    mod_two = (normed * (1.0 + mod[0, :, 4:5]) + mod[0, :, 3:4]).astype(BF16)
    mod_two_out[...] = mod_two
    half = FF // GROUPS
    slope = (2.0 / jnp.pi) ** 0.5
    total = None
    for part in range(GROUPS):
        rows = slice(part * half, (part + 1) * half)
        pre = dot_nn(w1_t[part], mod_two) + bias_1[rows]
        square = pre * pre
        tanh = jnp.tanh(slope * pre * (1.0 + 0.044715 * square))
        upper = 0.5 + 0.5 * tanh
        act = (pre * upper).astype(BF16)
        act_out[rows] = act
        slope_out[rows] = (
            upper
            + (0.5 * slope) * pre * (1.0 - tanh * tanh) * (1.0 + (3 * 0.044715) * square)
        ).astype(BF16)
        partial = dot_nn(w2_s[part], act)
        total = partial if total is None else total + partial
    mlp = total + bias_2[...]
    mlp_out[...] = mlp
    block_s[...] = hidden + mod[0, :, 5:6] * mlp
    split_features(block_s, (out0, out1, out2, out3), pos)


def mlp_backward(
    pos, g0, g1, g2, g3, x, branch, mod, mod_two, act, slope, mlp, attended,
    w10, w11, w12, w13, w20, w21, w22, w23, wp0, wp1, wp2, wp3,
    hidden_grad_out, context_out, mod_grad_out, send_out, keep_out, sum1_out, sum2_out, sump_out,
    g_s, w1_s, w2_s, w2_t, wp_s, acc1, acc2, accp, sum1, sum2, sump,
):
    step = pl.program_id(0)

    @pl.when(step == 0)
    def _():
        place_split((w10, w11, w12, w13), w1_s, pos)
        place_split((w20, w21, w22, w23), w2_s, pos)
        place_proj((wp0, wp1, wp2, wp3), wp_s, pos)
        for part in range(GROUPS):
            w2_t[part] = w2_s[part].T
        for acc in (acc1, acc2, accp, sum1, sum2, sump):
            acc[...] = jnp.zeros_like(acc)

    place_features((g0, g1, g2, g3), g_s, pos)
    grad = g_s[...]
    gate_one = mod[0, :, 2:3]
    gate_two = mod[0, :, 5:6]
    hidden = x[...].astype(F32) + gate_one * branch[...]
    normed, inverse = norm_stats(hidden)
    mod_grad_out[0, :, 3:4] = lane_sum(grad * mlp[...])
    mlp_grad = (gate_two * grad).astype(BF16)
    sum2[...] += lane_fold(mlp_grad.astype(F32))
    half = FF // GROUPS
    third = D // GROUPS
    mod_two_low = mod_two[...]
    back = None
    for part in range(GROUPS):
        rows = slice(part * half, (part + 1) * half)
        acc2[part] += dot_nt(mlp_grad, act[rows])
        pre_grad = (dot_nn(w2_t[part], mlp_grad) * slope[rows].astype(F32)).astype(BF16)
        sum1[rows] += lane_fold(pre_grad.astype(F32))
        acc1[part] += dot_nt(mod_two_low, pre_grad)
        partial = dot_nn(w1_s[part], pre_grad)
        back = partial if back is None else back + partial
    mod_grad_out[0, :, 1:2] = lane_sum(back)
    mod_grad_out[0, :, 2:3] = lane_sum(back * normed)
    hidden_grad = grad + norm_back(back * (1.0 + mod[0, :, 4:5]), normed, inverse)
    hidden_grad_out[...] = hidden_grad
    mod_grad_out[0, :, 0:1] = lane_sum(hidden_grad * branch[...])
    branch_grad = (gate_one * hidden_grad).astype(BF16)
    sump[...] += lane_fold(branch_grad.astype(F32))
    context = None
    for part in range(2):
        rows = slice(part * third, (part + 1) * third)
        accp[part] += dot_nt(attended[...], branch_grad[rows])
        partial = dot_nn(wp_s[part], branch_grad[rows])
        context = partial if context is None else context + partial
    context_out[...] = context.astype(BF16)

    @pl.when(step == pl.num_programs(0) - 1)
    def _():
        mine = pl.multiple_of(pos[0] * third, third)
        other = pl.multiple_of((1 - pos[0]) * third, third)
        for part in range(GROUPS):
            rows = slice(part * third, (part + 1) * third)
            for out, at, who in ((send_out, other, 1 - pos[0]), (keep_out, mine, pos[0])):
                out[part, :, :half] = acc1[part, pl.ds(at, third), :].astype(out.dtype)
                out[part, :, half : 2 * half] = acc2[part, pl.ds(at, third), :].astype(out.dtype)
                out[part, :, 2 * half :] = accp[who, rows, :].astype(out.dtype)
        sum1_out[...] = lane_sum(sum1[...])
        sum2_out[...] = lane_sum(sum2[...])
        sump_out[...] = lane_sum(sump[...])


def attention_backward(
    pos, x, mod_one, mod, qkv, probs, context, hidden_grad, wq0, wq1, wq2, wq3,
    out0, out1, out2, out3, mod_grad_out, send_out, keep_out, sumq_out, sumv_out,
    wq_s, acc, sumq, sumv, grad_s, block_s,
):
    step = pl.program_id(0)

    @pl.when(step == 0)
    def _():
        place_split((wq0, wq1, wq2, wq3), wq_s, pos)
        for item in (acc, sumq, sumv):
            item[...] = jnp.zeros_like(item)

    third = D // GROUPS
    scale = HD ** (-0.5)
    mod_one_low = mod_one[...]
    back = None
    for part in range(GROUPS):
        base = part * third
        for head in range(HEADS // GROUPS):
            at = head * HD
            query = qkv[part, at : at + HD]
            keys = qkv[part, third + at : third + at + HD]
            values = qkv[part, 2 * third + at : 2 * third + at + HD]
            out_grad = context[base + at : base + at + HD]
            weight = probs[0, part * (HEADS // GROUPS) + head]
            prob_grad = dot_tn(values, out_grad)
            values_grad = dot_nt(out_grad, weight)
            wide = weight.astype(F32)
            product = wide * prob_grad
            row_dot = jnp.sum(product, axis=0, keepdims=True)
            score_grad = (product - wide * row_dot).astype(BF16)
            query_grad = dot_nn(keys, score_grad) * scale
            keys_grad = dot_nt(query, score_grad) * scale
            grad_s[at : at + HD] = query_grad.astype(BF16)
            grad_s[third + at : third + at + HD] = keys_grad.astype(BF16)
            grad_s[2 * third + at : 2 * third + at + HD] = values_grad.astype(BF16)
        qkv_grad = grad_s[...]
        sumq[base : base + third] += lane_fold(qkv_grad[:third].astype(F32))
        sumv[base : base + third] += lane_fold(qkv_grad[2 * third :].astype(F32))
        acc[part] += dot_nt(mod_one_low, qkv_grad)
        partial = dot_nn(wq_s[part], qkv_grad)
        back = partial if back is None else back + partial
    normed, inverse = norm_stats(x[...].astype(F32))
    mod_grad_out[0, :, 0:1] = lane_sum(back)
    mod_grad_out[0, :, 1:2] = lane_sum(back * normed)
    block_s[...] = hidden_grad[...] + norm_back(back * (1.0 + mod[0, :, 1:2]), normed, inverse)
    split_features(block_s, (out0, out1, out2, out3), pos)

    @pl.when(step == pl.num_programs(0) - 1)
    def _():
        mine = pl.multiple_of(pos[0] * third, third)
        other = pl.multiple_of((1 - pos[0]) * third, third)
        for part in range(GROUPS):
            send_out[part] = acc[part, pl.ds(other, third), :].astype(send_out.dtype)
            keep_out[part] = acc[part, pl.ds(mine, third), :].astype(keep_out.dtype)
        sumq_out[...] = lane_sum(sumq[...])
        sumv_out[...] = lane_sum(sumv[...])


def call(kernel, pos, steps, seq, inputs, outputs, scratch, flops, name):
    def spec(kind, shape):
        rank = len(shape)
        if kind == "t":
            lead = (0,) * (rank - 1)
            return pl.BlockSpec(shape[:-1] + (seq,), lambda i, p: lead + (i,))
        if kind == "l":
            tail = (0,) * (rank - 1)
            return pl.BlockSpec((1,) + shape[1:], lambda i, p: (i,) + tail)
        zeros = (0,) * rank
        return pl.BlockSpec(shape, lambda i, p: zeros)

    size = sum(a.size * a.dtype.itemsize for _, a in inputs)
    size += sum(a.size * jnp.dtype(a.dtype).itemsize for _, a in outputs)
    return pl.pallas_call(
        kernel,
        grid_spec=pltpu.PrefetchScalarGridSpec(
            num_scalar_prefetch=1,
            grid=(steps,),
            in_specs=[spec(kind, a.shape) for kind, a in inputs],
            out_specs=[spec(kind, a.shape) for kind, a in outputs],
            scratch_shapes=scratch,
        ),
        out_shape=[a for _, a in outputs],
        compiler_params=pltpu.CompilerParams(
            dimension_semantics=("arbitrary",), vmem_limit_bytes=VMEM_BYTES
        ),
        cost_estimate=pl.CostEstimate(flops=flops, bytes_accessed=size, transcendentals=0),
        name=name,
    )(pos, *[a for _, a in inputs])


def swap(value, axis):
    return lax.ppermute(value, axis, [(0, 1), (1, 0)])


def group_step(value, step):
    return lax.ppermute(value, GROUP, [(at, at ^ step) for at in range(4)])


def gather_pieces(block):
    beside = swap(block, "col")
    return (block, beside, swap(block, "row"), swap(beside, "row"))


def spread_tokens(value, own):
    width = value.shape[1] // 4
    pieces = []
    for step in range(4):
        piece = lax.dynamic_slice_in_dim(value, (own ^ step) * width, width, 1)
        pieces.append(group_step(piece, step) if step else piece)
    return pieces


def collect_tokens(pieces, own):
    width = pieces[0].shape[1]
    moved = [group_step(piece, step) if step else piece for step, piece in enumerate(pieces)]
    out = jnp.zeros((pieces[0].shape[0], 4 * width), F32)
    for step, piece in enumerate(moved):
        out = lax.dynamic_update_slice_in_dim(out, piece.astype(F32), (own ^ step) * width, 1)
    return out


def in_order(own_first, other, index, axis):
    first = jnp.where(index == 0, own_first, other)
    second = jnp.where(index == 0, other, own_first)
    return jnp.stack([first, second], axis=axis)


def gather_dp(value):
    count = lax.axis_size("dp")
    return lax.all_to_all(jnp.broadcast_to(value[None], (count,) + value.shape), "dp", 0, 0)


def reduce_dp(value):
    count = lax.axis_size("dp")
    rows, columns = value.shape
    parts = lax.all_to_all(value.astype(BF16).reshape(count, rows // count, columns), "dp", 0, 0)
    total = jnp.sum(parts.astype(F32), axis=0)
    return gather_dp(total.astype(BF16)).reshape(rows, columns).astype(F32)


def reduce_grads(send, keep, col):
    half = keep + swap(send, "row").astype(F32)
    mine = lax.dynamic_index_in_dim(half, col, 0, keepdims=False)
    theirs = lax.dynamic_index_in_dim(half, 1 - col, 0, keepdims=False)
    return reduce_dp(mine + swap(theirs.astype(BF16), "col").astype(F32))


def local(
    block_input, condition, w_ada, b_ada, w_qkv, b_qkv, w_proj, b_proj, w_fc1, b_fc1, w_fc2,
    b_fc2, out_grad,
):
    row = lax.axis_index("row")
    col = lax.axis_index("col")
    own = row * 2 + col
    pos = jnp.stack([row, col]).astype(jnp.int32)
    latents = condition.shape[0]
    tokens = block_input.shape[1]
    seq = tokens // latents
    steps = latents // 4
    width = tokens // 4
    third = D // GROUPS
    half = FF // GROUPS

    def shape(dims, kind):
        return jax.ShapeDtypeStruct(dims, kind)

    x_pieces = spread_tokens(block_input, own)

    silu, silu_back = jax.vjp(jax.nn.silu, condition)
    cond_low = silu.astype(BF16)
    ada = jnp.dot(cond_low, w_ada, preferred_element_type=F32).reshape(latents, third, 6)
    bias_ada = lax.dynamic_update_slice_in_dim(
        jnp.zeros((third, 6), F32), b_ada.astype(F32).T, col * (third // 2), 0
    )
    ada = (ada + bias_ada[None]).reshape(2, 2, steps, third * 6)
    mine = lax.dynamic_index_in_dim(ada, col, 1, keepdims=False)
    theirs = lax.dynamic_index_in_dim(ada, 1 - col, 1, keepdims=False)
    ada = mine + swap(theirs, "col")
    mine = lax.dynamic_index_in_dim(ada, row, 0, keepdims=False)
    theirs = lax.dynamic_index_in_dim(ada, 1 - row, 0, keepdims=False)
    mod = in_order(mine, swap(theirs, "row"), row, 1).reshape(steps, D, 6)

    packed = jnp.concatenate([b_qkv[0], b_qkv[1], b_proj, b_fc1, b_fc2])
    packed = in_order(packed, swap(packed, "col"), col, 0)
    packed = in_order(packed, swap(packed, "row"), row, 0).astype(F32)
    bias_q = packed[0, :, :third].reshape(D, 1)
    bias_v = packed[0, :, third : 2 * third].reshape(D, 1)
    quarter = D // 4
    at = 2 * third
    bias_p = packed[:, :, at : at + quarter].reshape(D, 1)
    bias_1 = packed[0, :, at + quarter : at + quarter + half].reshape(FF, 1)
    bias_2 = packed[:, :, at + quarter + half :].reshape(D, 1)

    wq = gather_pieces(w_qkv)
    wp = gather_pieces(w_proj)

    t_low = shape((D, width), BF16)
    t_wide = shape((D, width), F32)
    t_ff = shape((FF, width), BF16)
    t_piece = shape((quarter, width), BF16)
    per_matmul = 2 * width * D

    x, mod_one, qkv, probs, attended, branch = call(
        attention_forward, pos, steps, seq,
        [("t", a) for a in x_pieces] + [("l", mod)] + [("w", a) for a in wq + wp]
        + [("w", bias_q), ("w", bias_v), ("w", bias_p)],
        [("t", t_low), ("t", t_low), ("t", shape((2, 3 * third, width), BF16)),
         ("l", shape((steps, HEADS, seq, seq), BF16)), ("t", t_low), ("t", t_wide)],
        [pltpu.VMEM((D, seq), F32), pltpu.VMEM((2, D, 3 * third), BF16),
         pltpu.VMEM((2, 3 * third, D), BF16), pltpu.VMEM((2, D, third), BF16),
         pltpu.VMEM((2, third, D), BF16)],
        per_matmul * (4 * D + 8 * seq), "attention_forward",
    )

    w_fc1, w_fc2, _ = lax.optimization_barrier((w_fc1, w_fc2, x_pieces))
    w1 = gather_pieces(w_fc1)
    w2 = gather_pieces(w_fc2)

    out0, out1, out2, out3, mod_two, act, slope, mlp = call(
        mlp_forward, pos, steps, seq,
        [("t", x), ("t", branch), ("l", mod)] + [("w", a) for a in w1 + w2]
        + [("w", bias_1), ("w", bias_2)],
        [("t", t_piece)] * 4 + [("t", t_low), ("t", t_ff), ("t", t_ff), ("t", t_wide)],
        [pltpu.VMEM((2, D, half), BF16), pltpu.VMEM((2, half, D), BF16),
         pltpu.VMEM((2, D, half), BF16), pltpu.VMEM((D, seq), F32)],
        per_matmul * 2 * FF, "mlp_forward",
    )
    block_output = collect_tokens((out0, out1, out2, out3), own)

    out_grad, _ = lax.optimization_barrier((out_grad, w1[1]))
    g_pieces = spread_tokens(out_grad, own)
    fc_block = (2, third, 2 * half + third)
    hidden_grad, context, mod_grad_two, send_fc, keep_fc, sum1, sum2, sump = call(
        mlp_backward, pos, steps, seq,
        [("t", a) for a in g_pieces]
        + [("t", x), ("t", branch), ("l", mod), ("t", mod_two), ("t", act), ("t", slope),
           ("t", mlp), ("t", attended)]
        + [("w", a) for a in w1 + w2 + wp],
        [("t", t_wide), ("t", t_low), ("l", shape((steps, D, 4), F32)),
         ("w", shape(fc_block, BF16)), ("w", shape(fc_block, F32)),
         ("w", shape((FF, 1), F32)), ("w", shape((D, 1), F32)), ("w", shape((D, 1), F32))],
        [pltpu.VMEM((D, seq), F32), pltpu.VMEM((2, D, half), BF16), pltpu.VMEM((2, D, half), BF16),
         pltpu.VMEM((2, half, D), BF16), pltpu.VMEM((2, D, third), BF16),
         pltpu.VMEM((2, D, half), F32), pltpu.VMEM((2, D, half), F32),
         pltpu.VMEM((2, D, third), F32), pltpu.VMEM((FF, 128), F32),
         pltpu.VMEM((D, 128), F32), pltpu.VMEM((D, 128), F32)],
        per_matmul * (4 * FF + 2 * D), "mlp_backward",
    )
    grads_fc = reduce_grads(send_fc, keep_fc, col)

    in0, in1, in2, in3, mod_grad_one, send_qkv, keep_qkv, sumq, sumv = call(
        attention_backward, pos, steps, seq,
        [("t", x), ("t", mod_one), ("l", mod), ("t", qkv), ("l", probs), ("t", context),
         ("t", hidden_grad)] + [("w", a) for a in wq],
        [("t", t_piece)] * 4
        + [("l", shape((steps, D, 2), F32)), ("w", shape((2, third, 3 * third), BF16)),
           ("w", shape((2, third, 3 * third), F32)),
           ("w", shape((D, 1), F32)), ("w", shape((D, 1), F32))],
        [pltpu.VMEM((2, D, 3 * third), BF16), pltpu.VMEM((2, D, 3 * third), F32),
         pltpu.VMEM((D, 128), F32), pltpu.VMEM((D, 128), F32),
         pltpu.VMEM((3 * third, seq), BF16), pltpu.VMEM((D, seq), F32)],
        per_matmul * (6 * D + 16 * seq), "attention_backward",
    )
    input_grad = collect_tokens((in0, in1, in2, in3), own)
    grads_qkv = reduce_grads(send_qkv, keep_qkv, col)

    span = third * 6
    mod_grad = jnp.concatenate([mod_grad_one, mod_grad_two], axis=2).astype(BF16).astype(F32)
    halves = mod_grad.reshape(steps, 2, span)
    mine = lax.dynamic_index_in_dim(halves, row, 1, keepdims=False)
    theirs = lax.dynamic_index_in_dim(halves, 1 - row, 1, keepdims=False)
    sums = jnp.concatenate([sumq, sumv, sump, sum1, sum2])[:, 0]
    sums = jnp.pad(sums, (0, 3 * span - sums.shape[0])).reshape(3, span)
    moved = swap(jnp.concatenate([theirs, sums]), "row")
    sums = sums + moved[steps:]
    pair = in_order(mine, moved[:steps], row, 0)
    moved = swap(jnp.concatenate([pair.reshape(2 * steps, span), sums]), "col")
    sums = (sums + moved[2 * steps :]).reshape(-1)
    pairs = in_order(pair, moved[: 2 * steps].reshape(pair.shape), col, 1)
    mod_here = pairs.reshape(latents, span).astype(BF16)

    def part_of(start, size, index):
        return lax.dynamic_slice_in_dim(sums, start + index * size, size)

    mine = jnp.concatenate(
        [part_of(0, third, col), part_of(D, third, col), part_of(2 * D, quarter, own),
         part_of(3 * D, half, col), part_of(3 * D + FF, quarter, own)]
    )
    mine = jnp.pad(mine, (0, 2 * span - mine.shape[0])).reshape(2, span)
    everyone = gather_dp(jnp.concatenate([mod_here, mine.astype(BF16)]))
    cond_all = gather_dp(cond_low).reshape(-1, cond_low.shape[1])
    mod_all = everyone[:, :latents].reshape(-1, span)
    grad_w_ada = dot_tn(cond_all, mod_all)
    grad_b_ada = jnp.sum(mod_all.astype(F32), axis=0).reshape(third, 6)
    grad_b_ada = lax.dynamic_slice_in_dim(grad_b_ada, col * quarter, quarter, 0).T
    totals = jnp.sum(everyone[:, latents:].astype(F32), axis=0).reshape(-1)
    cond_part = dot_nt(mod_here, w_ada)
    cond_grad = silu_back(cond_part + swap(cond_part, "row"))[0]

    at = 2 * third
    return (
        block_output,
        input_grad,
        cond_grad,
        grad_w_ada,
        grad_b_ada,
        grads_qkv,
        totals[:at].reshape(2, third),
        grads_fc[:, 2 * half :],
        totals[at : at + quarter],
        grads_fc[:, :half],
        totals[at + quarter : at + quarter + half],
        grads_fc[:, half : 2 * half],
        totals[at + quarter + half : at + 2 * quarter + half],
    )


def solution(mesh):
    return jax.shard_map(
        local,
        mesh=mesh,
        in_specs=(
            P(("row", "col"), "dp"),
            P("dp", "col"),
            P("col", "row"),
            P(None, ("row", "col")),
            P("row", "col"),
            P(None, "col"),
            P("col", "row"),
            P(("row", "col")),
            P("row", "col"),
            P("col"),
            P("row", "col"),
            P(("row", "col")),
            P(("row", "col"), "dp"),
        ),
        out_specs=(
            P(("row", "col"), "dp"),
            P(("row", "col"), "dp"),
            P("dp", "col"),
            P("col", "row"),
            P(None, ("row", "col")),
            P("row", "col"),
            P(None, "col"),
            P("col", "row"),
            P(("row", "col")),
            P("row", "col"),
            P("col"),
            P("row", "col"),
            P(("row", "col")),
        ),
        check_vma=False,
    )
```

time: 719 us -> 242 us (0.34)
  waiting for transfers between devices: 405 us -> 66.4 us
  blocking collectives: 101 us -> 0 us
  matrix products: 82.1 us -> 2.54 us
  Pallas kernels: 0 us -> 65.4 us
  starting transfers between devices: 1.92 us -> 49.8 us
  other arithmetic: 62.7 us -> 23.9 us
  local copies, waits for them, and re-layouts: 45.6 us -> 30.9 us
  between operations: 15.3 us -> 1.49 us
    reduce_scatter x8 -> x0, waiting for transfers between devices: 186 us -> none  [the longest x4 117 us: sum_features(): return lax.psum_scatter(value, 'col', scatter_dimension=dim, tiled=True)]
    all_gather x8 -> x0, waiting for transfers between devices: 146 us -> none  [the longest x4 88.7 us: gather_features(): return lax.all_gather(value, 'col', axis=dim, tiled=True)]
    psum x6 -> x0, blocking collectives: 93.1 us -> none  [the longest x4 50.7 us: norm_totals(): return lax.psum((first, second), ('row', 'col'))]
    dot_general x21 -> x3, matrix products: 82.1 us -> 2.54 us  [the longest x1 2.17 us: dot_tn(): lax.dot_general(left, right, (((0,), (0,)), ((), ())), preferred_element_...]
    psum x1 -> x0, waiting for transfers between devices: 72.1 us -> none  [local(): lax.psum((grad_w_ada, grad_b_ada, grad_w_qkv, grad_b_qkv, grad_w_proj, gr...]
    pallas_call x0 -> x4, Pallas kernels: none -> 65.4 us  [call(): pl.pallas_call(kernel, grid_spec=pltpu.PrefetchScalarGridSpec(num_scalar_...]
    all_to_all x0 -> x6, waiting for transfers between devices: none -> 35.1 us  [the longest x2 18.7 us: reduce_dp(): lax.all_to_all(value.astype(BF16).reshape(count, rows // count, columns),...]
    ppermute x0 -> x35, waiting for transfers between devices: none -> 31.3 us  [the longest x23 31.3 us: swap(): return lax.ppermute(value, axis, [(0, 1), (1, 0)])]
  transfers between devices with their start and end apart: 18 -> 41, of which waited for: 17 -> 10; matrix products, arithmetic and copies ran while one was open for 12% -> 21% of each run, Pallas kernels for 0% -> 27%
where the time goes in v1:
time: 242 us; the launch traced here: 241 us
  waiting for transfers between devices  66.4 us (27%)
  Pallas kernels  65.4 us (27%)
  starting transfers between devices  49.8 us (21%)
  local copies, waits for them, and re-layouts  30.9 us (13%)
  other arithmetic  23.9 us (10%)
  matrix products  2.54 us (1%)
    pallas_call x4, Pallas kernels, call(): pl.pallas_call(kernel, grid_spec=pltpu.PrefetchScalarGridSpec(num_scalar_...  65.4 us
    ppermute x23, waiting for transfers between devices, swap(): return lax.ppermute(value, axis, [(0, 1), (1, 0)])  31.3 us
    all_to_all x4, starting transfers between devices, gather_dp(): lax.all_to_all(jnp.broadcast_to(value[None], (count,) + value.shape), 'dp...  19.5 us
    all_to_all x2, waiting for transfers between devices, reduce_dp(): lax.all_to_all(value.astype(BF16).reshape(count, rows // count, columns),...  18.7 us
    all_to_all x4, waiting for transfers between devices, gather_dp(): lax.all_to_all(jnp.broadcast_to(value[None], (count,) + value.shape), 'dp...  16.4 us
    ppermute x23, starting transfers between devices, swap(): return lax.ppermute(value, axis, [(0, 1), (1, 0)])  13.6 us
    all_to_all x2, starting transfers between devices, reduce_dp(): lax.all_to_all(value.astype(BF16).reshape(count, rows // count, columns),...  9.67 us
    dynamic_update_slice x8, other arithmetic, collect_tokens(): lax.dynamic_update_slice_in_dim(out, piece.astype(F32), (own ^ step) * wi...  7.88 us
  transfers between devices with their start and end apart: 41, of which 10 were waited for; matrix products, arithmetic and copies ran while one was open for 21% of the time, Pallas kernels for 27%

profile of v1, /device:TPU:0, one launch (start us, length us, event | category | flops | bytes accessed | tf_op | source)
XLA Modules:
  0.0 240.5 jit_solution(12848216048711259032)
XLA Ops:
  2.7 3.0 %collective-permute-start.3 = (f32[2,4,1152]{2,1,0:T(4,128)S(1)}, f32[2,4,1152]{2,1,0:T(4,128)S(1)}, u32[]{:S(2)}, u32[]{:S(2)}) collective-permute-start(f32[2,4,1152]{2,1,0:T(4,128)S(1)} %dynamic-slice_bitcast_fusion.1), channel_id=1, source_target_pairs={{0,1},{1,0},{2,3},{3,2},{4,5},{5,4},{6,7},{7,6},{8,9},{9,8},{10,11... | collective-permute-start | bytes 110600 | tf_op jit(solution)/shard_map/ppermute | solution.py:337
  6.5 2.1 concatenate.37
  9.5 2.0 collective-permute-start
  12.2 6.3 %all-to-all-start = ((bf16[8,16,192]{2,1,0:T(8,128)(2,1)}), bf16[8,16,192]{2,1,0:T(8,128)(2,1)S(1)}, u32[]{:S(2)}, u32[]{:S(2)}) async-start(bf16[8,16,192]{2,1,0:T(8,128)(2,1)} %broadcast_in_dim.8), calls=%async_computation | async-start | bytes 131072 | tf_op jit(solution)/shard_map/all_to_all | solution.py:375
  30.4 5.4 %collective-permute-done.5.wq1 = bf16[192,576]{1,0:T(8,128)(2,1)S(1)} collective-permute-done((bf16[192,576]{1,0:T(8,128)(2,1)S(1)}, bf16[192,576]{1,0:T(8,128)(2,1)S(1)}, u32[]{:S(2)}, u32[]{:S(2)}) %collective-permute-start.5) | collective-permute-done | bytes 221216 | tf_op jit(solution)/shard_map/ppermute | solution.py:337
  35.9 1.7 reshape.173.mod
  38.2 4.0 %collective-permute-done.13.w11 = bf16[192,768]{1,0:T(8,128)(2,1)S(1)} collective-permute-done((bf16[192,768]{1,0:T(8,128)(2,1)S(1)}, bf16[192,768]{1,0:T(8,128)(2,1)S(1)}, u32[]{:S(2)}, u32[]{:S(2)}) %collective-permute-start.13) | collective-permute-done | bytes 294944 | tf_op jit(solution)/shard_map/ppermute | solution.py:337
  42.2 5.4 %collective-permute-done.16.w21 = bf16[192,768]{1,0:T(8,128)(2,1)S(1)} collective-permute-done((bf16[192,768]{1,0:T(8,128)(2,1)S(1)}, bf16[192,768]{1,0:T(8,128)(2,1)S(1)}, u32[]{:S(2)}, u32[]{:S(2)}) %collective-permute-start.16) | collective-permute-done | bytes 294944 | tf_op jit(solution)/shard_map/ppermute | solution.py:337
  48.4 16.7 %attention_forward.1 = (bf16[384,1024]{1,0:T(8,128)(2,1)}, bf16[384,1024]{1,0:T(8,128)(2,1)}, bf16[2,576,1024]{2,1,0:T(8,128)(2,1)}, bf16[4,6,256,256]{3,2,1,0:T...) custom-call(s32[2]{0:T(128)} %pad_add_fusion.pos, bf16[96,1024]{1,0:T(8,128)(2,1)} %get-tuple-element.117.x0, ...), custom_call_target="tpu_custom_call" | custom-call | flops 2818572288 | bytes 11444736 | tf_op jit(solution)/shard_map/attention_forward/pallas_call | solution.py:318
  68.9 12.7 %mlp_forward.1 = (bf16[96,1024]{1,0:T(8,128)(2,1)}, bf16[96,1024]{1,0:T(8,128)(2,1)}, bf16[96,1024]{1,0:T(8,128)(2,1)}, bf16[96,1024]{1,0:T(8,128)(2,1)}, bf16[3...) custom-call(s32[2]{0:T(128)} %pad_add_fusion.pos, ...), custom_call_target="tpu_custom_call" | custom-call | flops 2415919104 | bytes 14200320 | tf_op jit(solution)/shard_map/mlp_forward/pallas_call | solution.py:318
  82.4 20.4 %mlp_backward.1 = (f32[384,1024]{1,0:T(8,128)}, bf16[384,1024]{1,0:T(8,128)(2,1)}, f32[4,384,4]{2,1,0:T(8,128)}, bf16[2,192,1728]{2,1,0:T(8,128)(2,1)}, f32[2,19...) custom-call(s32[2]{0:T(128)} %pad_add_fusion.pos, ...), custom_call_target="tpu_custom_call" | custom-call | flops 5435817984 | bytes 21648384 | tf_op jit(solution)/shard_map/mlp_backward/pallas_call | solution.py:318
  103.1 15.7 %attention_backward.1 = (bf16[96,1024]{1,0:T(8,128)(2,1)}, bf16[96,1024]{1,0:T(8,128)(2,1)}, bf16[96,1024]{1,0:T(8,128)(2,1)}, bf16[96,1024]{1,0:T(8,128)(2,1)},...) custom-call(s32[2]{0:T(128)} %pad_add_fusion.pos, ...), custom_call_target="tpu_custom_call" | custom-call | flops 5033164800 | bytes 12487680 | tf_op jit(solution)/shard_map/attention_backward/pallas_call | solution.py:318
  128.3 1.6 collective-permute-start.29
  129.9 4.6 %collective-permute-done.29 = f32[11,1152]{1,0:T(8,128)S(1)} collective-permute-done((f32[11,1152]{1,0:T(8,128)S(1)}, f32[11,1152]{1,0:T(8,128)S(1)}, u32[]{:S(2)}, u32[]{:S(2)}) %collective-permute-start.29) | collective-permute-done | bytes 50720 | tf_op jit(solution)/shard_map/ppermute | solution.py:337
  136.1 2.4 convert_add_fusion
  140.6 2.1 convert_add_fusion.1
  143.5 6.0 %all-to-all-start.1 = ((bf16[8,18,1152]{2,1,0:T(8,128)(2,1)}), bf16[8,18,1152]{2,1,0:T(8,128)(2,1)}, u32[]{:S(2)}, u32[]{:S(2)}) async-start(bf16[8,18,1152]{2,1,0:T(8,128)(2,1)} %broadcast_in_dim.9), calls=%async_computation.1 | async-start | bytes 884736 | tf_op jit(solution)/shard_map/all_to_all | solution.py:375
  151.6 11.3 %collective-permute-done.32 = bf16[192,576]{1,0:T(8,128)(2,1)S(1)} collective-permute-done((bf16[192,576]{1,0:T(8,128)(2,1)S(1)}, bf16[192,576]{1,0:T(8,128)(2,1)S(1)}, u32[]{:S(2)}, u32[]{:S(2)}) %collective-permute-start.32) | collective-permute-done | bytes 221216 | tf_op jit(solution)/shard_map/ppermute | solution.py:337
  164.4 1.8 fusion.2
  166.2 6.0 %all-to-all-start.2 = ((bf16[8,24,576]{2,1,0:T(8,128)(2,1)}), bf16[8,24,576]{2,1,0:T(8,128)(2,1)S(1)}, u32[]{:S(2)}, u32[]{:S(2)}) async-start(bf16[8,24,576]{2,1,0:T(8,128)(2,1)} %bitcast.78), calls=%async_computation.2 | async-start | bytes 491520 | tf_op jit(solution)/shard_map/all_to_all | solution.py:381
  172.2 2.1 fusion
  174.2 7.3 %all-to-all-done.2 = bf16[8,24,576]{2,1,0:T(8,128)(2,1)S(1)} async-done(((bf16[8,24,576]{2,1,0:T(8,128)(2,1)}), bf16[8,24,576]{2,1,0:T(8,128)(2,1)S(1)}, u32[]{:S(2)}, u32[]{:S(2)}) %all-to-all-start.2) | async-done | bytes 221216 | tf_op jit(solution)/shard_map/all_to_all | solution.py:381
  181.5 3.7 %all-to-all-start.4 = ((bf16[8,24,1728]{2,1,0:T(8,128)(2,1)}), bf16[8,24,1728]{2,1,0:T(8,128)(2,1)S(1)}, u32[]{:S(2)}, u32[]{:S(2)}) async-start(bf16[8,24,1728]{2,1,0:T(8,128)(2,1)} %bitcast.77), calls=%async_computation.4 | async-start | bytes 1376256 | tf_op jit(solution)/shard_map/all_to_all | solution.py:381
  186.8 1.7 convert_dynamic-update-slice_fusion.2
  188.5 1.7 convert_dynamic-update-slice_fusion.1
  190.2 1.7 convert_dynamic-update-slice_fusion
  191.9 11.4 %all-to-all-done.4 = bf16[8,24,1728]{2,1,0:T(8,128)(2,1)S(1)} async-done(((bf16[8,24,1728]{2,1,0:T(8,128)(2,1)}), bf16[8,24,1728]{2,1,0:T(8,128)(2,1)S(1)}, u32[]{:S(2)}, u32[]{:S(2)}) %all-to-all-start.4) | async-done | bytes 663584 | tf_op jit(solution)/shard_map/all_to_all | solution.py:381
  204.0 3.6 %all-to-all-start.3 = ((bf16[8,24,576]{2,1,0:T(8,128)(2,1)}), bf16[8,24,576]{2,1,0:T(8,128)(2,1)S(1)}, u32[]{:S(2)}, u32[]{:S(2)}) async-start(bf16[8,24,576]{2,1,0:T(8,128)(2,1)} %broadcast_in_dim.10), calls=%async_computation.3 | async-start | bytes 491520 | tf_op jit(solution)/shard_map/all_to_all | solution.py:375
  208.8 7.7 %all-to-all-done.3 = bf16[8,24,576]{2,1,0:T(8,128)(2,1)S(1)} async-done(((bf16[8,24,576]{2,1,0:T(8,128)(2,1)}), bf16[8,24,576]{2,1,0:T(8,128)(2,1)S(1)}, u32[]{:S(2)}, u32[]{:S(2)}) %all-to-all-start.3) | async-done | bytes 221216 | tf_op jit(solution)/shard_map/all_to_all | solution.py:375
  217.5 3.5 %all-to-all-start.5 = ((bf16[8,24,1728]{2,1,0:T(8,128)(2,1)}), bf16[8,24,1728]{2,1,0:T(8,128)(2,1)S(1)}, u32[]{:S(2)}, u32[]{:S(2)}) async-start(bf16[8,24,1728]{2,1,0:T(8,128)(2,1)} %broadcast_in_dim.11), calls=%async_computation.5 | async-start | bytes 1376256 | tf_op jit(solution)/shard_map/all_to_all | solution.py:375
  226.3 2.2 convolution_bitcast_fusion
  229.9 8.7 %all-to-all-done.5 = bf16[8,24,1728]{2,1,0:T(8,128)(2,1)S(1)} async-done(((bf16[8,24,1728]{2,1,0:T(8,128)(2,1)}), bf16[8,24,1728]{2,1,0:T(8,128)(2,1)S(1)}, u32[]{:S(2)}, u32[]{:S(2)}) %all-to-all-start.5) | async-done | bytes 663584 | tf_op jit(solution)/shard_map/all_to_all | solution.py:375
  (237 shorter events, 52.8 us)
Async XLA Ops:
  2.7 18.8 %collective-permute-start.3 = (f32[2,4,1152]{2,1,0:T(4,128)S(1)}, f32[2,4,1152]{2,1,0:T(4,128)S(1)}, u32[]{:S(2)}, u32[]{:S(2)}) collective-permute-start(f32[2,4,1152]{2,1,0:T(4,128)S(1)} %dynamic-slice_bitcast_fusion.1), channel_id=1, source_target_pairs={{0,1},{1,0},{2,3},{3,2},{4,5},{5,4},{6,7},{7,6},{8,9},{9,8},{10,11... | collective-permute-start | bytes 110600 | tf_op jit(solution)/shard_map/ppermute | solution.py:337
  9.5 17.0 %collective-permute-start = (bf16[96,1024]{1,0:T(8,128)(2,1)S(1)}, bf16[96,1024]{1,0:T(8,128)(2,1)S(1)}, u32[]{:S(2)}, u32[]{:S(2)}) collective-permute-start(bf16[96,1024]{1,0:T(8,128)(2,1)S(1)} %get-tuple-element.116), channel_id=1, source_target_pairs={{0,1},{1,0},{2,3},{3,2},{4,5},{5,4},{6,7},{7,6},{8,9},{9,8},{10,11... | collective-permute-start | bytes 589832 | tf_op jit(solution)/shard_map/ppermute | solution.py:341
  11.4 15.6 %collective-permute-start.1 = (bf16[96,1024]{1,0:T(8,128)(2,1)S(1)}, bf16[96,1024]{1,0:T(8,128)(2,1)S(1)}, u32[]{:S(2)}, u32[]{:S(2)}) collective-permute-start(bf16[96,1024]{1,0:T(8,128)(2,1)S(1)} %get-tuple-element.118), channel_id=1, source_target_pairs={{0,2},{1,3},{2,0},{3,1},{4,6},{5,7},{6,4},{7,5},{8,10},{9,11},{10,... | collective-permute-start | bytes 589832 | tf_op jit(solution)/shard_map/ppermute | solution.py:341
  11.4 16.2 %collective-permute-start.2 = (bf16[96,1024]{1,0:T(8,128)(2,1)S(1)}, bf16[96,1024]{1,0:T(8,128)(2,1)S(1)}, u32[]{:S(2)}, u32[]{:S(2)}) collective-permute-start(bf16[96,1024]{1,0:T(8,128)(2,1)S(1)} %get-tuple-element.115), channel_id=1, source_target_pairs={{0,3},{1,2},{2,1},{3,0},{4,7},{5,6},{6,5},{7,4},{8,11},{9,10},{10,... | collective-permute-start | bytes 589832 | tf_op jit(solution)/shard_map/ppermute | solution.py:341
  12.2 130.5 %all-to-all-start = ((bf16[8,16,192]{2,1,0:T(8,128)(2,1)}), bf16[8,16,192]{2,1,0:T(8,128)(2,1)S(1)}, u32[]{:S(2)}, u32[]{:S(2)}) async-start(bf16[8,16,192]{2,1,0:T(8,128)(2,1)} %broadcast_in_dim.8), calls=%async_computation | async-start | bytes 131072 | tf_op jit(solution)/shard_map/all_to_all | solution.py:375
  19.8 10.0 %collective-permute-start.8 = (bf16[192,192]{1,0:T(8,128)(2,1)}, bf16[192,192]{1,0:T(8,128)(2,1)}, u32[]{:S(2)}, u32[]{:S(2)}) collective-permute-start(bf16[192,192]{1,0:T(8,128)(2,1)} %wp0.3), channel_id=1, source_target_pairs={{0,1},{1,0},{2,3},{3,2},{4,5},{5,4},{6,7},{7,6},{8,9},{9,8},{10,11... | collective-permute-start | bytes 221192 | tf_op jit(solution)/shard_map/ppermute | solution.py:337
  27.7 14.5 %collective-permute-start.13 = (bf16[192,768]{1,0:T(8,128)(2,1)S(1)}, bf16[192,768]{1,0:T(8,128)(2,1)S(1)}, u32[]{:S(2)}, u32[]{:S(2)}) collective-permute-start(bf16[192,768]{1,0:T(8,128)(2,1)S(1)} %copy-done.12), channel_id=1, source_target_pairs={{0,1},{1,0},{2,3},{3,2},{4,5},{5,4},{6,7},{7,6},{8,9},{9,8},{10,11... | collective-permute-start | bytes 884744 | tf_op jit(solution)/shard_map/ppermute | solution.py:337
  29.2 18.4 %collective-permute-start.16 = (bf16[192,768]{1,0:T(8,128)(2,1)S(1)}, bf16[192,768]{1,0:T(8,128)(2,1)S(1)}, u32[]{:S(2)}, u32[]{:S(2)}) collective-permute-start(bf16[192,768]{1,0:T(8,128)(2,1)S(1)} %copy-done.13), channel_id=1, source_target_pairs={{0,1},{1,0},{2,3},{3,2},{4,5},{5,4},{6,7},{7,6},{8,9},{9,8},{10,11... | collective-permute-start | bytes 884744 | tf_op jit(solution)/shard_map/ppermute | solution.py:337
  35.9 11.7 %collective-permute-start.7 = (bf16[192,576]{1,0:T(8,128)(2,1)S(1)}, bf16[192,576]{1,0:T(8,128)(2,1)S(1)}, u32[]{:S(2)}, u32[]{:S(2)}) collective-permute-start(bf16[192,576]{1,0:T(8,128)(2,1)S(1)} %collective-permute-done.5.wq1), channel_id=1, source_target_pairs={{0,2},{2,0},{1,3},{3,1},{4,6},{6,4},{5,7},{7,5},{8,10},{10,8},{9,1... | collective-permute-start | bytes 663560 | tf_op jit(solution)/shard_map/ppermute | solution.py:337
  37.6 28.8 %collective-permute-start.14 = (bf16[192,768]{1,0:T(8,128)(2,1)S(1)}, bf16[192,768]{1,0:T(8,128)(2,1)S(1)}, u32[]{:S(2)}, u32[]{:S(2)}) collective-permute-start(bf16[192,768]{1,0:T(8,128)(2,1)S(1)} %copy-done.12), channel_id=1, source_target_pairs={{0,2},{2,0},{1,3},{3,1},{4,6},{6,4},{5,7},{7,5},{8,10},{10,8},{9,1... | collective-permute-start | bytes 884744 | tf_op jit(solution)/shard_map/ppermute | solution.py:337
  38.1 28.5 %collective-permute-start.17 = (bf16[192,768]{1,0:T(8,128)(2,1)S(1)}, bf16[192,768]{1,0:T(8,128)(2,1)S(1)}, u32[]{:S(2)}, u32[]{:S(2)}) collective-permute-start(bf16[192,768]{1,0:T(8,128)(2,1)S(1)} %copy-done.13), channel_id=1, source_target_pairs={{0,2},{2,0},{1,3},{3,1},{4,6},{6,4},{5,7},{7,5},{8,10},{10,8},{9,1... | collective-permute-start | bytes 884744 | tf_op jit(solution)/shard_map/ppermute | solution.py:337
  42.2 25.8 %collective-permute-start.15 = (bf16[192,768]{1,0:T(8,128)(2,1)S(1)}, bf16[192,768]{1,0:T(8,128)(2,1)S(1)}, u32[]{:S(2)}, u32[]{:S(2)}) collective-permute-start(bf16[192,768]{1,0:T(8,128)(2,1)S(1)} %collective-permute-done.13.w11), channel_id=1, source_target_pairs={{0,2},{2,0},{1,3},{3,1},{4,6},{6,4},{5,7},{7,5},{8,10},{10,8},{9,1... | collective-permute-start | bytes 884744 | tf_op jit(solution)/shard_map/ppermute | solution.py:337
  47.6 20.4 %collective-permute-start.18 = (bf16[192,768]{1,0:T(8,128)(2,1)S(1)}, bf16[192,768]{1,0:T(8,128)(2,1)S(1)}, u32[]{:S(2)}, u32[]{:S(2)}) collective-permute-start(bf16[192,768]{1,0:T(8,128)(2,1)S(1)} %collective-permute-done.16.w21), channel_id=1, source_target_pairs={{0,2},{2,0},{1,3},{3,1},{4,6},{6,4},{5,7},{7,5},{8,10},{10,8},{9,1... | collective-permute-start | bytes 884744 | tf_op jit(solution)/shard_map/ppermute | solution.py:337
  65.9 15.7 %collective-permute-start.22 = (bf16[96,1024]{1,0:T(8,128)(2,1)S(1)}, bf16[96,1024]{1,0:T(8,128)(2,1)S(1)}, u32[]{:S(2)}, u32[]{:S(2)}) collective-permute-start(bf16[96,1024]{1,0:T(8,128)(2,1)S(1)} %get-tuple-element.113), channel_id=1, source_target_pairs={{0,1},{1,0},{2,3},{3,2},{4,5},{5,4},{6,7},{7,6},{8,9},{9,8},{10,11... | collective-permute-start | bytes 589832 | tf_op jit(solution)/shard_map/ppermute | solution.py:341
  66.4 15.2 %collective-permute-start.23 = (bf16[96,1024]{1,0:T(8,128)(2,1)S(1)}, bf16[96,1024]{1,0:T(8,128)(2,1)S(1)}, u32[]{:S(2)}, u32[]{:S(2)}) collective-permute-start(bf16[96,1024]{1,0:T(8,128)(2,1)S(1)} %get-tuple-element.112), channel_id=1, source_target_pairs={{0,2},{1,3},{2,0},{3,1},{4,6},{5,7},{6,4},{7,5},{8,10},{9,11},{10,... | collective-permute-start | bytes 589832 | tf_op jit(solution)/shard_map/ppermute | solution.py:341
  66.6 15.0 %collective-permute-start.24 = (bf16[96,1024]{1,0:T(8,128)(2,1)S(1)}, bf16[96,1024]{1,0:T(8,128)(2,1)S(1)}, u32[]{:S(2)}, u32[]{:S(2)}) collective-permute-start(bf16[96,1024]{1,0:T(8,128)(2,1)S(1)} %get-tuple-element.111), channel_id=1, source_target_pairs={{0,3},{1,2},{2,1},{3,0},{4,7},{5,6},{6,5},{7,4},{8,11},{9,10},{10,... | collective-permute-start | bytes 589832 | tf_op jit(solution)/shard_map/ppermute | solution.py:341
  102.8 32.2 %collective-permute-start.33 = (bf16[2,192,1728]{2,1,0:T(8,128)(2,1)}, bf16[2,192,1728]{2,1,0:T(8,128)(2,1)S(1)}, u32[]{:S(2)}, u32[]{:S(2)}) collective-permute-start(bf16[2,192,1728]{2,1,0:T(8,128)(2,1)} %get-tuple-element.80), channel_id=1, source_target_pairs={{0,2},{2,0},{1,3},{3,1},{4,6},{6,4},{5,7},{7,5},{8,10},{10,8},{9,1... | collective-permute-start | bytes 3981320 | tf_op jit(solution)/shard_map/ppermute | solution.py:337
  118.7 21.9 %collective-permute-start.31 = (bf16[2,192,576]{2,1,0:T(8,128)(2,1)}, bf16[2,192,576]{2,1,0:T(8,128)(2,1)}, u32[]{:S(2)}, u32[]{:S(2)}) collective-permute-start(bf16[2,192,576]{2,1,0:T(8,128)(2,1)} %get-tuple-element.78), channel_id=1, source_target_pairs={{0,2},{2,0},{1,3},{3,1},{4,6},{6,4},{5,7},{7,5},{8,10},{10,8},{9,1... | collective-permute-start | bytes 1327112 | tf_op jit(solution)/shard_map/ppermute | solution.py:337
  125.5 60.6 %collective-permute-start.25 = (bf16[96,1024]{1,0:T(8,128)(2,1)}, bf16[96,1024]{1,0:T(8,128)(2,1)}, u32[]{:S(2)}, u32[]{:S(2)}) collective-permute-start(bf16[96,1024]{1,0:T(8,128)(2,1)} %get-tuple-element.67), channel_id=1, source_target_pairs={{0,1},{1,0},{2,3},{3,2},{4,5},{5,4},{6,7},{7,6},{8,9},{9,8},{10,11... | collective-permute-start | bytes 589832 | tf_op jit(solution)/shard_map/ppermute | solution.py:341
  126.1 62.4 %collective-permute-start.26 = (bf16[96,1024]{1,0:T(8,128)(2,1)}, bf16[96,1024]{1,0:T(8,128)(2,1)}, u32[]{:S(2)}, u32[]{:S(2)}) collective-permute-start(bf16[96,1024]{1,0:T(8,128)(2,1)} %get-tuple-element.68), channel_id=1, source_target_pairs={{0,2},{1,3},{2,0},{3,1},{4,6},{5,7},{6,4},{7,5},{8,10},{9,11},{10,... | collective-permute-start | bytes 589832 | tf_op jit(solution)/shard_map/ppermute | solution.py:341
  134.5 55.7 %collective-permute-start.27 = (bf16[96,1024]{1,0:T(8,128)(2,1)}, bf16[96,1024]{1,0:T(8,128)(2,1)}, u32[]{:S(2)}, u32[]{:S(2)}) collective-permute-start(bf16[96,1024]{1,0:T(8,128)(2,1)} %get-tuple-element.69), channel_id=1, source_target_pairs={{0,3},{1,2},{2,1},{3,0},{4,7},{5,6},{6,5},{7,4},{8,11},{9,10},{10,... | collective-permute-start | bytes 589832 | tf_op jit(solution)/shard_map/ppermute | solution.py:341
  139.4 26.7 %collective-permute-start.34 = (bf16[192,1728]{1,0:T(8,128)(2,1)}, bf16[192,1728]{1,0:T(8,128)(2,1)}, u32[]{:S(2)}, u32[]{:S(2)}) collective-permute-start(bf16[192,1728]{1,0:T(8,128)(2,1)} %fusion.1), channel_id=1, source_target_pairs={{0,1},{1,0},{2,3},{3,2},{4,5},{5,4},{6,7},{7,6},{8,9},{9,8},{10,11... | collective-permute-start | bytes 1990664 | tf_op jit(solution)/shard_map/ppermute | solution.py:337
  143.5 22.7 %all-to-all-start.1 = ((bf16[8,18,1152]{2,1,0:T(8,128)(2,1)}), bf16[8,18,1152]{2,1,0:T(8,128)(2,1)}, u32[]{:S(2)}, u32[]{:S(2)}) async-start(bf16[8,18,1152]{2,1,0:T(8,128)(2,1)} %broadcast_in_dim.9), calls=%async_computation.1 | async-start | bytes 884736 | tf_op jit(solution)/shard_map/all_to_all | solution.py:375
  150.5 12.4 %collective-permute-start.32 = (bf16[192,576]{1,0:T(8,128)(2,1)S(1)}, bf16[192,576]{1,0:T(8,128)(2,1)S(1)}, u32[]{:S(2)}, u32[]{:S(2)}) collective-permute-start(bf16[192,576]{1,0:T(8,128)(2,1)S(1)} %fusion.4), channel_id=1, source_target_pairs={{0,1},{1,0},{2,3},{3,2},{4,5},{5,4},{6,7},{7,6},{8,9},{9,8},{10,11... | collective-permute-start | bytes 663560 | tf_op jit(solution)/shard_map/ppermute | solution.py:337
  162.9 44.8 %collective-permute-start.19 = (bf16[96,1024]{1,0:T(8,128)(2,1)}, bf16[96,1024]{1,0:T(8,128)(2,1)}, u32[]{:S(2)}, u32[]{:S(2)}) collective-permute-start(bf16[96,1024]{1,0:T(8,128)(2,1)} %get-tuple-element.52), channel_id=1, source_target_pairs={{0,1},{1,0},{2,3},{3,2},{4,5},{5,4},{6,7},{7,6},{8,9},{9,8},{10,11... | collective-permute-start | bytes 589832 | tf_op jit(solution)/shard_map/ppermute | solution.py:341
  166.2 19.2 %collective-permute-start.30 = (f32[16,192]{1,0:T(8,128)S(1)}, f32[16,192]{1,0:T(8,128)S(1)}, u32[]{:S(2)}, u32[]{:S(2)}) collective-permute-start(f32[16,192]{1,0:T(8,128)S(1)} %fusion.20), channel_id=1, source_target_pairs={{0,2},{2,0},{1,3},{3,1},{4,6},{6,4},{5,7},{7,5},{8,10},{10,8},{9,1... | collective-permute-start | bytes 36872 | tf_op jit(solution)/shard_map/ppermute | solution.py:337
  166.2 15.3 %all-to-all-start.2 = ((bf16[8,24,576]{2,1,0:T(8,128)(2,1)}), bf16[8,24,576]{2,1,0:T(8,128)(2,1)S(1)}, u32[]{:S(2)}, u32[]{:S(2)}) async-start(bf16[8,24,576]{2,1,0:T(8,128)(2,1)} %bitcast.78), calls=%async_computation.2 | async-start | bytes 491520 | tf_op jit(solution)/shard_map/all_to_all | solution.py:381
  181.5 21.8 %all-to-all-start.4 = ((bf16[8,24,1728]{2,1,0:T(8,128)(2,1)}), bf16[8,24,1728]{2,1,0:T(8,128)(2,1)S(1)}, u32[]{:S(2)}, u32[]{:S(2)}) async-start(bf16[8,24,1728]{2,1,0:T(8,128)(2,1)} %bitcast.77), calls=%async_computation.4 | async-start | bytes 1376256 | tf_op jit(solution)/shard_map/all_to_all | solution.py:381
  185.4 23.2 %collective-permute-start.20 = (bf16[96,1024]{1,0:T(8,128)(2,1)}, bf16[96,1024]{1,0:T(8,128)(2,1)S(1)}, u32[]{:S(2)}, u32[]{:S(2)}) collective-permute-start(bf16[96,1024]{1,0:T(8,128)(2,1)} %get-tuple-element.53), channel_id=1, source_target_pairs={{0,2},{1,3},{2,0},{3,1},{4,6},{5,7},{6,4},{7,5},{8,10},{9,11},{10,... | collective-permute-start | bytes 589832 | tf_op jit(solution)/shard_map/ppermute | solution.py:341
  186.1 34.9 %collective-permute-start.21 = (bf16[96,1024]{1,0:T(8,128)(2,1)}, bf16[96,1024]{1,0:T(8,128)(2,1)}, u32[]{:S(2)}, u32[]{:S(2)}) collective-permute-start(bf16[96,1024]{1,0:T(8,128)(2,1)} %get-tuple-element.54), channel_id=1, source_target_pairs={{0,3},{1,2},{2,1},{3,0},{4,7},{5,6},{6,5},{7,4},{8,11},{9,10},{10,... | collective-permute-start | bytes 589832 | tf_op jit(solution)/shard_map/ppermute | solution.py:341
  204.0 12.5 %all-to-all-start.3 = ((bf16[8,24,576]{2,1,0:T(8,128)(2,1)}), bf16[8,24,576]{2,1,0:T(8,128)(2,1)S(1)}, u32[]{:S(2)}, u32[]{:S(2)}) async-start(bf16[8,24,576]{2,1,0:T(8,128)(2,1)} %broadcast_in_dim.10), calls=%async_computation.3 | async-start | bytes 491520 | tf_op jit(solution)/shard_map/all_to_all | solution.py:375
  217.5 21.1 %all-to-all-start.5 = ((bf16[8,24,1728]{2,1,0:T(8,128)(2,1)}), bf16[8,24,1728]{2,1,0:T(8,128)(2,1)S(1)}, u32[]{:S(2)}, u32[]{:S(2)}) async-start(bf16[8,24,1728]{2,1,0:T(8,128)(2,1)} %broadcast_in_dim.11), calls=%async_computation.5 | async-start | bytes 1376256 | tf_op jit(solution)/shard_map/all_to_all | solution.py:375
  (42 other events, 307.8 us)

commit v2 on v1

v2 whole, which is shorter than its diff:
```python
import jax
import jax.numpy as jnp
from jax import lax
from jax.experimental import pallas as pl
from jax.experimental.pallas import tpu as pltpu
from jax.sharding import PartitionSpec as P

D = 384
HEADS = 6
HD = 64
FF = 1536
GROUPS = 2
EPSILON = 1e-06
BF16 = jnp.bfloat16
F32 = jnp.float32
GROUP = ("row", "col")
VMEM_BYTES = 56 * 1024 * 1024


def dot_nn(left, right):
    return lax.dot_general(left, right, (((1,), (0,)), ((), ())), preferred_element_type=F32)


def dot_nt(left, right):
    return lax.dot_general(left, right, (((1,), (1,)), ((), ())), preferred_element_type=F32)


def dot_tn(left, right):
    return lax.dot_general(left, right, (((0,), (0,)), ((), ())), preferred_element_type=F32)


def lane_sum(value):
    return jnp.sum(value, axis=1, keepdims=True)


def lane_fold(value):
    parts = [value[:, at : at + 128] for at in range(0, value.shape[1], 128)]
    return sum(parts[1:], parts[0])


def norm_stats(value):
    center = jnp.sum(value, axis=0, keepdims=True) * (1.0 / D)
    square = jnp.sum(value * value, axis=0, keepdims=True) * (1.0 / D)
    inverse = lax.rsqrt(square - center * center + EPSILON)
    return (value - center) * inverse, inverse


def norm_back(grad, normed, inverse):
    first = jnp.sum(grad, axis=0, keepdims=True) * (1.0 / D)
    second = jnp.sum(grad * normed, axis=0, keepdims=True) * (1.0 / D)
    return inverse * (grad - first - normed * second)


PIECES = ((0, 0), (0, 1), (1, 0), (1, 1))


def place_split(pieces, target, pos):
    row, col = pos[0], pos[1]
    for piece, (step_row, step_col) in zip(pieces, PIECES):
        height = piece.shape[0]
        at = pl.multiple_of((row ^ step_row) * height, height)
        target[col ^ step_col, pl.ds(at, height), :] = piece[...]


def place_proj(pieces, target, pos):
    row, col = pos[0], pos[1]
    for piece, (step_row, step_col) in zip(pieces, PIECES):
        height = piece.shape[0]
        at = pl.multiple_of((col ^ step_col) * height, height)
        target[row ^ step_row, pl.ds(at, height), :] = piece[...]


BIAS_ROWS = 8


def bias_columns(packs, pos, query_s, value_s, proj_s, last_s):
    own, col = pos[0] * 2 + pos[1], pos[1]
    third = D // GROUPS
    quarter = D // 4
    for step, pack in enumerate(packs):
        columns = pack[pack.shape[0] - BIAS_ROWS :, :].T
        if step < 2 and query_s is not None:
            at = pl.multiple_of((col ^ step) * third, third)
            query_s[pl.ds(at, third), :] = columns[:, 0:1]
            value_s[pl.ds(at, third), :] = columns[:, 1:2]
        at = pl.multiple_of((own ^ step) * quarter, quarter)
        if proj_s is not None:
            proj_s[pl.ds(at, quarter), :] = columns[:quarter, 2:3]
        if last_s is not None:
            last_s[pl.ds(at, quarter), :] = columns[:quarter, 3:4]


def cut_tokens(pos, x, out1, out2, out3):
    own = pos[0] * 2 + pos[1]
    width = out1.shape[1]
    for step, out in ((1, out1), (2, out2), (3, out3)):
        at = pl.multiple_of((own ^ step) * width, width)
        out[...] = x[:, pl.ds(at, width)]


def piece_order(latents, steps, own):
    here = lax.broadcasted_iota(jnp.int32, (latents, latents), 0)
    there = lax.broadcasted_iota(jnp.int32, (latents, latents), 1)
    return (there == (own ^ (here // steps)) * steps + here % steps).astype(BF16)


def modulation_parts(
    pos, condition, w_ada, b_ada, b_qkv, b_proj, b_fc2,
    pack0, pack1, pack2, pack3, cond_out, w_ada_out,
):
    own, col = pos[0] * 2 + pos[1], pos[1]
    latents = condition.shape[0]
    steps = latents // 4
    third = D // GROUPS
    quarter = D // 4
    value = condition[...]
    cond_low = (value * jax.nn.sigmoid(value)).astype(BF16)
    cond_out[...] = cond_low
    ordered = dot_nn(piece_order(latents, steps, own), cond_low).astype(BF16)
    zeros = jnp.zeros((6, quarter), F32)
    bias = b_ada[...].astype(F32)
    bias = jnp.where(
        col == 0, jnp.concatenate([bias, zeros], 1), jnp.concatenate([zeros, bias], 1)
    )
    rows = lax.broadcasted_iota(jnp.int32, (third * 6, third), 0)
    columns = lax.broadcasted_iota(jnp.int32, (third * 6, third), 1)
    packs = (pack0, pack1, pack2, pack3)
    for vector in range(6):
        select = (rows == columns * 6 + vector).astype(BF16)
        weight = dot_nn(w_ada[...], select).astype(BF16)
        w_ada_out[vector] = weight
        part = dot_nn(ordered, weight) + bias[vector : vector + 1]
        for step in range(4):
            for at in range(steps):
                packs[step][at * 8 + vector : at * 8 + vector + 1, :] = part[
                    step * steps + at : step * steps + at + 1
                ]
    for pack in packs:
        at = steps * 8
        pack[at : at + 2, :] = b_qkv[...].astype(F32)
        pack[at + 2 : at + 8, :] = jnp.zeros((6, third), F32)
        pack[at + 2 : at + 3, :quarter] = b_proj[...].astype(F32)
        pack[at + 3 : at + 4, :quarter] = b_fc2[...].astype(F32)
        for latent in range(steps):
            pack[latent * 8 + 6 : latent * 8 + 8, :] = jnp.zeros((2, third), F32)


def join_tokens(pos, x0, x1, x2, x3, out):
    for step, piece in enumerate((x0, x1, x2, x3)):

        @pl.when(pl.program_id(0) == step)
        def _():
            out[...] = piece[...].astype(out.dtype)


def group_vectors(pos, pack0, pack1, pack2, pack3, cond, w_ada, everyone, cond_part):
    own = pos[0] * 2 + pos[1]
    packs = (pack0, pack1, pack2, pack3)
    latents = cond.shape[0]
    steps = latents // 4
    low = jnp.concatenate([pack[: steps * 8, :].astype(BF16) for pack in packs], 0)
    wanted = lax.broadcasted_iota(jnp.int32, (6 * latents, 4 * steps * 8), 0)
    source = lax.broadcasted_iota(jnp.int32, (6 * latents, 4 * steps * 8), 1)
    latent = wanted % latents
    found = ((own ^ (latent // steps)) * steps + latent % steps) * 8 + wanted // latents
    rows = dot_nn((source == found).astype(BF16), low).astype(BF16)
    everyone[: 6 * latents] = rows
    total = None
    for vector in range(6):
        partial = dot_nt(rows[vector * latents : (vector + 1) * latents], w_ada[vector])
        total = partial if total is None else total + partial
    cond_part[...] = total
    sums = sum(pack[steps * 8 :, :] for pack in packs)
    sums = jnp.concatenate([sums, jnp.zeros_like(sums)], 0)
    everyone[6 * latents : 6 * latents + 2 * BIAS_ROWS] = sums.astype(BF16)
    everyone[6 * latents + 2 * BIAS_ROWS :] = cond[...]


def modulation_grads(pos, *refs):
    everyone, (w_out, b_out, fc1_out, qkv_out, proj_out, fc2_out) = refs[:-6], refs[-6:]
    third = D // GROUPS
    quarter = D // 4
    latents = (refs[0].shape[1] - 2 * BIAS_ROWS) // 7

    def rows_of(start, size):
        found = [ref[:, start : start + size, :].reshape(-1, third) for ref in everyone]
        return jnp.concatenate(found, 0)

    rows = lax.broadcasted_iota(jnp.int32, (third, third * 6), 0)
    columns = lax.broadcasted_iota(jnp.int32, (third, third * 6), 1)
    total = None
    for vector in range(6):
        grads = rows_of(vector * latents, latents)
        select = (columns == rows * 6 + vector).astype(BF16)
        partial = dot_nn(grads, select)
        total = partial if total is None else total + partial
        summed = jnp.sum(grads.astype(F32), axis=0, keepdims=True)
        b_out[vector : vector + 1, :] = jnp.where(
            pos[1] == 0, summed[:, :quarter], summed[:, quarter:]
        )
    cond = rows_of(6 * latents + 2 * BIAS_ROWS, latents)
    w_out[...] = dot_tn(cond, total.astype(BF16))
    sums = rows_of(6 * latents, 2 * BIAS_ROWS).astype(F32)
    sums = jnp.sum(sums.reshape(-1, 2 * BIAS_ROWS, third), axis=0)
    qkv_out[...] = sums[0:2]
    proj_out[...] = sums[2:3, :quarter]
    fc2_out[...] = sums[3:4, :quarter]
    fc1_out[...] = sums[4:8]


def place_features(pieces, target, pos):
    own = pos[0] * 2 + pos[1]
    for step, piece in enumerate(pieces):
        height = piece.shape[0]
        at = pl.multiple_of((own ^ step) * height, height)
        target[pl.ds(at, height), :] = piece[...].astype(target.dtype)


def split_features(source, pieces, pos):
    own = pos[0] * 2 + pos[1]
    for step, piece in enumerate(pieces):
        height = piece.shape[0]
        at = pl.multiple_of((own ^ step) * height, height)
        piece[...] = source[pl.ds(at, height), :].astype(piece.dtype)


def attention_forward(
    pos, x0, x1, x2, x3, wq0, wq1, wq2, wq3, wp0, wp1, wp2, wp3, pack0, pack1, pack2, pack3,
    x_out, mod_one_out, qkv_out, probs_out, attended_out, branch_out, mod,
    x_s, wq_s, wq_t, wp_s, wp_t, bias_q, bias_v, bias_p,
):
    @pl.when(pl.program_id(0) == 0)
    def _():
        place_split((wq0, wq1, wq2, wq3), wq_s, pos)
        place_proj((wp0, wp1, wp2, wp3), wp_s, pos)
        bias_columns((pack0, pack1, pack2, pack3), pos, bias_q, bias_v, bias_p, None)
        for part in range(GROUPS):
            wq_t[part] = wq_s[part].T
            wp_t[part] = wp_s[part].T

    third = D // GROUPS
    for first, second, who in ((pack0, pack1, pos[0]), (pack2, pack3, 1 - pos[0])):
        rows = pl.ds(pl.multiple_of(pl.program_id(0) * 8, 8), 8)
        at = pl.multiple_of(who * third, third)
        mod[0, pl.ds(at, third), :] = (first[rows, :] + second[rows, :]).T
    place_features((x0, x1, x2, x3), x_s, pos)
    x = x_s[...]
    x_out[...] = x.astype(BF16)
    normed, _ = norm_stats(x)
    mod_one = (normed * (1.0 + mod[0, :, 1:2]) + mod[0, :, 0:1]).astype(BF16)
    mod_one_out[...] = mod_one
    per_group = HEADS // GROUPS
    heads = []
    for part in range(GROUPS):
        qkv = dot_nn(wq_t[part], mod_one)
        base = part * third
        query = (qkv[:third] + bias_q[base : base + third]).astype(BF16)
        keys = qkv[third : 2 * third].astype(BF16)
        values = (qkv[2 * third :] + bias_v[base : base + third]).astype(BF16)
        qkv_out[part, :third] = query
        qkv_out[part, third : 2 * third] = keys
        qkv_out[part, 2 * third :] = values
        scaled = query * jnp.asarray(HD ** (-0.5), BF16)
        for head in range(per_group):
            rows = slice(head * HD, (head + 1) * HD)
            heads.append((keys[rows], scaled[rows], values[rows]))
    scores = [dot_nn(keys.T, query) for keys, query, _ in heads]
    probs = []
    for score in scores:
        raised = jnp.exp(score - jnp.max(score, axis=0, keepdims=True))
        total = jnp.sum(raised, axis=0, keepdims=True)
        probs.append((raised * (1.0 / total)).astype(BF16))
    for head, prob in enumerate(probs):
        probs_out[0, head] = prob
        attended_out[head * HD : (head + 1) * HD] = dot_nn(heads[head][2], prob).astype(BF16)
    attended = attended_out[...]
    for part in range(2):
        rows = slice(part * third, (part + 1) * third)
        branch_out[rows] = dot_nn(wp_t[part], attended) + bias_p[rows]


def mlp_forward(
    pos, x, branch, mod, w10, w11, w12, w13, w20, w21, w22, w23, pack0, pack1, pack2, pack3,
    b10, b11,
    out0, out1, out2, out3, mod_two_out, act_out, slope_out, mlp_out,
    w1_s, w1_t, w2_s, block_s, bias_1, bias_2,
):
    @pl.when(pl.program_id(0) == 0)
    def _():
        bias_columns((pack0, pack1, pack2, pack3), pos, None, None, None, bias_2)
        for step, piece in enumerate((b10, b11)):
            height = piece.shape[1]
            column = jnp.broadcast_to(piece[...].astype(F32), (8, height)).T
            at = pl.multiple_of((pos[1] ^ step) * height, height)
            bias_1[pl.ds(at, height), :] = column[:, 0:1]
        place_split((w10, w11, w12, w13), w1_s, pos)
        place_split((w20, w21, w22, w23), w2_s, pos)
        for part in range(GROUPS):
            w1_t[part] = w1_s[part].T

    hidden = x[...].astype(F32) + mod[0, :, 2:3] * branch[...]
    normed, _ = norm_stats(hidden)
    mod_two = (normed * (1.0 + mod[0, :, 4:5]) + mod[0, :, 3:4]).astype(BF16)
    mod_two_out[...] = mod_two
    half = FF // GROUPS
    slope = (2.0 / jnp.pi) ** 0.5
    parts = [slice(part * half, (part + 1) * half) for part in range(GROUPS)]
    pres = [dot_nn(w1_t[part], mod_two) + bias_1[rows] for part, rows in enumerate(parts)]
    acts = []
    for pre, rows in zip(pres, parts):
        square = pre * pre
        tanh = jnp.tanh(pre * (slope + (slope * 0.044715) * square))
        upper = 0.5 + 0.5 * tanh
        acts.append((pre * upper).astype(BF16))
        act_out[rows] = acts[-1]
        slope_out[rows] = (
            upper + pre * (1.0 - tanh * tanh) * (0.5 * slope + (1.5 * slope * 0.044715) * square)
        ).astype(BF16)
    total = dot_nn(w2_s[0], acts[0]) + dot_nn(w2_s[1], acts[1])
    mlp = total + bias_2[...]
    mlp_out[...] = mlp
    block_s[...] = hidden + mod[0, :, 5:6] * mlp
    split_features(block_s, (out0, out1, out2, out3), pos)


def mlp_backward(
    pos, g0, g1, g2, g3, x, branch, mod, mod_two, act, slope, mlp, attended,
    w10, w11, w12, w13, w20, w21, w22, w23, wp0, wp1, wp2, wp3,
    hidden_grad_out, context_out, mod_grad_out, send_out, keep_out, sum1_out, sum2_out, sump_out,
    g_s, w1_s, w2_s, w2_t, wp_s, acc1, acc2, accp, sum1, sum2, sump,
):
    step = pl.program_id(0)

    @pl.when(step == 0)
    def _():
        place_split((w10, w11, w12, w13), w1_s, pos)
        place_split((w20, w21, w22, w23), w2_s, pos)
        place_proj((wp0, wp1, wp2, wp3), wp_s, pos)
        for part in range(GROUPS):
            w2_t[part] = w2_s[part].T
        for acc in (acc1, acc2, accp, sum1, sum2, sump):
            acc[...] = jnp.zeros_like(acc)

    place_features((g0, g1, g2, g3), g_s, pos)
    grad = g_s[...]
    gate_one = mod[0, :, 2:3]
    gate_two = mod[0, :, 5:6]
    hidden = x[...].astype(F32) + gate_one * branch[...]
    normed, inverse = norm_stats(hidden)
    mod_grad_out[0, :, 3:4] = lane_sum(grad * mlp[...])
    mlp_grad = (gate_two * grad).astype(BF16)
    sum2[...] += lane_fold(mlp_grad.astype(F32))
    half = FF // GROUPS
    third = D // GROUPS
    mod_two_low = mod_two[...]
    parts = [slice(part * half, (part + 1) * half) for part in range(GROUPS)]
    act_grads = [dot_nn(w2_t[part], mlp_grad) for part in range(GROUPS)]
    pre_grads = []
    for act_grad, rows in zip(act_grads, parts):
        pre_grads.append((act_grad * slope[rows].astype(F32)).astype(BF16))
        sum1[rows] += lane_fold(pre_grads[-1].astype(F32))
    back = dot_nn(w1_s[0], pre_grads[0]) + dot_nn(w1_s[1], pre_grads[1])
    for part, rows in enumerate(parts):
        acc2[part] += dot_nt(mlp_grad, act[rows])
        acc1[part] += dot_nt(mod_two_low, pre_grads[part])
    mod_grad_out[0, :, 1:2] = lane_sum(back)
    mod_grad_out[0, :, 2:3] = lane_sum(back * normed)
    hidden_grad = grad + norm_back(back * (1.0 + mod[0, :, 4:5]), normed, inverse)
    hidden_grad_out[...] = hidden_grad
    mod_grad_out[0, :, 0:1] = lane_sum(hidden_grad * branch[...])
    branch_grad = (gate_one * hidden_grad).astype(BF16)
    sump[...] += lane_fold(branch_grad.astype(F32))
    context = None
    for part in range(2):
        rows = slice(part * third, (part + 1) * third)
        accp[part] += dot_nt(attended[...], branch_grad[rows])
        partial = dot_nn(wp_s[part], branch_grad[rows])
        context = partial if context is None else context + partial
    context_out[...] = context.astype(BF16)

    @pl.when(step == pl.num_programs(0) - 1)
    def _():
        mine = pl.multiple_of(pos[0] * third, third)
        other = pl.multiple_of((1 - pos[0]) * third, third)
        for part in range(GROUPS):
            rows = slice(part * third, (part + 1) * third)
            for out, at, who in ((send_out, other, 1 - pos[0]), (keep_out, mine, pos[0])):
                out[part, :, :half] = acc1[part, pl.ds(at, third), :].astype(out.dtype)
                out[part, :, half : 2 * half] = acc2[part, pl.ds(at, third), :].astype(out.dtype)
                out[part, :, 2 * half :] = accp[who, rows, :].astype(out.dtype)
        sum1_out[...] = lane_sum(sum1[...])
        sum2_out[...] = lane_sum(sum2[...])
        sump_out[...] = lane_sum(sump[...])


def attention_backward(
    pos, x, mod_one, mod, qkv, probs, context, hidden_grad, mod_grad, sum1, sum2, sump,
    wq0, wq1, wq2, wq3,
    left0, left1, left2, left3,
    out0, out1, out2, out3, send_out, keep_out, pack0, pack1, pack2, pack3, joined,
    wq_s, acc, sumq, sumv, grad_s, block_s, mod_s, bias_s,
):
    step = pl.program_id(0)

    @pl.when(step == 0)
    def _():
        place_split((wq0, wq1, wq2, wq3), wq_s, pos)
        for item in (acc, sumq, sumv):
            item[...] = jnp.zeros_like(item)

    third = D // GROUPS
    scale = HD ** (-0.5)
    mod_one_low = mod_one[...]
    per_group = HEADS // GROUPS
    heads = []
    for head in range(HEADS):
        part, at = head // per_group, head % per_group * HD
        heads.append(
            (
                qkv[part, at : at + HD],
                qkv[part, third + at : third + at + HD],
                qkv[part, 2 * third + at : 2 * third + at + HD],
                context[head * HD : (head + 1) * HD],
                probs[0, head],
            )
        )
    prob_grads = [dot_nn(values.T, grad) for _, _, values, grad, _ in heads]
    score_grads = []
    for prob_grad, (_, _, _, _, weight) in zip(prob_grads, heads):
        wide = weight.astype(F32)
        product = wide * prob_grad
        row_dot = jnp.sum(product, axis=0, keepdims=True)
        score_grads.append((product - wide * row_dot).astype(BF16))
    for head, (query, keys, _, grad, weight) in enumerate(heads):
        part, at = head // per_group, head % per_group * HD
        parts = (
            dot_nn(keys, score_grads[head]) * scale,
            dot_nt(query, score_grads[head]) * scale,
            dot_nt(grad, weight),
        )
        for which, value in enumerate(parts):
            start = which * third + at
            grad_s[part, start : start + HD] = value.astype(BF16)
    back = dot_nn(wq_s[0], grad_s[0]) + dot_nn(wq_s[1], grad_s[1])
    for part in range(GROUPS):
        base = part * third
        qkv_grad = grad_s[part]
        sumq[base : base + third] += lane_fold(qkv_grad[:third].astype(F32))
        sumv[base : base + third] += lane_fold(qkv_grad[2 * third :].astype(F32))
        acc[part] += dot_nt(mod_one_low, qkv_grad)
    normed, inverse = norm_stats(x[...].astype(F32))
    mod_s[...] = jnp.zeros_like(mod_s)
    mod_s[:, 0:1] = lane_sum(back)
    mod_s[:, 1:2] = lane_sum(back * normed)
    mod_s[:, 2:6] = mod_grad[0]
    packs = (pack0, pack1, pack2, pack3)
    rows = pl.ds(pl.multiple_of(step * 8, 8), 8)
    mine = pl.multiple_of(pos[0] * third, third)
    other = pl.multiple_of((1 - pos[0]) * third, third)
    vectors = mod_s[pl.ds(mine, third), :].T
    pack0[rows, :] = vectors
    pack1[rows, :] = vectors
    vectors = mod_s[pl.ds(other, third), :].T
    pack2[rows, :] = vectors
    pack3[rows, :] = vectors
    block_s[...] = hidden_grad[...] + norm_back(back * (1.0 + mod[0, :, 1:2]), normed, inverse)
    split_features(block_s, (out0, out1, out2, out3), pos)
    join_tokens(pos, left0, left1, left2, left3, joined)

    @pl.when(step == pl.num_programs(0) - 1)
    def _():
        for part in range(GROUPS):
            send_out[part] = acc[part, pl.ds(other, third), :].astype(send_out.dtype)
            keep_out[part] = acc[part, pl.ds(mine, third), :].astype(keep_out.dtype)

        own = pos[0] * 2 + pos[1]
        quarter = D // 4
        half = FF // GROUPS
        sumq[:, 0:1] = lane_sum(sumq[...])
        sumv[:, 0:1] = lane_sum(sumv[...])
        for index, pack in enumerate(packs):
            col = pos[1] ^ (index & 1)
            bias_s[...] = jnp.zeros_like(bias_s)
            for part in range(4):
                at = pl.multiple_of(col * half + part * third, third)
                bias_s[:, 4 + part : 5 + part] = sum1[pl.ds(at, third), :]
            at = pl.multiple_of(col * third, third)
            bias_s[:, 0:1] = sumq[pl.ds(at, third), 0:1]
            bias_s[:, 1:2] = sumv[pl.ds(at, third), 0:1]
            at = pl.multiple_of((own ^ index) * quarter, quarter)
            bias_s[:quarter, 2:3] = sump[pl.ds(at, quarter), :]
            bias_s[:quarter, 3:4] = sum2[pl.ds(at, quarter), :]
            pack[pack.shape[0] - BIAS_ROWS :, :] = bias_s[...].T


def call(kernel, pos, steps, seq, inputs, outputs, scratch, micros, name):
    def spec(kind, shape):
        rank = len(shape)
        if kind == "t":
            lead = (0,) * (rank - 1)
            return pl.BlockSpec(shape[:-1] + (seq,), lambda i, p: lead + (i,))
        if kind == "o":
            return pl.BlockSpec(
                shape[:-1] + (seq,), lambda i, p: (0, (p[0] * 2 + p[1]) * steps + i)
            )
        if kind == "j":
            return pl.BlockSpec(
                shape[:-1] + (shape[-1] // 4,), lambda i, p: (0, (p[0] * 2 + p[1]) ^ i)
            )
        if kind == "l":
            tail = (0,) * (rank - 1)
            return pl.BlockSpec((1,) + shape[1:], lambda i, p: (i,) + tail)
        zeros = (0,) * rank
        return pl.BlockSpec(shape, lambda i, p: zeros)

    size = sum(a.size * a.dtype.itemsize for _, a in inputs)
    size += sum(a.size * jnp.dtype(a.dtype).itemsize for _, a in outputs)
    return pl.pallas_call(
        kernel,
        grid_spec=pltpu.PrefetchScalarGridSpec(
            num_scalar_prefetch=1,
            grid=(steps,),
            in_specs=[spec(kind, a.shape) for kind, a in inputs],
            out_specs=[spec(kind, a.shape) for kind, a in outputs],
            scratch_shapes=scratch,
        ),
        out_shape=[a for _, a in outputs],
        compiler_params=pltpu.CompilerParams(
            dimension_semantics=("arbitrary",), vmem_limit_bytes=VMEM_BYTES
        ),
        cost_estimate=pl.CostEstimate(
            flops=int(micros * 1e9), bytes_accessed=size, transcendentals=0
        ),
        name=name,
    )(pos, *[a for _, a in inputs])


def swap(value, axis):
    return lax.ppermute(value, axis, [(0, 1), (1, 0)])


def group_step(value, step):
    return lax.ppermute(value, GROUP, [(at, at ^ step) for at in range(4)])


def gather_pieces(block, beside):
    return (block, beside, swap(block, "row"), swap(beside, "row"))


def in_order(own_first, other, index, axis):
    first = jnp.where(index == 0, own_first, other)
    second = jnp.where(index == 0, other, own_first)
    return jnp.stack([first, second], axis=axis)


def dp_bits():
    count = lax.axis_size("dp")
    return [1 << at for at in range(count.bit_length() - 1)]


def dp_step(value, bit):
    count = lax.axis_size("dp")
    return lax.ppermute(value, "dp", [(at, at ^ bit) for at in range(count)])


def scatter_terms(value):
    count = lax.axis_size("dp")
    cols, rows, columns = value.shape
    blocks = value.reshape(cols * count, rows // count, columns)
    return lax.all_to_all(blocks, ("col", "dp"), 0, 0)


def after(value, token):
    return lax.optimization_barrier((value, token))[0]


def double(value, bit):
    here = (lax.axis_index("dp") // bit) % 2
    return in_order(value, dp_step(value, bit), here, value.ndim - 2)


def local(
    block_input, condition, w_ada, b_ada, w_qkv, b_qkv, w_proj, b_proj, w_fc1, b_fc1, w_fc2,
    b_fc2, out_grad,
):
    row = lax.axis_index("row")
    col = lax.axis_index("col")
    pos = jnp.stack([row, col]).astype(jnp.int32)
    latents = condition.shape[0]
    tokens = block_input.shape[1]
    seq = tokens // latents
    steps = latents // 4
    width = tokens // 4
    third = D // GROUPS
    half = FF // GROUPS
    quarter = D // 4
    pack_rows = steps * 8 + BIAS_ROWS

    def shape(dims, kind):
        return jax.ShapeDtypeStruct(dims, kind)

    t_low = shape((D, width), BF16)
    t_wide = shape((D, width), F32)
    t_ff = shape((FF, width), BF16)
    t_piece = shape((quarter, width), BF16)
    pack = ("w", shape((pack_rows, third), F32))

    wq_beside, wp_beside = swap(w_qkv, "col"), swap(w_proj, "col")
    *packs, cond_low, w_ada_by_vector = call(
        modulation_parts, pos, 1, seq,
        [("w", condition), ("w", w_ada), ("w", b_ada), ("w", b_qkv),
         ("w", b_proj.reshape(1, -1)), ("w", b_fc2.reshape(1, -1))],
        [pack] * 4 + [("w", shape(condition.shape, BF16)), ("w", shape((6, third, third), BF16))],
        [], 6, "modulation_parts",
    )

    def cut(value, name):
        return call(
            cut_tokens, pos, 1, seq, [("w", value)], [("w", t_piece)] * 3, [], 3, name
        )

    packs, wq_beside, wp_beside, block_input = lax.optimization_barrier(
        (packs, wq_beside, wp_beside, block_input)
    )
    x_cuts = cut(block_input, "cut_input")
    x_moved = [group_step(piece, step) for step, piece in zip((1, 2, 3), x_cuts)]
    packs = [packs[0]] + [group_step(packs[step], step) for step in (1, 2, 3)]
    wq = gather_pieces(w_qkv, wq_beside)
    wp = gather_pieces(w_proj, wp_beside)
    out_late, b_fc1 = after((out_grad, b_fc1), x_cuts[0])
    g_cuts = cut(out_late, "cut_grad")
    b_fc1 = b_fc1.reshape(1, -1)
    x_moved, wq, wp, packs, g_cuts, w_fc1, w_fc2, b_fc1 = lax.optimization_barrier(
        (x_moved, wq, wp, packs, g_cuts, w_fc1, w_fc2, b_fc1)
    )
    w1_beside, w2_beside = swap(w_fc1, "col"), swap(w_fc2, "col")
    w1_row, w2_row = swap(w_fc1, "row"), swap(w_fc2, "row")
    b_fc1 = (b_fc1, swap(b_fc1, "col"))
    x, mod_one, qkv, probs, attended, branch, mod = call(
        attention_forward, pos, steps, seq,
        [("o", block_input)] + [("t", a) for a in x_moved]
        + [("w", a) for a in (*wq, *wp, *packs)],
        [("t", t_low), ("t", t_low), ("t", shape((2, 3 * third, width), BF16)),
         ("l", shape((steps, HEADS, seq, seq), BF16)), ("t", t_low), ("t", t_wide),
         ("l", shape((steps, D, 8), F32))],
        [pltpu.VMEM((D, seq), F32), pltpu.VMEM((2, D, 3 * third), BF16),
         pltpu.VMEM((2, 3 * third, D), BF16), pltpu.VMEM((2, D, third), BF16),
         pltpu.VMEM((2, third, D), BF16), pltpu.VMEM((D, 1), F32), pltpu.VMEM((D, 1), F32),
         pltpu.VMEM((D, 1), F32)],
        16, "attention_forward",
    )

    g_cuts, branch, w1_beside, w2_beside, w1_row, w2_row, b_fc1 = lax.optimization_barrier(
        (g_cuts, branch, w1_beside, w2_beside, w1_row, w2_row, b_fc1)
    )
    w1 = (w_fc1, w1_beside, w1_row, swap(w1_beside, "row"))
    w2 = (w_fc2, w2_beside, w2_row, swap(w2_beside, "row"))
    g_moved = [group_step(piece, step) for step, piece in zip((1, 2, 3), g_cuts)]
    *outs, mod_two, act, slope, mlp = call(
        mlp_forward, pos, steps, seq,
        [("t", x), ("t", branch), ("l", mod)] + [("w", a) for a in w1 + w2]
        + [("w", a) for a in (*packs, *b_fc1)],
        [("t", t_piece)] * 4 + [("t", t_low), ("t", t_ff), ("t", t_ff), ("t", t_wide)],
        [pltpu.VMEM((2, D, half), BF16), pltpu.VMEM((2, half, D), BF16),
         pltpu.VMEM((2, D, half), BF16), pltpu.VMEM((D, seq), F32), pltpu.VMEM((FF, 1), F32),
         pltpu.VMEM((D, 1), F32)],
        12, "mlp_forward",
    )
    outs, g_moved, mlp = lax.optimization_barrier((outs, g_moved, mlp))
    outs = [outs[0]] + [group_step(outs[step], step) for step in (1, 2, 3)]
    fc_block = (2, third, 2 * half + third)
    qkv_block = (2, third, 3 * third)
    blocks = lambda dims: [("w", shape(dims, BF16))] * 2
    hidden_grad, context, mod_grad, send_fc, keep_fc, sum1, sum2, sump = call(
        mlp_backward, pos, steps, seq,
        [("o", out_grad)] + [("t", a) for a in g_moved]
        + [("t", x), ("t", branch), ("l", mod), ("t", mod_two), ("t", act), ("t", slope),
           ("t", mlp), ("t", attended)]
        + [("w", a) for a in w1 + w2 + wp],
        [("t", t_wide), ("t", t_low), ("l", shape((steps, D, 4), F32))] + blocks(fc_block)
        + [("w", shape((FF, 1), F32)), ("w", shape((D, 1), F32)), ("w", shape((D, 1), F32))],
        [pltpu.VMEM((D, seq), F32), pltpu.VMEM((2, D, half), BF16), pltpu.VMEM((2, D, half), BF16),
         pltpu.VMEM((2, half, D), BF16), pltpu.VMEM((2, D, third), BF16),
         pltpu.VMEM((2, D, half), F32), pltpu.VMEM((2, D, half), F32),
         pltpu.VMEM((2, D, third), F32), pltpu.VMEM((FF, 128), F32),
         pltpu.VMEM((D, 128), F32), pltpu.VMEM((D, 128), F32)],
        20, "mlp_backward",
    )
    outs, send_fc = lax.optimization_barrier((outs, send_fc))
    fc = (keep_fc.astype(F32) + swap(send_fc, "row").astype(F32)).astype(BF16)
    fc, context = lax.optimization_barrier((fc, context))
    fc_parts = scatter_terms(fc)

    *ins, send_qkv, keep_qkv, back0, back1, back2, back3, block_output = call(
        attention_backward, pos, steps, seq,
        [("t", x), ("t", mod_one), ("l", mod), ("t", qkv), ("l", probs), ("t", context),
         ("t", hidden_grad), ("l", mod_grad), ("w", sum1), ("w", sum2), ("w", sump)]
        + [("w", a) for a in (*wq, *outs)],
        [("t", t_piece)] * 4 + blocks(qkv_block) + [pack] * 4
        + [("j", shape((quarter, tokens), F32))],
        [pltpu.VMEM((2, D, 3 * third), BF16), pltpu.VMEM((2, D, 3 * third), F32),
         pltpu.VMEM((D, 128), F32), pltpu.VMEM((D, 128), F32),
         pltpu.VMEM((2, 3 * third, seq), BF16), pltpu.VMEM((D, seq), F32), pltpu.VMEM((D, 8), F32),
         pltpu.VMEM((third, 8), F32)],
        16, "attention_backward",
    )
    bits = list(reversed(dp_bits()))
    count = lax.axis_size("dp")
    qkv = (keep_qkv.astype(F32) + swap(send_qkv, "row").astype(F32)).astype(BF16)
    backs = [back0] + [group_step(a, step) for step, a in ((1, back1), (2, back2), (3, back3))]
    ins = [ins[0]] + [group_step(ins[step], step) for step in (1, 2, 3)]
    rows = 7 * latents + 2 * BIAS_ROWS
    everyone, cond_part = call(
        group_vectors, pos, 1, seq,
        [("w", a) for a in backs] + [("w", cond_low), ("w", w_ada_by_vector)],
        [("w", shape((rows, third), BF16)), ("w", shape(condition.shape, F32))], [], 2,
        "group_vectors",
    )
    everyone = everyone[None]
    for bit in bits[:-2]:
        everyone = jnp.concatenate([everyone, dp_step(everyone, bit)])
    cond_part = cond_part + swap(cond_part, "row")
    fc_parts, qkv, ins, everyone, cond_part = lax.optimization_barrier(
        (fc_parts, qkv, ins, everyone, cond_part)
    )
    qkv_parts = scatter_terms(qkv)
    fc = jnp.sum(fc_parts.astype(F32), axis=0).astype(BF16)
    for bit in bits[:-2]:
        fc = double(fc, bit)
    for bit in bits[-2:-1]:
        everyone = jnp.concatenate([everyone, dp_step(everyone, bit)])
    input_grad = call(
        join_tokens, pos, 4, seq, [("w", a) for a in ins],
        [("j", shape((quarter, tokens), F32))], [], 2, "join_tokens",
    )[0]
    qkv_parts, fc, everyone, input_grad = lax.optimization_barrier(
        (qkv_parts, fc, everyone, input_grad)
    )
    qkv = jnp.sum(qkv_parts.astype(F32), axis=0).astype(BF16)
    qkv = lax.all_to_all(jnp.broadcast_to(qkv[None], (count,) + qkv.shape), "dp", 0, 0)
    for bit in bits[-2:]:
        fc = double(fc, bit)
    for bit in bits[-1:]:
        everyone = jnp.concatenate([everyone, dp_step(everyone, bit)])
    grads_fc = fc.reshape(fc_block[1:]).astype(F32)
    grad_w_ada, grad_b_ada, grad_b_fc1, grad_b_qkv, grad_b_proj, grad_b_fc2 = call(
        modulation_grads, pos, 1, seq, [("w", everyone)],
        [("w", shape((third, 6 * third), F32)), ("w", shape((6, quarter), F32)),
         ("w", shape((4, third), F32)), ("w", shape((2, third), F32)),
         ("w", shape((1, quarter), F32)), ("w", shape((1, quarter), F32))], [], 2,
        "modulation_grads",
    )
    grads_qkv = qkv.reshape(qkv_block[1:]).astype(F32)
    silu_back = jax.vjp(jax.nn.silu, condition)[1]
    cond_grad = silu_back(cond_part)[0]
    return (
        block_output,
        input_grad,
        cond_grad,
        grad_w_ada,
        grad_b_ada,
        grads_qkv,
        grad_b_qkv,
        grads_fc[:, 2 * half :],
        grad_b_proj.reshape(-1),
        grads_fc[:, :half],
        grad_b_fc1.reshape(-1),
        grads_fc[:, half : 2 * half],
        grad_b_fc2.reshape(-1),
    )


def solution(mesh):
    return jax.shard_map(
        local,
        mesh=mesh,
        in_specs=(
            P(("row", "col"), "dp"),
            P("dp", "col"),
            P("col", "row"),
            P(None, ("row", "col")),
            P("row", "col"),
            P(None, "col"),
            P("col", "row"),
            P(("row", "col")),
            P("row", "col"),
            P("col"),
            P("row", "col"),
            P(("row", "col")),
            P(("row", "col"), "dp"),
        ),
        out_specs=(
            P(("row", "col"), "dp"),
            P(("row", "col"), "dp"),
            P("dp", "col"),
            P("col", "row"),
            P(None, ("row", "col")),
            P("row", "col"),
            P(None, "col"),
            P("col", "row"),
            P(("row", "col")),
            P("row", "col"),
            P("col"),
            P("row", "col"),
            P(("row", "col")),
        ),
        check_vma=False,
    )
```

time: 242 us -> 175 us (0.72)
  waiting for transfers between devices: 66.4 us -> 33.5 us
  local copies, waits for them, and re-layouts: 30.9 us -> 5.38 us
  other arithmetic: 23.9 us -> 8.88 us
  Pallas kernels: 65.4 us -> 76.1 us
  matrix products: 2.54 us -> 0 us
    all_to_all x6 -> x3, waiting for transfers between devices: 35.1 us -> 0.11 us  [the longest x1 0.1 us: local(): lax.all_to_all(jnp.broadcast_to(qkv[None], (count,) + qkv.shape), 'dp', 0...]
    ppermute x23 -> x16, waiting for transfers between devices: 31.3 us -> 6.47 us  [swap(): return lax.ppermute(value, axis, [(0, 1), (1, 0)])]
    ppermute x0 -> x6, waiting for transfers between devices: none -> 16.9 us  [dp_step(): return lax.ppermute(value, 'dp', [(at, at ^ bit) for at in range(count)])]
    all_to_all x6 -> x3, starting transfers between devices: 29.1 us -> 15.6 us  [the longest x2 12.2 us: scatter_terms(): return lax.all_to_all(blocks, ('col', 'dp'), 0, 0)]
    ppermute x0 -> x6, starting transfers between devices: none -> 11 us  [dp_step(): return lax.ppermute(value, 'dp', [(at, at ^ bit) for at in range(count)])]
    pallas_call x4 -> x10, Pallas kernels: 65.4 us -> 76.1 us  [call(): pl.pallas_call(kernel, grid_spec=pltpu.PrefetchScalarGridSpec(num_scalar_...]
    ppermute x12 -> x18, waiting for transfers between devices: 0.03 us -> 10 us  [group_step(): return lax.ppermute(value, GROUP, [(at, at ^ step) for at in range(4)])]
    dynamic_update_slice x8 -> x0, other arithmetic: 7.88 us -> none  [collect_tokens(): lax.dynamic_update_slice_in_dim(out, piece.astype(F32), (own ^ step) * wi...]
  transfers between devices with their start and end apart: 41 -> 43, of which waited for: 10 -> 13; matrix products, arithmetic and copies ran while one was open for 21% -> 5% of each run, Pallas kernels for 27% -> 44%
where the time goes in v2:
time: 175 us; the launch traced here: 174 us
  Pallas kernels  76.1 us (43%)
  starting transfers between devices  48.5 us (28%)
  waiting for transfers between devices  33.5 us (19%)
  other arithmetic  8.88 us (5%)
  local copies, waits for them, and re-layouts  5.38 us (3%)
    pallas_call x10, Pallas kernels, call(): pl.pallas_call(kernel, grid_spec=pltpu.PrefetchScalarGridSpec(num_scalar_...  76.1 us
    ppermute x6, waiting for transfers between devices, dp_step(): return lax.ppermute(value, 'dp', [(at, at ^ bit) for at in range(count)])  16.9 us
    ppermute x18, starting transfers between devices, group_step(): return lax.ppermute(value, GROUP, [(at, at ^ step) for at in range(4)])  12.8 us
    all_to_all x2, starting transfers between devices, scatter_terms(): return lax.all_to_all(blocks, ('col', 'dp'), 0, 0)  12.2 us
    ppermute x6, starting transfers between devices, dp_step(): return lax.ppermute(value, 'dp', [(at, at ^ bit) for at in range(count)])  11 us
    ppermute x18, waiting for transfers between devices, group_step(): return lax.ppermute(value, GROUP, [(at, at ^ step) for at in range(4)])  10 us
    ppermute x16, starting transfers between devices, swap(): return lax.ppermute(value, axis, [(0, 1), (1, 0)])  9.07 us
    ppermute x16, waiting for transfers between devices, swap(): return lax.ppermute(value, axis, [(0, 1), (1, 0)])  6.47 us
  transfers between devices with their start and end apart: 43, of which 13 were waited for; matrix products, arithmetic and copies ran while one was open for 5% of the time, Pallas kernels for 44%

profile of v2, /device:TPU:0, one launch (start us, length us, event | category | flops | bytes accessed | tf_op | source)
XLA Modules:
  0.0 173.6 jit_solution(1025451298970122271)
XLA Ops:
  0.6 3.0 %collective-permute-start = (bf16[192,576]{1,0:T(8,128)(2,1)}, bf16[192,576]{1,0:T(8,128)(2,1)S(1)}, u32[]{:S(2)}, u32[]{:S(2)}) collective-permute-start(bf16[192,576]{1,0:T(8,128)(2,1)} %wq0.1), channel_id=1, source_target_pairs={{0,1},{1,0},{2,3},{3,2},{4,5},{5,4},{6,7},{7,6},{8,9},{9,8},{10,11... | collective-permute-start | bytes 663560 | tf_op jit(solution)/shard_map/ppermute | solution.py:539
  4.8 4.7 %modulation_parts.1 = (f32[40,192]{1,0:T(8,128)}, f32[40,192]{1,0:T(8,128)}, f32[40,192]{1,0:T(8,128)}, f32[40,192]{1,0:T(8,128)}, bf16[16,192]{1,0:T(8,128)(2,1)}, /*index=5*/bf16[6,192,192]{2,1,0:T(8,128)(2,1)}) custom-call(s32[2]{0:T(128)} %pad_add_fusion.pos, f32[16,192]{1,0:T(8,128)} %condition.1, bf16[192,1152]{1,0:T(8,128)(2,1)} %w_ada.1, ...), custom_call_target="tpu_custom_call" | custom-call | flops 6000000000 | bytes 1028352 | tf_op jit(solution)/shard_map/modulation_parts/pallas_call | solution.py:518
  9.4 2.5 %collective-permute-done.1.wp1 = bf16[192,192]{1,0:T(8,128)(2,1)S(1)} collective-permute-done((bf16[192,192]{1,0:T(8,128)(2,1)}, bf16[192,192]{1,0:T(8,128)(2,1)S(1)}, u32[]{:S(2)}, u32[]{:S(2)}) %collective-permute-start.1) | collective-permute-done | bytes 73760 | tf_op jit(solution)/shard_map/ppermute | solution.py:539
  11.9 1.8 %collective-permute-start.9 = (f32[40,192]{1,0:T(8,128)}, f32[40,192]{1,0:T(8,128)S(1)}, u32[]{:S(2)}, u32[]{:S(2)}) collective-permute-start(f32[40,192]{1,0:T(8,128)} %get-tuple-element.145), channel_id=1, source_target_pairs={{0,1},{1,0},{2,3},{3,2},{4,5},{5,4},{6,7},{7,6},{8,9},{9,8},{10,11... | collective-permute-start | bytes 92168 | tf_op jit(solution)/shard_map/ppermute | solution.py:543
  14.1 2.6 %cut_input.1 = (bf16[96,1024]{1,0:T(8,128)(2,1)}, bf16[96,1024]{1,0:T(8,128)(2,1)}, bf16[96,1024]{1,0:T(8,128)(2,1)}) custom-call(s32[2]{0:T(128)} %pad_add_fusion.pos, bf16[96,4096]{1,0:T(8,128)(2,1)} %x0), custom_call_target="tpu_custom_call" | custom-call | flops 3000000000 | bytes 1376256 | tf_op jit(solution)/shard_map/cut_input/pallas_call | solution.py:518
  16.8 1.7 %collective-permute-start.2 = (bf16[96,1024]{1,0:T(8,128)(2,1)}, bf16[96,1024]{1,0:T(8,128)(2,1)S(1)}, u32[]{:S(2)}, u32[]{:S(2)}) collective-permute-start(bf16[96,1024]{1,0:T(8,128)(2,1)} %get-tuple-element.139), channel_id=1, source_target_pairs={{0,1},{1,0},{2,3},{3,2},{4,5},{5,4},{6,7},{7,6},{8,9},{9,8},{10,11... | collective-permute-start | bytes 589832 | tf_op jit(solution)/shard_map/ppermute | solution.py:543
  19.7 2.6 %cut_grad.1 = (bf16[96,1024]{1,0:T(8,128)(2,1)}, bf16[96,1024]{1,0:T(8,128)(2,1)}, bf16[96,1024]{1,0:T(8,128)(2,1)}) custom-call(s32[2]{0:T(128)} %pad_add_fusion.pos, bf16[96,4096]{1,0:T(8,128)(2,1)} %g0.1), custom_call_target="tpu_custom_call" | custom-call | flops 3000000000 | bytes 1376256 | tf_op jit(solution)/shard_map/cut_grad/pallas_call | solution.py:518
  22.4 2.3 %collective-permute-done.2.x1 = bf16[96,1024]{1,0:T(8,128)(2,1)S(1)} collective-permute-done((bf16[96,1024]{1,0:T(8,128)(2,1)}, bf16[96,1024]{1,0:T(8,128)(2,1)S(1)}, u32[]{:S(2)}, u32[]{:S(2)}) %collective-permute-start.2) | collective-permute-done | bytes 196640 | tf_op jit(solution)/shard_map/ppermute | solution.py:543
  24.7 2.6 %collective-permute-done.4.x3 = bf16[96,1024]{1,0:T(8,128)(2,1)S(1)} collective-permute-done((bf16[96,1024]{1,0:T(8,128)(2,1)}, bf16[96,1024]{1,0:T(8,128)(2,1)S(1)}, u32[]{:S(2)}, u32[]{:S(2)}) %collective-permute-start.4) | collective-permute-done | bytes 196640 | tf_op jit(solution)/shard_map/ppermute | solution.py:543
  29.8 1.6 collective-permute-start.16
  31.5 11.5 %attention_forward.1 = (bf16[384,1024]{1,0:T(8,128)(2,1)}, bf16[384,1024]{1,0:T(8,128)(2,1)}, bf16[2,576,1024]{2,1,0:T(8,128)(2,1)}, bf16[4,6,256,256]{3,2,1,0:T...) custom-call(s32[2]{0:T(128)} %pad_add_fusion.pos, bf16[96,4096]{1,0:T(8,128)(2,1)} %x0, ...), custom_call_target="tpu_custom_call" | custom-call | flops 16000000000 | bytes 12165120 | tf_op jit(solution)/shard_map/attention_forward/pallas_call | solution.py:518
  44.0 1.6 collective-permute-start.19
  47.0 12.4 %mlp_forward.1 = (bf16[96,1024]{1,0:T(8,128)(2,1)}, bf16[96,1024]{1,0:T(8,128)(2,1)}, bf16[96,1024]{1,0:T(8,128)(2,1)}, bf16[96,1024]{1,0:T(8,128)(2,1)}, bf16[3...) custom-call(s32[2]{0:T(128)} %pad_add_fusion.pos, ...), custom_call_target="tpu_custom_call" | custom-call | flops 12000000000 | bytes 14330880 | tf_op jit(solution)/shard_map/mlp_forward/pallas_call | solution.py:518
  59.4 1.7 collective-permute-start.22
  61.6 16.6 %mlp_backward.1 = (f32[384,1024]{1,0:T(8,128)}, bf16[384,1024]{1,0:T(8,128)(2,1)}, f32[4,384,4]{2,1,0:T(8,128)}, bf16[2,192,1728]{2,1,0:T(8,128)(2,1)}, bf16[2,1...) custom-call(s32[2]{0:T(128)} %pad_add_fusion.pos, bf16[96,4096]{1,0:T(8,128)(2,1)} %g0.1, ...), custom_call_target="tpu_custom_call" | custom-call | flops 20000000000 | bytes 20923392 | tf_op jit(solution)/shard_map/mlp_backward/pallas_call | solution.py:518
  78.4 3.3 %collective-permute-done.25 = bf16[2,192,1728]{2,1,0:T(8,128)(2,1)S(1)} collective-permute-done((bf16[2,192,1728]{2,1,0:T(8,128)(2,1)}, bf16[2,192,1728]{2,1,0:T(8,128)(2,1)S(1)}, u32[]{:S(2)}, u32[]{:S(2)}) %collective-permute-start.25) | collective-permute-done | bytes 1327136 | tf_op jit(solution)/shard_map/ppermute | solution.py:539
  81.7 2.8 %add_convert_fusion = bf16[2,192,1728]{2,1,0:T(8,128)(2,1)} fusion(bf16[2,192,1728]{2,1,0:T(8,128)(2,1)S(1)} %collective-permute-done.25, bf16[2,192,1728]{2,1,0:T(8,128)(2,1)} %get-tuple-element.203), kind=kLoop, calls=%fused_computation | loop fusion | flops 2654208 | bytes 3981312 | tf_op jit(solution)/shard_map/convert_element_type | solution.py:690
  84.5 7.0 %all-to-all-start = ((bf16[16,24,1728]{2,1,0:T(8,128)(2,1)}), bf16[16,24,1728]{2,1,0:T(8,128)(2,1)S(1)}, u32[]{:S(2)}, u32[]{:S(2)}) async-start(bf16[16,24,1728]{2,1,0:T(8,128)(2,1)} %bitcast.4), calls=%async_computation | async-start | bytes 2752512 | tf_op jit(solution)/shard_map/all_to_all | solution.py:570
  91.6 15.4 %attention_backward.1 = (bf16[96,1024]{1,0:T(8,128)(2,1)}, bf16[96,1024]{1,0:T(8,128)(2,1)}, bf16[96,1024]{1,0:T(8,128)(2,1)}, bf16[96,1024]{1,0:T(8,128)(2,1)},...) custom-call(s32[2]{0:T(128)} %pad_add_fusion.pos, ...), custom_call_target="tpu_custom_call" | custom-call | flops 16000000000 | bytes 14558208 | tf_op jit(solution)/shard_map/attention_backward/pallas_call | solution.py:518
  107.0 2.0 %collective-permute-start.30 = (f32[40,192]{1,0:T(8,128)}, f32[40,192]{1,0:T(8,128)S(1)}, u32[]{:S(2)}, u32[]{:S(2)}) collective-permute-start(f32[40,192]{1,0:T(8,128)} %get-tuple-element.230), channel_id=1, source_target_pairs={{0,1},{1,0},{2,3},{3,2},{4,5},{5,4},{6,7},{7,6},{8,9},{9,8},{10,11... | collective-permute-start | bytes 92168 | tf_op jit(solution)/shard_map/ppermute | solution.py:543
  109.2 2.1 %collective-permute-done.30.pack1 = f32[40,192]{1,0:T(8,128)S(1)} collective-permute-done((f32[40,192]{1,0:T(8,128)}, f32[40,192]{1,0:T(8,128)S(1)}, u32[]{:S(2)}, u32[]{:S(2)}) %collective-permute-start.30) | collective-permute-done | bytes 30752 | tf_op jit(solution)/shard_map/ppermute | solution.py:543
  113.4 3.0 %group_vectors.1 = (bf16[128,192]{1,0:T(8,128)(2,1)}, f32[16,192]{1,0:T(8,128)}) custom-call(s32[2]{0:T(128)} %pad_add_fusion.pos, f32[40,192]{1,0:T(8,128)} %get-tuple-element.229.pack0, f32[40,192]{1,0:T(8,128)} %copy-done.38, f32[40,192]{1,0:T(8,128)} %copy-done.39, f32[40,192]{1,0:T(8,128)} %copy-done.40, bf16[16,192]{1,0:T(8,128)(2,1)} %get-tuple-element.233.cond, ...), custom_call_target="tpu_custom_call" | custom-call | flops 2000000000 | bytes 632832 | tf_op jit(solution)/shard_map/group_vectors/pallas_call | solution.py:518
  116.4 3.1 %collective-permute-start.33 = (bf16[1,128,192]{2,1,0:T(8,128)(2,1)}, bf16[1,128,192]{2,1,0:T(8,128)(2,1)S(1)}, u32[]{:S(2)}, u32[]{:S(2)}) collective-permute-start(bf16[1,128,192]{2,1,0:T(8,128)(2,1)} %bitcast.31), channel_id=1, source_target_pairs={{0,16},{4,20},{8,24},{12,28},{16,0},{20,4},{24,8},{28,12},{1,17},{... | collective-permute-start | bytes 147464 | tf_op jit(solution)/shard_map/ppermute | solution.py:563
  122.6 4.8 %collective-permute-done.33 = bf16[1,128,192]{2,1,0:T(8,128)(2,1)S(1)} collective-permute-done((bf16[1,128,192]{2,1,0:T(8,128)(2,1)}, bf16[1,128,192]{2,1,0:T(8,128)(2,1)S(1)}, u32[]{:S(2)}, u32[]{:S(2)}) %collective-permute-start.33) | collective-permute-done | bytes 49184 | tf_op jit(solution)/shard_map/ppermute | solution.py:563
  130.6 5.2 %all-to-all-start.1 = ((bf16[16,24,576]{2,1,0:T(8,128)(2,1)}), bf16[16,24,576]{2,1,0:T(8,128)(2,1)S(1)}, u32[]{:S(2)}, u32[]{:S(2)}) async-start(bf16[16,24,576]{2,1,0:T(8,128)(2,1)} %bitcast.6), calls=%async_computation.1 | async-start | bytes 983040 | tf_op jit(solution)/shard_map/all_to_all | solution.py:570
  136.0 2.9 %collective-permute-start.35 = (bf16[24,1728]{1,0:T(8,128)(2,1)S(1)}, bf16[24,1728]{1,0:T(8,128)(2,1)S(1)}, u32[]{:S(2)}, u32[]{:S(2)}) collective-permute-start(bf16[24,1728]{1,0:T(8,128)(2,1)S(1)} %reduce_sum.24), channel_id=1, source_target_pairs={{0,16},{4,20},{8,24},{12,28},{16,0},{20,4},{24,8},{28,12},{1,17},{... | collective-permute-start | bytes 248840 | tf_op jit(solution)/shard_map/ppermute | solution.py:563
  140.3 3.6 %join_tokens.1 = f32[96,4096]{1,0:T(8,128)} custom-call(s32[2]{0:T(128)} %pad_add_fusion.pos, bf16[96,1024]{1,0:T(8,128)(2,1)} %get-tuple-element.240.x0, bf16[96,1024]{1,0:T(8,128)(2,1)} %copy-done.30, bf16[96,1024]{1,0:T(8,128)(2,1)} %copy-done.31, bf16[96,1024]{1,0:T(8,128)(2,1)} %collective-permute-done.29.x3), custom_call_target="tpu_custom_call" | custom-call | flops 2000000000 | bytes 2359296 | tf_op jit(solution)/shard_map/join_tokens/pallas_call | solution.py:518
  144.0 9.5 %collective-permute-done.35 = bf16[24,1728]{1,0:T(8,128)(2,1)S(1)} collective-permute-done((bf16[24,1728]{1,0:T(8,128)(2,1)S(1)}, bf16[24,1728]{1,0:T(8,128)(2,1)S(1)}, u32[]{:S(2)}, u32[]{:S(2)}) %collective-permute-start.35) | collective-permute-done | bytes 82976 | tf_op jit(solution)/shard_map/ppermute | solution.py:563
  156.5 3.4 %all-to-all-start.2 = ((bf16[8,24,576]{2,1,0:T(8,128)(2,1)}), bf16[8,24,576]{2,1,0:T(8,128)(2,1)S(1)}, u32[]{:S(2)}, u32[]{:S(2)}) async-start(bf16[8,24,576]{2,1,0:T(8,128)(2,1)} %broadcast_in_dim.10), calls=%async_computation.2 | async-start | bytes 491520 | tf_op jit(solution)/shard_map/all_to_all | solution.py:740
  160.0 2.0 %collective-permute-start.39 = (bf16[2,2,24,1728]{3,2,1,0:T(8,128)(2,1)S(1)}, bf16[2,2,24,1728]{3,2,1,0:T(8,128)(2,1)S(1)}, u32[]{:S(2)}, u32[]{:S(2)}) collective-permute-start(bf16[2,2,24,1728]{3,2,1,0:T(8,128)(2,1)S(1)} %pad_maximum_fusion.2), channel_id=1, source_target_pairs={{0,4},{4,0},{8,12},{12,8},{16,20},{20,16},{24,28},{28,24},{1,5},{5... | collective-permute-start | bytes 995336 | tf_op jit(solution)/shard_map/ppermute | solution.py:563
  162.9 3.8 %modulation_grads.1 = (f32[192,1152]{1,0:T(8,128)}, f32[6,96]{1,0:T(8,128)}, f32[4,192]{1,0:T(4,128)}, f32[2,192]{1,0:T(2,128)}, f32[1,96]{1,0:T(1,128)}, /*index=5*/f32[1,96]{1,0:T(1,128)}) custom-call(s32[2]{0:T(128)} %pad_add_fusion.pos, bf16[8,128,192]{2,1,0:T(8,128)(2,1)} %pad_maximum_fusion.1.refs_0_), custom_call_target="tpu_custom_call" | custom-call | flops 2000000000 | bytes 1285632 | tf_op jit(solution)/shard_map/modulation_grads/pallas_call | solution.py:518
  168.9 2.6 %collective-permute-done.39 = bf16[2,2,24,1728]{3,2,1,0:T(8,128)(2,1)S(1)} collective-permute-done((bf16[2,2,24,1728]{3,2,1,0:T(8,128)(2,1)S(1)}, bf16[2,2,24,1728]{3,2,1,0:T(8,128)(2,1)S(1)}, u32[]{:S(2)}, u32[]{:S(2)}) %collective-permute-start.39) | collective-permute-done | bytes 331808 | tf_op jit(solution)/shard_map/ppermute | solution.py:563
  (171 shorter events, 26.6 us)
Async XLA Ops:
  0.6 11.3 %collective-permute-start = (bf16[192,576]{1,0:T(8,128)(2,1)}, bf16[192,576]{1,0:T(8,128)(2,1)S(1)}, u32[]{:S(2)}, u32[]{:S(2)}) collective-permute-start(bf16[192,576]{1,0:T(8,128)(2,1)} %wq0.1), channel_id=1, source_target_pairs={{0,1},{1,0},{2,3},{3,2},{4,5},{5,4},{6,7},{7,6},{8,9},{9,8},{10,11... | collective-permute-start | bytes 663560 | tf_op jit(solution)/shard_map/ppermute | solution.py:539
  3.6 14.9 %collective-permute-start.5 = (bf16[192,576]{1,0:T(8,128)(2,1)}, bf16[192,576]{1,0:T(8,128)(2,1)S(1)}, u32[]{:S(2)}, u32[]{:S(2)}) collective-permute-start(bf16[192,576]{1,0:T(8,128)(2,1)} %wq0.1), channel_id=1, source_target_pairs={{0,2},{2,0},{1,3},{3,1},{4,6},{6,4},{5,7},{7,5},{8,10},{10,8},{9,1... | collective-permute-start | bytes 663560 | tf_op jit(solution)/shard_map/ppermute | solution.py:539
  3.6 8.3 %collective-permute-start.1 = (bf16[192,192]{1,0:T(8,128)(2,1)}, bf16[192,192]{1,0:T(8,128)(2,1)S(1)}, u32[]{:S(2)}, u32[]{:S(2)}) collective-permute-start(bf16[192,192]{1,0:T(8,128)(2,1)} %wp0.1), channel_id=1, source_target_pairs={{0,1},{1,0},{2,3},{3,2},{4,5},{5,4},{6,7},{7,6},{8,9},{9,8},{10,11... | collective-permute-start | bytes 221192 | tf_op jit(solution)/shard_map/ppermute | solution.py:539
  3.8 13.0 %collective-permute-start.7 = (bf16[192,192]{1,0:T(8,128)(2,1)}, bf16[192,192]{1,0:T(8,128)(2,1)S(1)}, u32[]{:S(2)}, u32[]{:S(2)}) collective-permute-start(bf16[192,192]{1,0:T(8,128)(2,1)} %wp0.1), channel_id=1, source_target_pairs={{0,2},{2,0},{1,3},{3,1},{4,6},{6,4},{5,7},{7,5},{8,10},{10,8},{9,1... | collective-permute-start | bytes 221192 | tf_op jit(solution)/shard_map/ppermute | solution.py:539
  11.9 6.6 %collective-permute-start.9 = (f32[40,192]{1,0:T(8,128)}, f32[40,192]{1,0:T(8,128)S(1)}, u32[]{:S(2)}, u32[]{:S(2)}) collective-permute-start(f32[40,192]{1,0:T(8,128)} %get-tuple-element.145), channel_id=1, source_target_pairs={{0,1},{1,0},{2,3},{3,2},{4,5},{5,4},{6,7},{7,6},{8,9},{9,8},{10,11... | collective-permute-start | bytes 92168 | tf_op jit(solution)/shard_map/ppermute | solution.py:543
  16.8 8.0 %collective-permute-start.2 = (bf16[96,1024]{1,0:T(8,128)(2,1)}, bf16[96,1024]{1,0:T(8,128)(2,1)S(1)}, u32[]{:S(2)}, u32[]{:S(2)}) collective-permute-start(bf16[96,1024]{1,0:T(8,128)(2,1)} %get-tuple-element.139), channel_id=1, source_target_pairs={{0,1},{1,0},{2,3},{3,2},{4,5},{5,4},{6,7},{7,6},{8,9},{9,8},{10,11... | collective-permute-start | bytes 589832 | tf_op jit(solution)/shard_map/ppermute | solution.py:543
  18.6 8.8 %collective-permute-start.4 = (bf16[96,1024]{1,0:T(8,128)(2,1)}, bf16[96,1024]{1,0:T(8,128)(2,1)S(1)}, u32[]{:S(2)}, u32[]{:S(2)}) collective-permute-start(bf16[96,1024]{1,0:T(8,128)(2,1)} %get-tuple-element.141), channel_id=1, source_target_pairs={{0,3},{1,2},{2,1},{3,0},{4,7},{5,6},{6,5},{7,4},{8,11},{9,10},{10,... | collective-permute-start | bytes 589832 | tf_op jit(solution)/shard_map/ppermute | solution.py:543
  19.0 8.4 %collective-permute-start.6 = (bf16[192,576]{1,0:T(8,128)(2,1)S(1)}, bf16[192,576]{1,0:T(8,128)(2,1)S(1)}, u32[]{:S(2)}, u32[]{:S(2)}) collective-permute-start(bf16[192,576]{1,0:T(8,128)(2,1)S(1)} %collective-permute-done.wq1), channel_id=1, source_target_pairs={{0,2},{2,0},{1,3},{3,1},{4,6},{6,4},{5,7},{7,5},{8,10},{10,8},{9,1... | collective-permute-start | bytes 663560 | tf_op jit(solution)/shard_map/ppermute | solution.py:539
  27.4 15.9 %collective-permute-start.12 = (bf16[192,768]{1,0:T(8,128)(2,1)S(1)}, bf16[192,768]{1,0:T(8,128)(2,1)S(1)}, u32[]{:S(2)}, u32[]{:S(2)}) collective-permute-start(bf16[192,768]{1,0:T(8,128)(2,1)S(1)} %copy-done.4), channel_id=1, source_target_pairs={{0,1},{1,0},{2,3},{3,2},{4,5},{5,4},{6,7},{7,6},{8,9},{9,8},{10,11... | collective-permute-start | bytes 884744 | tf_op jit(solution)/shard_map/ppermute | solution.py:539
  28.9 14.5 %collective-permute-start.14 = (bf16[192,768]{1,0:T(8,128)(2,1)S(1)}, bf16[192,768]{1,0:T(8,128)(2,1)S(1)}, u32[]{:S(2)}, u32[]{:S(2)}) collective-permute-start(bf16[192,768]{1,0:T(8,128)(2,1)S(1)} %copy-done.4), channel_id=1, source_target_pairs={{0,2},{2,0},{1,3},{3,1},{4,6},{6,4},{5,7},{7,5},{8,10},{10,8},{9,1... | collective-permute-start | bytes 884744 | tf_op jit(solution)/shard_map/ppermute | solution.py:539
  29.4 14.0 %collective-permute-start.13 = (bf16[192,768]{1,0:T(8,128)(2,1)S(1)}, bf16[192,768]{1,0:T(8,128)(2,1)S(1)}, u32[]{:S(2)}, u32[]{:S(2)}) collective-permute-start(bf16[192,768]{1,0:T(8,128)(2,1)S(1)} %copy-done.5), channel_id=1, source_target_pairs={{0,1},{1,0},{2,3},{3,2},{4,5},{5,4},{6,7},{7,6},{8,9},{9,8},{10,11... | collective-permute-start | bytes 884744 | tf_op jit(solution)/shard_map/ppermute | solution.py:539
  29.8 13.6 %collective-permute-start.15 = (bf16[192,768]{1,0:T(8,128)(2,1)S(1)}, bf16[192,768]{1,0:T(8,128)(2,1)S(1)}, u32[]{:S(2)}, u32[]{:S(2)}) collective-permute-start(bf16[192,768]{1,0:T(8,128)(2,1)S(1)} %copy-done.5), channel_id=1, source_target_pairs={{0,2},{2,0},{1,3},{3,1},{4,6},{6,4},{5,7},{7,5},{8,10},{10,8},{9,1... | collective-permute-start | bytes 884744 | tf_op jit(solution)/shard_map/ppermute | solution.py:539
  29.8 13.5 %collective-permute-start.16 = (bf16[1,768]{1,0:T(2,128)(2,1)S(1)}, bf16[1,768]{1,0:T(2,128)(2,1)S(1)}, u32[]{:S(2)}, u32[]{:S(2)}) collective-permute-start(bf16[1,768]{1,0:T(2,128)(2,1)S(1)} %reshape.59.b10), channel_id=1, source_target_pairs={{0,1},{1,0},{2,3},{3,2},{4,5},{5,4},{6,7},{7,6},{8,9},{9,8},{10,11... | collective-permute-start | bytes 4616 | tf_op jit(solution)/shard_map/ppermute | solution.py:539
  44.0 15.4 %collective-permute-start.19 = (bf16[96,1024]{1,0:T(8,128)(2,1)S(1)}, bf16[96,1024]{1,0:T(8,128)(2,1)S(1)}, u32[]{:S(2)}, u32[]{:S(2)}) collective-permute-start(bf16[96,1024]{1,0:T(8,128)(2,1)S(1)} %copy-done.20), channel_id=1, source_target_pairs={{0,1},{1,0},{2,3},{3,2},{4,5},{5,4},{6,7},{7,6},{8,9},{9,8},{10,11... | collective-permute-start | bytes 589832 | tf_op jit(solution)/shard_map/ppermute | solution.py:543
  45.6 13.7 %collective-permute-start.20 = (bf16[96,1024]{1,0:T(8,128)(2,1)S(1)}, bf16[96,1024]{1,0:T(8,128)(2,1)S(1)}, u32[]{:S(2)}, u32[]{:S(2)}) collective-permute-start(bf16[96,1024]{1,0:T(8,128)(2,1)S(1)} %copy-done.19), channel_id=1, source_target_pairs={{0,2},{1,3},{2,0},{3,1},{4,6},{5,7},{6,4},{7,5},{8,10},{9,11},{10,... | collective-permute-start | bytes 589832 | tf_op jit(solution)/shard_map/ppermute | solution.py:543
  45.6 13.8 %collective-permute-start.21 = (bf16[96,1024]{1,0:T(8,128)(2,1)S(1)}, bf16[96,1024]{1,0:T(8,128)(2,1)S(1)}, u32[]{:S(2)}, u32[]{:S(2)}) collective-permute-start(bf16[96,1024]{1,0:T(8,128)(2,1)S(1)} %copy-done.18), channel_id=1, source_target_pairs={{0,3},{1,2},{2,1},{3,0},{4,7},{5,6},{6,5},{7,4},{8,11},{9,10},{10,... | collective-permute-start | bytes 589832 | tf_op jit(solution)/shard_map/ppermute | solution.py:543
  59.4 18.9 %collective-permute-start.22 = (bf16[96,1024]{1,0:T(8,128)(2,1)}, bf16[96,1024]{1,0:T(8,128)(2,1)S(1)}, u32[]{:S(2)}, u32[]{:S(2)}) collective-permute-start(bf16[96,1024]{1,0:T(8,128)(2,1)} %get-tuple-element.205), channel_id=1, source_target_pairs={{0,1},{1,0},{2,3},{3,2},{4,5},{5,4},{6,7},{7,6},{8,9},{9,8},{10,11... | collective-permute-start | bytes 589832 | tf_op jit(solution)/shard_map/ppermute | solution.py:543
  61.1 17.2 %collective-permute-start.23 = (bf16[96,1024]{1,0:T(8,128)(2,1)}, bf16[96,1024]{1,0:T(8,128)(2,1)S(1)}, u32[]{:S(2)}, u32[]{:S(2)}) collective-permute-start(bf16[96,1024]{1,0:T(8,128)(2,1)} %get-tuple-element.206), channel_id=1, source_target_pairs={{0,2},{1,3},{2,0},{3,1},{4,6},{5,7},{6,4},{7,5},{8,10},{9,11},{10,... | collective-permute-start | bytes 589832 | tf_op jit(solution)/shard_map/ppermute | solution.py:543
  61.1 17.2 %collective-permute-start.24 = (bf16[96,1024]{1,0:T(8,128)(2,1)}, bf16[96,1024]{1,0:T(8,128)(2,1)S(1)}, u32[]{:S(2)}, u32[]{:S(2)}) collective-permute-start(bf16[96,1024]{1,0:T(8,128)(2,1)} %get-tuple-element.207), channel_id=1, source_target_pairs={{0,3},{1,2},{2,1},{3,0},{4,7},{5,6},{6,5},{7,4},{8,11},{9,10},{10,... | collective-permute-start | bytes 589832 | tf_op jit(solution)/shard_map/ppermute | solution.py:543
  84.5 46.1 %all-to-all-start = ((bf16[16,24,1728]{2,1,0:T(8,128)(2,1)}), bf16[16,24,1728]{2,1,0:T(8,128)(2,1)S(1)}, u32[]{:S(2)}, u32[]{:S(2)}) async-start(bf16[16,24,1728]{2,1,0:T(8,128)(2,1)} %bitcast.4), calls=%async_computation | async-start | bytes 2752512 | tf_op jit(solution)/shard_map/all_to_all | solution.py:570
  107.0 21.3 %collective-permute-start.26 = (bf16[2,192,576]{2,1,0:T(8,128)(2,1)}, bf16[2,192,576]{2,1,0:T(8,128)(2,1)S(1)}, u32[]{:S(2)}, u32[]{:S(2)}) collective-permute-start(bf16[2,192,576]{2,1,0:T(8,128)(2,1)} %get-tuple-element.224), channel_id=1, source_target_pairs={{0,2},{2,0},{1,3},{3,1},{4,6},{6,4},{5,7},{7,5},{8,10},{10,8},{9,1... | collective-permute-start | bytes 1327112 | tf_op jit(solution)/shard_map/ppermute | solution.py:539
  116.4 11.0 %collective-permute-start.33 = (bf16[1,128,192]{2,1,0:T(8,128)(2,1)}, bf16[1,128,192]{2,1,0:T(8,128)(2,1)S(1)}, u32[]{:S(2)}, u32[]{:S(2)}) collective-permute-start(bf16[1,128,192]{2,1,0:T(8,128)(2,1)} %bitcast.31), channel_id=1, source_target_pairs={{0,16},{4,20},{8,24},{12,28},{16,0},{20,4},{24,8},{28,12},{1,17},{... | collective-permute-start | bytes 147464 | tf_op jit(solution)/shard_map/ppermute | solution.py:563
  119.7 9.4 %collective-permute-start.27 = (bf16[96,1024]{1,0:T(8,128)(2,1)S(1)}, bf16[96,1024]{1,0:T(8,128)(2,1)S(1)}, u32[]{:S(2)}, u32[]{:S(2)}) collective-permute-start(bf16[96,1024]{1,0:T(8,128)(2,1)S(1)} %copy-done.17), channel_id=1, source_target_pairs={{0,1},{1,0},{2,3},{3,2},{4,5},{5,4},{6,7},{7,6},{8,9},{9,8},{10,11... | collective-permute-start | bytes 589832 | tf_op jit(solution)/shard_map/ppermute | solution.py:543
  120.5 8.6 %collective-permute-start.28 = (bf16[96,1024]{1,0:T(8,128)(2,1)S(1)}, bf16[96,1024]{1,0:T(8,128)(2,1)S(1)}, u32[]{:S(2)}, u32[]{:S(2)}) collective-permute-start(bf16[96,1024]{1,0:T(8,128)(2,1)S(1)} %copy-done.16), channel_id=1, source_target_pairs={{0,2},{1,3},{2,0},{3,1},{4,6},{5,7},{6,4},{7,5},{8,10},{9,11},{10,... | collective-permute-start | bytes 589832 | tf_op jit(solution)/shard_map/ppermute | solution.py:543
  120.9 9.7 %collective-permute-start.29 = (bf16[96,1024]{1,0:T(8,128)(2,1)S(1)}, bf16[96,1024]{1,0:T(8,128)(2,1)}, u32[]{:S(2)}, u32[]{:S(2)}) collective-permute-start(bf16[96,1024]{1,0:T(8,128)(2,1)S(1)} %copy-done.15), channel_id=1, source_target_pairs={{0,3},{1,2},{2,1},{3,0},{4,7},{5,6},{6,5},{7,4},{8,11},{9,10},{10,... | collective-permute-start | bytes 589832 | tf_op jit(solution)/shard_map/ppermute | solution.py:543
  130.6 23.0 %all-to-all-start.1 = ((bf16[16,24,576]{2,1,0:T(8,128)(2,1)}), bf16[16,24,576]{2,1,0:T(8,128)(2,1)S(1)}, u32[]{:S(2)}, u32[]{:S(2)}) async-start(bf16[16,24,576]{2,1,0:T(8,128)(2,1)} %bitcast.6), calls=%async_computation.1 | async-start | bytes 983040 | tf_op jit(solution)/shard_map/all_to_all | solution.py:570
  136.0 17.4 %collective-permute-start.35 = (bf16[24,1728]{1,0:T(8,128)(2,1)S(1)}, bf16[24,1728]{1,0:T(8,128)(2,1)S(1)}, u32[]{:S(2)}, u32[]{:S(2)}) collective-permute-start(bf16[24,1728]{1,0:T(8,128)(2,1)S(1)} %reduce_sum.24), channel_id=1, source_target_pairs={{0,16},{4,20},{8,24},{12,28},{16,0},{20,4},{24,8},{28,12},{1,17},{... | collective-permute-start | bytes 248840 | tf_op jit(solution)/shard_map/ppermute | solution.py:563
  138.9 14.6 %collective-permute-start.36 = (bf16[2,128,192]{2,1,0:T(8,128)(2,1)S(1)}, bf16[2,128,192]{2,1,0:T(8,128)(2,1)S(1)}, u32[]{:S(2)}, u32[]{:S(2)}) collective-permute-start(bf16[2,128,192]{2,1,0:T(8,128)(2,1)S(1)} %pad_maximum_fusion.5), channel_id=1, source_target_pairs={{0,8},{4,12},{8,0},{12,4},{16,24},{20,28},{24,16},{28,20},{1,9},{5... | collective-permute-start | bytes 294920 | tf_op jit(solution)/shard_map/ppermute | solution.py:563
  153.6 6.4 %collective-permute-start.38 = (bf16[2,24,1728]{2,1,0:T(8,128)(2,1)S(1)}, bf16[2,24,1728]{2,1,0:T(8,128)(2,1)S(1)}, u32[]{:S(2)}, u32[]{:S(2)}) collective-permute-start(bf16[2,24,1728]{2,1,0:T(8,128)(2,1)S(1)} %pad_maximum_fusion.4), channel_id=1, source_target_pairs={{0,8},{4,12},{8,0},{12,4},{16,24},{20,28},{24,16},{28,20},{1,9},{5... | collective-permute-start | bytes 497672 | tf_op jit(solution)/shard_map/ppermute | solution.py:563
  154.6 7.4 %collective-permute-start.37 = (bf16[4,128,192]{2,1,0:T(8,128)(2,1)S(1)}, bf16[4,128,192]{2,1,0:T(8,128)(2,1)S(1)}, u32[]{:S(2)}, u32[]{:S(2)}) collective-permute-start(bf16[4,128,192]{2,1,0:T(8,128)(2,1)S(1)} %pad_maximum_fusion.3), channel_id=1, source_target_pairs={{0,4},{4,0},{8,12},{12,8},{16,20},{20,16},{24,28},{28,24},{1,5},{5... | collective-permute-start | bytes 589832 | tf_op jit(solution)/shard_map/ppermute | solution.py:563
  156.5 11.6 %all-to-all-start.2 = ((bf16[8,24,576]{2,1,0:T(8,128)(2,1)}), bf16[8,24,576]{2,1,0:T(8,128)(2,1)S(1)}, u32[]{:S(2)}, u32[]{:S(2)}) async-start(bf16[8,24,576]{2,1,0:T(8,128)(2,1)} %broadcast_in_dim.10), calls=%async_computation.2 | async-start | bytes 491520 | tf_op jit(solution)/shard_map/all_to_all | solution.py:740
  160.0 11.5 %collective-permute-start.39 = (bf16[2,2,24,1728]{3,2,1,0:T(8,128)(2,1)S(1)}, bf16[2,2,24,1728]{3,2,1,0:T(8,128)(2,1)S(1)}, u32[]{:S(2)}, u32[]{:S(2)}) collective-permute-start(bf16[2,2,24,1728]{3,2,1,0:T(8,128)(2,1)S(1)} %pad_maximum_fusion.2), channel_id=1, source_target_pairs={{0,4},{4,0},{8,12},{12,8},{16,20},{20,16},{24,28},{28,24},{1,5},{5... | collective-permute-start | bytes 995336 | tf_op jit(solution)/shard_map/ppermute | solution.py:563
  (53 other events, 322.8 us)

commit v3 on v2

--- a/solution.py
+++ b/solution.py
@@ -14,7 +14,7 @@
 BF16 = jnp.bfloat16
 F32 = jnp.float32
 GROUP = ("row", "col")
-VMEM_BYTES = 56 * 1024 * 1024
+LIMITS = {"modulation_parts": 60, "attention_forward": 15, "mlp_forward": 16, "mlp_backward": 27, "attention_backward": 20}
 
 
 def dot_nn(left, right):
@@ -105,9 +105,10 @@
 
 
 def modulation_parts(
-    pos, condition, w_ada, b_ada, b_qkv, b_proj, b_fc2,
-    pack0, pack1, pack2, pack3, cond_out, w_ada_out,
+    pos, x, condition, w_ada, b_ada, b_qkv, b_proj, b_fc2,
+    out1, out2, out3, pack0, pack1, pack2, pack3, cond_out, w_ada_out,
 ):
+    cut_tokens(pos, x, out1, out2, out3)
     own, col = pos[0] * 2 + pos[1], pos[1]
     latents = condition.shape[0]
     steps = latents // 4
@@ -326,7 +327,7 @@
 def mlp_backward(
     pos, g0, g1, g2, g3, x, branch, mod, mod_two, act, slope, mlp, attended,
     w10, w11, w12, w13, w20, w21, w22, w23, wp0, wp1, wp2, wp3,
-    hidden_grad_out, context_out, mod_grad_out, send_out, keep_out, sum1_out, sum2_out, sump_out,
+    hidden_grad_out, context_out, mod_grad_out, send_t, send_m, keep_t, keep_m, sum1_out, sum2_out, sump_out,
     g_s, w1_s, w2_s, w2_t, wp_s, acc1, acc2, accp, sum1, sum2, sump,
 ):
     step = pl.program_id(0)
@@ -382,12 +383,12 @@
     def _():
         mine = pl.multiple_of(pos[0] * third, third)
         other = pl.multiple_of((1 - pos[0]) * third, third)
-        for part in range(GROUPS):
-            rows = slice(part * third, (part + 1) * third)
-            for out, at, who in ((send_out, other, 1 - pos[0]), (keep_out, mine, pos[0])):
-                out[part, :, :half] = acc1[part, pl.ds(at, third), :].astype(out.dtype)
-                out[part, :, half : 2 * half] = acc2[part, pl.ds(at, third), :].astype(out.dtype)
-                out[part, :, 2 * half :] = accp[who, rows, :].astype(out.dtype)
+        for part, pair in ((pos[1], (send_m, keep_m)), (1 - pos[1], (send_t, keep_t))):
+            rows = pl.ds(pl.multiple_of(part * third, third), third)
+            for out, at, who in ((pair[0], other, 1 - pos[0]), (pair[1], mine, pos[0])):
+                out[:, :half] = acc1[part, pl.ds(at, third), :].astype(out.dtype)
+                out[:, half : 2 * half] = acc2[part, pl.ds(at, third), :].astype(out.dtype)
+                out[:, 2 * half :] = accp[who, rows, :].astype(out.dtype)
         sum1_out[...] = lane_sum(sum1[...])
         sum2_out[...] = lane_sum(sum2[...])
         sump_out[...] = lane_sum(sump[...])
@@ -397,7 +398,7 @@
     pos, x, mod_one, mod, qkv, probs, context, hidden_grad, mod_grad, sum1, sum2, sump,
     wq0, wq1, wq2, wq3,
     left0, left1, left2, left3,
-    out0, out1, out2, out3, send_out, keep_out, pack0, pack1, pack2, pack3, joined,
+    out0, out1, out2, out3, send_t, send_m, keep_t, keep_m, pack0, pack1, pack2, pack3, joined,
     wq_s, acc, sumq, sumv, grad_s, block_s, mod_s, bias_s,
 ):
     step = pl.program_id(0)
@@ -469,9 +470,9 @@
 
     @pl.when(step == pl.num_programs(0) - 1)
     def _():
-        for part in range(GROUPS):
-            send_out[part] = acc[part, pl.ds(other, third), :].astype(send_out.dtype)
-            keep_out[part] = acc[part, pl.ds(mine, third), :].astype(keep_out.dtype)
+        for part, send, keep in ((pos[1], send_m, keep_m), (1 - pos[1], send_t, keep_t)):
+            send[...] = acc[part, pl.ds(other, third), :].astype(send.dtype)
+            keep[...] = acc[part, pl.ds(mine, third), :].astype(keep.dtype)
 
         own = pos[0] * 2 + pos[1]
         quarter = D // 4
@@ -495,6 +496,7 @@
 
 def call(kernel, pos, steps, seq, inputs, outputs, scratch, micros, name):
     def spec(kind, shape):
+        kind = kind[0]
         rank = len(shape)
         if kind == "t":
             lead = (0,) * (rank - 1)
@@ -511,6 +513,8 @@
             tail = (0,) * (rank - 1)
             return pl.BlockSpec((1,) + shape[1:], lambda i, p: (i,) + tail)
         zeros = (0,) * rank
+        if steps > 1:
+            return pl.BlockSpec(shape, lambda i, p: zeros, pipeline_mode=pl.Buffered(1))
         return pl.BlockSpec(shape, lambda i, p: zeros)
 
     size = sum(a.size * a.dtype.itemsize for _, a in inputs)
@@ -524,9 +528,11 @@
             out_specs=[spec(kind, a.shape) for kind, a in outputs],
             scratch_shapes=scratch,
         ),
-        out_shape=[a for _, a in outputs],
+        out_shape=[
+            pltpu.VMEM(a.shape, a.dtype) if kind.endswith("v") else a for kind, a in outputs
+        ],
         compiler_params=pltpu.CompilerParams(
-            dimension_semantics=("arbitrary",), vmem_limit_bytes=VMEM_BYTES
+            dimension_semantics=("arbitrary",), vmem_limit_bytes=LIMITS.get(name, 16) * 1024 * 1024
         ),
         cost_estimate=pl.CostEstimate(
             flops=int(micros * 1e9), bytes_accessed=size, transcendentals=0
@@ -565,9 +571,12 @@
 
 def scatter_terms(value):
     count = lax.axis_size("dp")
-    cols, rows, columns = value.shape
-    blocks = value.reshape(cols * count, rows // count, columns)
-    return lax.all_to_all(blocks, ("col", "dp"), 0, 0)
+    rows, columns = value.shape
+    return lax.all_to_all(value.reshape(count, rows // count, columns), "dp", 0, 0)
+
+
+def add_low(*values):
+    return sum(value.astype(F32) for value in values).astype(BF16)
 
 
 def after(value, token):
@@ -606,11 +615,11 @@
     pack = ("w", shape((pack_rows, third), F32))
 
     wq_beside, wp_beside = swap(w_qkv, "col"), swap(w_proj, "col")
-    *packs, cond_low, w_ada_by_vector = call(
+    cut1, cut2, cut3, *packs, cond_low, w_ada_by_vector = call(
         modulation_parts, pos, 1, seq,
-        [("w", condition), ("w", w_ada), ("w", b_ada), ("w", b_qkv),
+        [("w", block_input), ("w", condition), ("w", w_ada), ("w", b_ada), ("w", b_qkv),
          ("w", b_proj.reshape(1, -1)), ("w", b_fc2.reshape(1, -1))],
-        [pack] * 4 + [("w", shape(condition.shape, BF16)), ("w", shape((6, third, third), BF16))],
+        [("w", t_piece)] * 3 + [pack] * 4 + [("w", shape(condition.shape, BF16)), ("w", shape((6, third, third), BF16))],
         [], 6, "modulation_parts",
     )
 
@@ -619,10 +628,9 @@
             cut_tokens, pos, 1, seq, [("w", value)], [("w", t_piece)] * 3, [], 3, name
         )
 
-    packs, wq_beside, wp_beside, block_input = lax.optimization_barrier(
-        (packs, wq_beside, wp_beside, block_input)
-    )
-    x_cuts = cut(block_input, "cut_input")
+    packs, wq_beside, wp_beside, x_cuts = lax.optimization_barrier(
+        (packs, wq_beside, wp_beside, (cut1, cut2, cut3))
+    )
     x_moved = [group_step(piece, step) for step, piece in zip((1, 2, 3), x_cuts)]
     packs = [packs[0]] + [group_step(packs[step], step) for step in (1, 2, 3)]
     wq = gather_pieces(w_qkv, wq_beside)
@@ -640,9 +648,9 @@
         attention_forward, pos, steps, seq,
         [("o", block_input)] + [("t", a) for a in x_moved]
         + [("w", a) for a in (*wq, *wp, *packs)],
-        [("t", t_low), ("t", t_low), ("t", shape((2, 3 * third, width), BF16)),
-         ("l", shape((steps, HEADS, seq, seq), BF16)), ("t", t_low), ("t", t_wide),
-         ("l", shape((steps, D, 8), F32))],
+        [("tv", t_low), ("tv", t_low), ("tv", shape((2, 3 * third, width), BF16)),
+         ("lv", shape((steps, HEADS, seq, seq), BF16)), ("tv", t_low), ("tv", t_wide),
+         ("lv", shape((steps, D, 8), F32))],
         [pltpu.VMEM((D, seq), F32), pltpu.VMEM((2, D, 3 * third), BF16),
          pltpu.VMEM((2, 3 * third, D), BF16), pltpu.VMEM((2, D, third), BF16),
          pltpu.VMEM((2, third, D), BF16), pltpu.VMEM((D, 1), F32), pltpu.VMEM((D, 1), F32),
@@ -660,7 +668,7 @@
         mlp_forward, pos, steps, seq,
         [("t", x), ("t", branch), ("l", mod)] + [("w", a) for a in w1 + w2]
         + [("w", a) for a in (*packs, *b_fc1)],
-        [("t", t_piece)] * 4 + [("t", t_low), ("t", t_ff), ("t", t_ff), ("t", t_wide)],
+        [("t", t_piece)] * 4 + [("tv", t_low), ("tv", t_ff), ("tv", t_ff), ("tv", t_wide)],
         [pltpu.VMEM((2, D, half), BF16), pltpu.VMEM((2, half, D), BF16),
          pltpu.VMEM((2, D, half), BF16), pltpu.VMEM((D, seq), F32), pltpu.VMEM((FF, 1), F32),
          pltpu.VMEM((D, 1), F32)],
@@ -668,16 +676,16 @@
     )
     outs, g_moved, mlp = lax.optimization_barrier((outs, g_moved, mlp))
     outs = [outs[0]] + [group_step(outs[step], step) for step in (1, 2, 3)]
-    fc_block = (2, third, 2 * half + third)
-    qkv_block = (2, third, 3 * third)
-    blocks = lambda dims: [("w", shape(dims, BF16))] * 2
-    hidden_grad, context, mod_grad, send_fc, keep_fc, sum1, sum2, sump = call(
+    fc_block = (third, 2 * half + third)
+    qkv_block = (third, 3 * third)
+    blocks = lambda dims: [("w", shape(dims, BF16))] * 4
+    hidden_grad, context, mod_grad, send_t, send_m, keep_t, keep_m, sum1, sum2, sump = call(
         mlp_backward, pos, steps, seq,
         [("o", out_grad)] + [("t", a) for a in g_moved]
         + [("t", x), ("t", branch), ("l", mod), ("t", mod_two), ("t", act), ("t", slope),
            ("t", mlp), ("t", attended)]
         + [("w", a) for a in w1 + w2 + wp],
-        [("t", t_wide), ("t", t_low), ("l", shape((steps, D, 4), F32))] + blocks(fc_block)
+        [("tv", t_wide), ("tv", t_low), ("lv", shape((steps, D, 4), F32))] + blocks(fc_block)
         + [("w", shape((FF, 1), F32)), ("w", shape((D, 1), F32)), ("w", shape((D, 1), F32))],
         [pltpu.VMEM((D, seq), F32), pltpu.VMEM((2, D, half), BF16), pltpu.VMEM((2, D, half), BF16),
          pltpu.VMEM((2, half, D), BF16), pltpu.VMEM((2, D, third), BF16),
@@ -686,12 +694,12 @@
          pltpu.VMEM((D, 128), F32), pltpu.VMEM((D, 128), F32)],
         20, "mlp_backward",
     )
-    outs, send_fc = lax.optimization_barrier((outs, send_fc))
-    fc = (keep_fc.astype(F32) + swap(send_fc, "row").astype(F32)).astype(BF16)
-    fc, context = lax.optimization_barrier((fc, context))
-    fc_parts = scatter_terms(fc)
-
-    *ins, send_qkv, keep_qkv, back0, back1, back2, back3, block_output = call(
+    outs, send_t = lax.optimization_barrier((outs, send_t))
+    theirs = add_low(keep_t, swap(send_t, "row"))
+    theirs, context, send_m = lax.optimization_barrier((theirs, context, send_m))
+    fc_terms = (keep_m, swap(send_m, "row"), swap(theirs, "col"))
+
+    *ins, send_t, send_m, keep_t, keep_m, back0, back1, back2, back3, block_output = call(
         attention_backward, pos, steps, seq,
         [("t", x), ("t", mod_one), ("l", mod), ("t", qkv), ("l", probs), ("t", context),
          ("t", hidden_grad), ("l", mod_grad), ("w", sum1), ("w", sum2), ("w", sump)]
@@ -706,7 +714,10 @@
     )
     bits = list(reversed(dp_bits()))
     count = lax.axis_size("dp")
-    qkv = (keep_qkv.astype(F32) + swap(send_qkv, "row").astype(F32)).astype(BF16)
+    fc_terms, send_t = lax.optimization_barrier((fc_terms, send_t))
+    fc_parts = scatter_terms(add_low(*fc_terms))
+    theirs = add_low(keep_t, swap(send_t, "row"))
+    qkv = add_low(keep_m, swap(send_m, "row"), swap(theirs, "col"))
     backs = [back0] + [group_step(a, step) for step, a in ((1, back1), (2, back2), (3, back3))]
     ins = [ins[0]] + [group_step(ins[step], step) for step in (1, 2, 3)]
     rows = 7 * latents + 2 * BIAS_ROWS
@@ -716,7 +727,7 @@
         [("w", shape((rows, third), BF16)), ("w", shape(condition.shape, F32))], [], 2,
         "group_vectors",
     )
-    everyone = everyone[None]
+    everyone, ins = lax.optimization_barrier((everyone[None], ins))
     for bit in bits[:-2]:
         everyone = jnp.concatenate([everyone, dp_step(everyone, bit)])
     cond_part = cond_part + swap(cond_part, "row")
@@ -725,7 +736,7 @@
     )
     qkv_parts = scatter_terms(qkv)
     fc = jnp.sum(fc_parts.astype(F32), axis=0).astype(BF16)
-    for bit in bits[:-2]:
+    for bit in bits[:-1]:
         fc = double(fc, bit)
     for bit in bits[-2:-1]:
         everyone = jnp.concatenate([everyone, dp_step(everyone, bit)])
@@ -738,11 +749,11 @@
     )
     qkv = jnp.sum(qkv_parts.astype(F32), axis=0).astype(BF16)
     qkv = lax.all_to_all(jnp.broadcast_to(qkv[None], (count,) + qkv.shape), "dp", 0, 0)
-    for bit in bits[-2:]:
+    for bit in bits[-1:]:
         fc = double(fc, bit)
     for bit in bits[-1:]:
         everyone = jnp.concatenate([everyone, dp_step(everyone, bit)])
-    grads_fc = fc.reshape(fc_block[1:]).astype(F32)
+    grads_fc = fc.reshape(fc_block).astype(F32)
     grad_w_ada, grad_b_ada, grad_b_fc1, grad_b_qkv, grad_b_proj, grad_b_fc2 = call(
         modulation_grads, pos, 1, seq, [("w", everyone)],
         [("w", shape((third, 6 * third), F32)), ("w", shape((6, quarter), F32)),
@@ -750,7 +761,7 @@
          ("w", shape((1, quarter), F32)), ("w", shape((1, quarter), F32))], [], 2,
         "modulation_grads",
     )
-    grads_qkv = qkv.reshape(qkv_block[1:]).astype(F32)
+    grads_qkv = qkv.reshape(qkv_block).astype(F32)
     silu_back = jax.vjp(jax.nn.silu, condition)[1]
     cond_grad = silu_back(cond_part)[0]
     return (

time: 175 us -> 159 us (0.909)
  Pallas kernels: 76.1 us -> 57.3 us
  waiting for transfers between devices: 33.5 us -> 40.1 us
  other arithmetic: 8.88 us -> 5.93 us
  starting transfers between devices: 48.5 us -> 50.9 us
  local copies, waits for them, and re-layouts: 5.38 us -> 3.22 us
    pallas_call x10 -> x9, Pallas kernels: 76.1 us -> 57.3 us  [call(): pl.pallas_call(kernel, grid_spec=pltpu.PrefetchScalarGridSpec(num_scalar_...]
    ppermute x16 -> x20, waiting for transfers between devices: 6.47 us -> 12.7 us  [swap(): return lax.ppermute(value, axis, [(0, 1), (1, 0)])]
    ppermute x16 -> x20, starting transfers between devices: 9.07 us -> 12.7 us  [swap(): return lax.ppermute(value, axis, [(0, 1), (1, 0)])]
    ppermute x18, waiting for transfers between devices: 10 us -> 12.9 us  [group_step(): return lax.ppermute(value, GROUP, [(at, at ^ step) for at in range(4)])]
    ppermute x6, waiting for transfers between devices: 16.9 us -> 14.5 us  [dp_step(): return lax.ppermute(value, 'dp', [(at, at ^ bit) for at in range(count)])]
    convert_element_type x4 -> x6, other arithmetic: 4.64 us -> 3.09 us  [the longest x4 2.12 us: add_low(): return sum((value.astype(F32) for value in values)).astype(BF16)]
  transfers between devices with their start and end apart: 43 -> 47, of which waited for: 13 -> 18; matrix products, arithmetic and copies ran while one was open for 5% -> 4% of each run, Pallas kernels for 44% -> 36%
where the time goes in v3:
time: 159 us; the launch traced here: 158 us
  Pallas kernels  57.3 us (36%)
  starting transfers between devices  50.9 us (32%)
  waiting for transfers between devices  40.1 us (25%)
  other arithmetic  5.93 us (4%)
  local copies, waits for them, and re-layouts  3.22 us (2%)
    pallas_call x9, Pallas kernels, call(): pl.pallas_call(kernel, grid_spec=pltpu.PrefetchScalarGridSpec(num_scalar_...  57.3 us
    ppermute x6, waiting for transfers between devices, dp_step(): return lax.ppermute(value, 'dp', [(at, at ^ bit) for at in range(count)])  14.5 us
    ppermute x18, waiting for transfers between devices, group_step(): return lax.ppermute(value, GROUP, [(at, at ^ step) for at in range(4)])  12.9 us
    ppermute x20, waiting for transfers between devices, swap(): return lax.ppermute(value, axis, [(0, 1), (1, 0)])  12.7 us
    ppermute x20, starting transfers between devices, swap(): return lax.ppermute(value, axis, [(0, 1), (1, 0)])  12.7 us
    ppermute x18, starting transfers between devices, group_step(): return lax.ppermute(value, GROUP, [(at, at ^ step) for at in range(4)])  12.7 us
    all_to_all x2, starting transfers between devices, scatter_terms(): lax.all_to_all(value.reshape(count, rows // count, columns), 'dp', 0, 0)  11 us
    ppermute x6, starting transfers between devices, dp_step(): return lax.ppermute(value, 'dp', [(at, at ^ bit) for at in range(count)])  9.99 us
  transfers between devices with their start and end apart: 47, of which 18 were waited for; matrix products, arithmetic and copies ran while one was open for 4% of the time, Pallas kernels for 36%

profile of v3, /device:TPU:0, one launch (start us, length us, event | category | flops | bytes accessed | tf_op | source)
XLA Modules:
  0.0 158.5 jit_solution(18012483004081589685)
XLA Ops:
  0.6 3.0 %collective-permute-start = (bf16[192,576]{1,0:T(8,128)(2,1)}, bf16[192,576]{1,0:T(8,128)(2,1)S(1)}, u32[]{:S(2)}, u32[]{:S(2)}) collective-permute-start(bf16[192,576]{1,0:T(8,128)(2,1)} %wq0.1), channel_id=1, source_target_pairs={{0,1},{1,0},{2,3},{3,2},{4,5},{5,4},{6,7},{7,6},{8,9},{9,8},{10,11... | collective-permute-start | bytes 663560 | tf_op jit(solution)/shard_map/ppermute | solution.py:545
  4.8 5.3 %modulation_parts.1 = (bf16[96,1024]{1,0:T(8,128)(2,1)}, bf16[96,1024]{1,0:T(8,128)(2,1)}, bf16[96,1024]{1,0:T(8,128)(2,1)}, f32[40,192]{1,0:T(8,128)}, f32[40,1...) custom-call(s32[2]{0:T(128)} %pad_add_fusion.pos, ...), custom_call_target="tpu_custom_call" | custom-call | flops 6000000000 | bytes 2404608 | tf_op jit(solution)/shard_map/modulation_parts/pallas_call | solution.py:522
  10.0 1.9 %collective-permute-done.1.wp1 = bf16[192,192]{1,0:T(8,128)(2,1)S(1)} collective-permute-done((bf16[192,192]{1,0:T(8,128)(2,1)}, bf16[192,192]{1,0:T(8,128)(2,1)S(1)}, u32[]{:S(2)}, u32[]{:S(2)}) %collective-permute-start.1) | collective-permute-done | bytes 73760 | tf_op jit(solution)/shard_map/ppermute | solution.py:545
  12.0 1.8 %collective-permute-start.9 = (f32[40,192]{1,0:T(8,128)}, f32[40,192]{1,0:T(8,128)S(1)}, u32[]{:S(2)}, u32[]{:S(2)}) collective-permute-start(f32[40,192]{1,0:T(8,128)} %get-tuple-element.163), channel_id=1, source_target_pairs={{0,1},{1,0},{2,3},{3,2},{4,5},{5,4},{6,7},{7,6},{8,9},{9,8},{10,11... | collective-permute-start | bytes 92168 | tf_op jit(solution)/shard_map/ppermute | solution.py:549
  14.2 1.7 %collective-permute-start.2 = (bf16[96,1024]{1,0:T(8,128)(2,1)}, bf16[96,1024]{1,0:T(8,128)(2,1)S(1)}, u32[]{:S(2)}, u32[]{:S(2)}) collective-permute-start(bf16[96,1024]{1,0:T(8,128)(2,1)} %get-tuple-element.157), channel_id=1, source_target_pairs={{0,1},{1,0},{2,3},{3,2},{4,5},{5,4},{6,7},{7,6},{8,9},{9,8},{10,11... | collective-permute-start | bytes 589832 | tf_op jit(solution)/shard_map/ppermute | solution.py:549
  16.3 2.0 %collective-permute-start.6 = (bf16[192,576]{1,0:T(8,128)(2,1)S(1)}, bf16[192,576]{1,0:T(8,128)(2,1)S(1)}, u32[]{:S(2)}, u32[]{:S(2)}) collective-permute-start(bf16[192,576]{1,0:T(8,128)(2,1)S(1)} %collective-permute-done.wq1), channel_id=1, source_target_pairs={{0,2},{2,0},{1,3},{3,1},{4,6},{6,4},{5,7},{7,5},{8,10},{10,8},{9,1... | collective-permute-start | bytes 663560 | tf_op jit(solution)/shard_map/ppermute | solution.py:545
  19.7 3.0 %collective-permute-done.2.x1 = bf16[96,1024]{1,0:T(8,128)(2,1)S(1)} collective-permute-done((bf16[96,1024]{1,0:T(8,128)(2,1)}, bf16[96,1024]{1,0:T(8,128)(2,1)S(1)}, u32[]{:S(2)}, u32[]{:S(2)}) %collective-permute-start.2) | collective-permute-done | bytes 196640 | tf_op jit(solution)/shard_map/ppermute | solution.py:549
  22.7 2.9 %collective-permute-done.4.x3 = bf16[96,1024]{1,0:T(8,128)(2,1)S(1)} collective-permute-done((bf16[96,1024]{1,0:T(8,128)(2,1)}, bf16[96,1024]{1,0:T(8,128)(2,1)S(1)}, u32[]{:S(2)}, u32[]{:S(2)}) %collective-permute-start.4) | collective-permute-done | bytes 196640 | tf_op jit(solution)/shard_map/ppermute | solution.py:549
  28.8 9.6 %attention_forward.1 = (bf16[384,1024]{1,0:T(8,128)(2,1)S(1)}, bf16[384,1024]{1,0:T(8,128)(2,1)S(1)}, bf16[2,576,1024]{2,1,0:T(8,128)(2,1)S(1)}, bf16[4,6,256,25...) custom-call(s32[2]{0:T(128)S(1)} %copy-done.6, ...), custom_call_target="tpu_custom_call" | custom-call | flops 16000000000 | bytes 12165120 | tf_op jit(solution)/shard_map/attention_forward/pallas_call | solution.py:522
  38.4 3.0 %collective-permute-done.16.b11 = bf16[1,768]{1,0:T(2,128)(2,1)S(1)} collective-permute-done((bf16[1,768]{1,0:T(2,128)(2,1)S(1)}, bf16[1,768]{1,0:T(2,128)(2,1)S(1)}, u32[]{:S(2)}, u32[]{:S(2)}) %collective-permute-start.16) | collective-permute-done | bytes 1568 | tf_op jit(solution)/shard_map/ppermute | solution.py:545
  42.9 1.3 collective-permute-start.21
  44.2 10.7 %mlp_forward.1 = (bf16[96,1024]{1,0:T(8,128)(2,1)S(1)}, bf16[96,1024]{1,0:T(8,128)(2,1)S(1)}, bf16[96,1024]{1,0:T(8,128)(2,1)S(1)}, bf16[96,1024]{1,0:T(8,128)(2...) custom-call(s32[2]{0:T(128)S(1)} %copy-done.6, ...), custom_call_target="tpu_custom_call" | custom-call | flops 12000000000 | bytes 14330880 | tf_op jit(solution)/shard_map/mlp_forward/pallas_call | solution.py:522
  55.9 1.3 collective-permute-start.24
  57.1 12.6 %mlp_backward.1 = (f32[384,1024]{1,0:T(8,128)S(1)}, bf16[384,1024]{1,0:T(8,128)(2,1)S(1)}, f32[4,384,4]{2,1,0:T(8,128)S(1)}, bf16[192,1728]{1,0:T(8,128)(2,1)S(1...) custom-call(s32[2]{0:T(128)S(1)} %copy-done.6, ...), custom_call_target="tpu_custom_call" | custom-call | flops 20000000000 | bytes 20923392 | tf_op jit(solution)/shard_map/mlp_backward/pallas_call | solution.py:522
  69.9 2.1 %collective-permute-done.25 = bf16[192,1728]{1,0:T(8,128)(2,1)S(1)} collective-permute-done((bf16[192,1728]{1,0:T(8,128)(2,1)S(1)}, bf16[192,1728]{1,0:T(8,128)(2,1)S(1)}, u32[]{:S(2)}, u32[]{:S(2)}) %collective-permute-start.25) | collective-permute-done | bytes 663584 | tf_op jit(solution)/shard_map/ppermute | solution.py:545
  73.3 12.8 %attention_backward.1 = (bf16[96,1024]{1,0:T(8,128)(2,1)S(1)}, bf16[96,1024]{1,0:T(8,128)(2,1)S(1)}, bf16[96,1024]{1,0:T(8,128)(2,1)S(1)}, bf16[96,1024]{1,0:T(8...) custom-call(s32[2]{0:T(128)S(1)} %copy-done.6, ...), custom_call_target="tpu_custom_call" | custom-call | flops 16000000000 | bytes 14558208 | tf_op jit(solution)/shard_map/attention_backward/pallas_call | solution.py:522
  86.1 4.0 %collective-permute-done.27 = bf16[192,1728]{1,0:T(8,128)(2,1)S(1)} collective-permute-done((bf16[192,1728]{1,0:T(8,128)(2,1)S(1)}, bf16[192,1728]{1,0:T(8,128)(2,1)S(1)}, u32[]{:S(2)}, u32[]{:S(2)}) %collective-permute-start.27) | collective-permute-done | bytes 663584 | tf_op jit(solution)/shard_map/ppermute | solution.py:545
  91.2 6.0 %all-to-all-start = ((bf16[8,24,1728]{2,1,0:T(8,128)(2,1)}), bf16[8,24,1728]{2,1,0:T(8,128)(2,1)}, u32[]{:S(2)}, u32[]{:S(2)}) async-start(bf16[8,24,1728]{2,1,0:T(8,128)(2,1)} %bitcast.33), calls=%async_computation | async-start | bytes 1376256 | tf_op jit(solution)/shard_map/all_to_all | solution.py:575
  104.5 2.6 %collective-permute-done.34.x1 = bf16[96,1024]{1,0:T(8,128)(2,1)S(1)} collective-permute-done((bf16[96,1024]{1,0:T(8,128)(2,1)S(1)}, bf16[96,1024]{1,0:T(8,128)(2,1)S(1)}, u32[]{:S(2)}, u32[]{:S(2)}) %collective-permute-start.34) | collective-permute-done | bytes 196640 | tf_op jit(solution)/shard_map/ppermute | solution.py:549
  107.1 3.1 %collective-permute-done.36.x3 = bf16[96,1024]{1,0:T(8,128)(2,1)S(1)} collective-permute-done((bf16[96,1024]{1,0:T(8,128)(2,1)S(1)}, bf16[96,1024]{1,0:T(8,128)(2,1)S(1)}, u32[]{:S(2)}, u32[]{:S(2)}) %collective-permute-start.36) | collective-permute-done | bytes 196640 | tf_op jit(solution)/shard_map/ppermute | solution.py:549
  110.2 2.9 %collective-permute-start.37 = (bf16[1,128,192]{2,1,0:T(8,128)(2,1)S(1)}, bf16[1,128,192]{2,1,0:T(8,128)(2,1)S(1)}, u32[]{:S(2)}, u32[]{:S(2)}) collective-permute-start(bf16[1,128,192]{2,1,0:T(8,128)(2,1)S(1)} %bitcast.31), channel_id=1, source_target_pairs={{0,16},{4,20},{8,24},{12,28},{16,0},{20,4},{24,8},{28,12},{1,17},{... | collective-permute-start | bytes 147464 | tf_op jit(solution)/shard_map/ppermute | solution.py:569
  118.1 2.9 %collective-permute-start.39 = (bf16[24,1728]{1,0:T(8,128)(2,1)S(1)}, bf16[24,1728]{1,0:T(8,128)(2,1)S(1)}, u32[]{:S(2)}, u32[]{:S(2)}) collective-permute-start(bf16[24,1728]{1,0:T(8,128)(2,1)S(1)} %reduce_sum.24), channel_id=1, source_target_pairs={{0,16},{4,20},{8,24},{12,28},{16,0},{20,4},{24,8},{28,12},{1,17},{... | collective-permute-start | bytes 248840 | tf_op jit(solution)/shard_map/ppermute | solution.py:569
  121.0 5.1 %all-to-all-start.1 = ((bf16[8,24,576]{2,1,0:T(8,128)(2,1)}), bf16[8,24,576]{2,1,0:T(8,128)(2,1)S(1)}, u32[]{:S(2)}, u32[]{:S(2)}) async-start(bf16[8,24,576]{2,1,0:T(8,128)(2,1)} %bitcast.6), calls=%async_computation.1 | async-start | bytes 491520 | tf_op jit(solution)/shard_map/all_to_all | solution.py:575
  126.0 2.0 %collective-permute-start.41 = (bf16[2,128,192]{2,1,0:T(8,128)(2,1)S(1)}, bf16[2,128,192]{2,1,0:T(8,128)(2,1)S(1)}, u32[]{:S(2)}, u32[]{:S(2)}) collective-permute-start(bf16[2,128,192]{2,1,0:T(8,128)(2,1)S(1)} %pad_maximum_fusion.5), channel_id=1, source_target_pairs={{0,8},{4,12},{8,0},{12,4},{16,24},{20,28},{24,16},{28,20},{1,9},{5... | collective-permute-start | bytes 294920 | tf_op jit(solution)/shard_map/ppermute | solution.py:569
  128.2 2.3 %join_tokens.1 = f32[96,4096]{1,0:T(8,128)} custom-call(s32[2]{0:T(128)S(1)} %copy-done.6, bf16[96,1024]{1,0:T(8,128)(2,1)S(1)} %get-tuple-element.272.x0, bf16[96,1024]{1,0:T(8,128)(2,1)S(1)} %collective-permute-done.34.x1, bf16[96,1024]{1,0:T(8,128)(2,1)S(1)} %collective-permute-done.35.x2, bf16[96,1024]{1,0:T(8,128)(2,1)S(1)} %collective-permute-done.36.x3), custom_call_target="tpu_custom_call" | custom-call | flops 2000000000 | bytes 2359296 | tf_op jit(solution)/shard_map/join_tokens/pallas_call | solution.py:522
  130.5 6.1 %collective-permute-done.41 = bf16[2,128,192]{2,1,0:T(8,128)(2,1)S(1)} collective-permute-done((bf16[2,128,192]{2,1,0:T(8,128)(2,1)S(1)}, bf16[2,128,192]{2,1,0:T(8,128)(2,1)S(1)}, u32[]{:S(2)}, u32[]{:S(2)}) %collective-permute-start.41) | collective-permute-done | bytes 98336 | tf_op jit(solution)/shard_map/ppermute | solution.py:569
  136.7 2.2 %collective-permute-done.40 = bf16[2,24,1728]{2,1,0:T(8,128)(2,1)S(1)} collective-permute-done((bf16[2,24,1728]{2,1,0:T(8,128)(2,1)S(1)}, bf16[2,24,1728]{2,1,0:T(8,128)(2,1)S(1)}, u32[]{:S(2)}, u32[]{:S(2)}) %collective-permute-start.40) | collective-permute-done | bytes 165920 | tf_op jit(solution)/shard_map/ppermute | solution.py:569
  138.9 1.5 collective-permute-start.42
  142.4 4.5 %all-to-all-start.2 = ((bf16[8,24,576]{2,1,0:T(8,128)(2,1)}), bf16[8,24,576]{2,1,0:T(8,128)(2,1)S(1)}, u32[]{:S(2)}, u32[]{:S(2)}) async-start(bf16[8,24,576]{2,1,0:T(8,128)(2,1)} %broadcast_in_dim.10), calls=%async_computation.2 | async-start | bytes 491520 | tf_op jit(solution)/shard_map/all_to_all | solution.py:751
  146.9 1.3 collective-permute-done.42
  148.3 2.6 %modulation_grads.1 = (f32[192,1152]{1,0:T(8,128)}, f32[6,96]{1,0:T(8,128)}, f32[4,192]{1,0:T(4,128)S(1)}, f32[2,192]{1,0:T(2,128)}, f32[1,96]{1,0:T(1,128)}, /*index=5*/f32[1,96]{1,0:T(1,128)}) custom-call(s32[2]{0:T(128)S(1)} %copy-done.6, bf16[8,128,192]{2,1,0:T(8,128)(2,1)S(1)} %pad_maximum_fusion.1.refs_0_), custom_call_target="tpu_custom_call" | custom-call | flops 2000000000 | bytes 1285632 | tf_op jit(solution)/shard_map/modulation_grads/pallas_call | solution.py:522
  151.6 4.0 %collective-permute-done.43 = bf16[2,2,24,1728]{3,2,1,0:T(8,128)(2,1)S(1)} collective-permute-done((bf16[2,2,24,1728]{3,2,1,0:T(8,128)(2,1)S(1)}, bf16[2,2,24,1728]{3,2,1,0:T(8,128)(2,1)S(1)}, u32[]{:S(2)}, u32[]{:S(2)}) %collective-permute-start.43) | collective-permute-done | bytes 331808 | tf_op jit(solution)/shard_map/ppermute | solution.py:569
  (120 shorter events, 29.3 us)
Async XLA Ops:
  0.6 11.3 %collective-permute-start = (bf16[192,576]{1,0:T(8,128)(2,1)}, bf16[192,576]{1,0:T(8,128)(2,1)S(1)}, u32[]{:S(2)}, u32[]{:S(2)}) collective-permute-start(bf16[192,576]{1,0:T(8,128)(2,1)} %wq0.1), channel_id=1, source_target_pairs={{0,1},{1,0},{2,3},{3,2},{4,5},{5,4},{6,7},{7,6},{8,9},{9,8},{10,11... | collective-permute-start | bytes 663560 | tf_op jit(solution)/shard_map/ppermute | solution.py:545
  3.6 12.3 %collective-permute-start.5 = (bf16[192,576]{1,0:T(8,128)(2,1)}, bf16[192,576]{1,0:T(8,128)(2,1)S(1)}, u32[]{:S(2)}, u32[]{:S(2)}) collective-permute-start(bf16[192,576]{1,0:T(8,128)(2,1)} %wq0.1), channel_id=1, source_target_pairs={{0,2},{2,0},{1,3},{3,1},{4,6},{6,4},{5,7},{7,5},{8,10},{10,8},{9,1... | collective-permute-start | bytes 663560 | tf_op jit(solution)/shard_map/ppermute | solution.py:545
  3.6 8.3 %collective-permute-start.1 = (bf16[192,192]{1,0:T(8,128)(2,1)}, bf16[192,192]{1,0:T(8,128)(2,1)S(1)}, u32[]{:S(2)}, u32[]{:S(2)}) collective-permute-start(bf16[192,192]{1,0:T(8,128)(2,1)} %wp0.1), channel_id=1, source_target_pairs={{0,1},{1,0},{2,3},{3,2},{4,5},{5,4},{6,7},{7,6},{8,9},{9,8},{10,11... | collective-permute-start | bytes 221192 | tf_op jit(solution)/shard_map/ppermute | solution.py:545
  3.8 10.4 %collective-permute-start.7 = (bf16[192,192]{1,0:T(8,128)(2,1)}, bf16[192,192]{1,0:T(8,128)(2,1)S(1)}, u32[]{:S(2)}, u32[]{:S(2)}) collective-permute-start(bf16[192,192]{1,0:T(8,128)(2,1)} %wp0.1), channel_id=1, source_target_pairs={{0,2},{2,0},{1,3},{3,1},{4,6},{6,4},{5,7},{7,5},{8,10},{10,8},{9,1... | collective-permute-start | bytes 221192 | tf_op jit(solution)/shard_map/ppermute | solution.py:545
  14.2 8.5 %collective-permute-start.2 = (bf16[96,1024]{1,0:T(8,128)(2,1)}, bf16[96,1024]{1,0:T(8,128)(2,1)S(1)}, u32[]{:S(2)}, u32[]{:S(2)}) collective-permute-start(bf16[96,1024]{1,0:T(8,128)(2,1)} %get-tuple-element.157), channel_id=1, source_target_pairs={{0,1},{1,0},{2,3},{3,2},{4,5},{5,4},{6,7},{7,6},{8,9},{9,8},{10,11... | collective-permute-start | bytes 589832 | tf_op jit(solution)/shard_map/ppermute | solution.py:549
  16.3 9.4 %collective-permute-start.4 = (bf16[96,1024]{1,0:T(8,128)(2,1)}, bf16[96,1024]{1,0:T(8,128)(2,1)S(1)}, u32[]{:S(2)}, u32[]{:S(2)}) collective-permute-start(bf16[96,1024]{1,0:T(8,128)(2,1)} %get-tuple-element.159), channel_id=1, source_target_pairs={{0,3},{1,2},{2,1},{3,0},{4,7},{5,6},{6,5},{7,4},{8,11},{9,10},{10,... | collective-permute-start | bytes 589832 | tf_op jit(solution)/shard_map/ppermute | solution.py:549
  16.3 9.3 %collective-permute-start.6 = (bf16[192,576]{1,0:T(8,128)(2,1)S(1)}, bf16[192,576]{1,0:T(8,128)(2,1)S(1)}, u32[]{:S(2)}, u32[]{:S(2)}) collective-permute-start(bf16[192,576]{1,0:T(8,128)(2,1)S(1)} %collective-permute-done.wq1), channel_id=1, source_target_pairs={{0,2},{2,0},{1,3},{3,1},{4,6},{6,4},{5,7},{7,5},{8,10},{10,8},{9,1... | collective-permute-start | bytes 663560 | tf_op jit(solution)/shard_map/ppermute | solution.py:545
  25.7 15.8 %collective-permute-start.12 = (bf16[192,768]{1,0:T(8,128)(2,1)S(1)}, bf16[192,768]{1,0:T(8,128)(2,1)S(1)}, u32[]{:S(2)}, u32[]{:S(2)}) collective-permute-start(bf16[192,768]{1,0:T(8,128)(2,1)S(1)} %copy-done.2), channel_id=1, source_target_pairs={{0,1},{1,0},{2,3},{3,2},{4,5},{5,4},{6,7},{7,6},{8,9},{9,8},{10,11... | collective-permute-start | bytes 884744 | tf_op jit(solution)/shard_map/ppermute | solution.py:545
  26.2 15.2 %collective-permute-start.14 = (bf16[192,768]{1,0:T(8,128)(2,1)S(1)}, bf16[192,768]{1,0:T(8,128)(2,1)S(1)}, u32[]{:S(2)}, u32[]{:S(2)}) collective-permute-start(bf16[192,768]{1,0:T(8,128)(2,1)S(1)} %copy-done.2), channel_id=1, source_target_pairs={{0,2},{2,0},{1,3},{3,1},{4,6},{6,4},{5,7},{7,5},{8,10},{10,8},{9,1... | collective-permute-start | bytes 884744 | tf_op jit(solution)/shard_map/ppermute | solution.py:545
  26.7 14.7 %collective-permute-start.13 = (bf16[192,768]{1,0:T(8,128)(2,1)S(1)}, bf16[192,768]{1,0:T(8,128)(2,1)S(1)}, u32[]{:S(2)}, u32[]{:S(2)}) collective-permute-start(bf16[192,768]{1,0:T(8,128)(2,1)S(1)} %copy-done.3), channel_id=1, source_target_pairs={{0,1},{1,0},{2,3},{3,2},{4,5},{5,4},{6,7},{7,6},{8,9},{9,8},{10,11... | collective-permute-start | bytes 884744 | tf_op jit(solution)/shard_map/ppermute | solution.py:545
  27.9 13.6 %collective-permute-start.15 = (bf16[192,768]{1,0:T(8,128)(2,1)S(1)}, bf16[192,768]{1,0:T(8,128)(2,1)S(1)}, u32[]{:S(2)}, u32[]{:S(2)}) collective-permute-start(bf16[192,768]{1,0:T(8,128)(2,1)S(1)} %copy-done.3), channel_id=1, source_target_pairs={{0,2},{2,0},{1,3},{3,1},{4,6},{6,4},{5,7},{7,5},{8,10},{10,8},{9,1... | collective-permute-start | bytes 884744 | tf_op jit(solution)/shard_map/ppermute | solution.py:545
  27.9 13.5 %collective-permute-start.16 = (bf16[1,768]{1,0:T(2,128)(2,1)S(1)}, bf16[1,768]{1,0:T(2,128)(2,1)S(1)}, u32[]{:S(2)}, u32[]{:S(2)}) collective-permute-start(bf16[1,768]{1,0:T(2,128)(2,1)S(1)} %reshape.59.b10), channel_id=1, source_target_pairs={{0,1},{1,0},{2,3},{3,2},{4,5},{5,4},{6,7},{7,6},{8,9},{9,8},{10,11... | collective-permute-start | bytes 4616 | tf_op jit(solution)/shard_map/ppermute | solution.py:545
  42.0 12.9 %collective-permute-start.19 = (bf16[96,1024]{1,0:T(8,128)(2,1)S(1)}, bf16[96,1024]{1,0:T(8,128)(2,1)S(1)}, u32[]{:S(2)}, u32[]{:S(2)}) collective-permute-start(bf16[96,1024]{1,0:T(8,128)(2,1)S(1)} %get-tuple-element.209), channel_id=1, source_target_pairs={{0,1},{1,0},{2,3},{3,2},{4,5},{5,4},{6,7},{7,6},{8,9},{9,8},{10,11... | collective-permute-start | bytes 589832 | tf_op jit(solution)/shard_map/ppermute | solution.py:549
  42.9 12.0 %collective-permute-start.20 = (bf16[96,1024]{1,0:T(8,128)(2,1)S(1)}, bf16[96,1024]{1,0:T(8,128)(2,1)S(1)}, u32[]{:S(2)}, u32[]{:S(2)}) collective-permute-start(bf16[96,1024]{1,0:T(8,128)(2,1)S(1)} %get-tuple-element.210), channel_id=1, source_target_pairs={{0,2},{1,3},{2,0},{3,1},{4,6},{5,7},{6,4},{7,5},{8,10},{9,11},{10,... | collective-permute-start | bytes 589832 | tf_op jit(solution)/shard_map/ppermute | solution.py:549
  42.9 12.0 %collective-permute-start.21 = (bf16[96,1024]{1,0:T(8,128)(2,1)S(1)}, bf16[96,1024]{1,0:T(8,128)(2,1)S(1)}, u32[]{:S(2)}, u32[]{:S(2)}) collective-permute-start(bf16[96,1024]{1,0:T(8,128)(2,1)S(1)} %get-tuple-element.211), channel_id=1, source_target_pairs={{0,3},{1,2},{2,1},{3,0},{4,7},{5,6},{6,5},{7,4},{8,11},{9,10},{10,... | collective-permute-start | bytes 589832 | tf_op jit(solution)/shard_map/ppermute | solution.py:549
  54.9 14.9 %collective-permute-start.22 = (bf16[96,1024]{1,0:T(8,128)(2,1)S(1)}, bf16[96,1024]{1,0:T(8,128)(2,1)S(1)}, u32[]{:S(2)}, u32[]{:S(2)}) collective-permute-start(bf16[96,1024]{1,0:T(8,128)(2,1)S(1)} %get-tuple-element.223), channel_id=1, source_target_pairs={{0,1},{1,0},{2,3},{3,2},{4,5},{5,4},{6,7},{7,6},{8,9},{9,8},{10,11... | collective-permute-start | bytes 589832 | tf_op jit(solution)/shard_map/ppermute | solution.py:549
  55.9 13.9 %collective-permute-start.23 = (bf16[96,1024]{1,0:T(8,128)(2,1)S(1)}, bf16[96,1024]{1,0:T(8,128)(2,1)S(1)}, u32[]{:S(2)}, u32[]{:S(2)}) collective-permute-start(bf16[96,1024]{1,0:T(8,128)(2,1)S(1)} %get-tuple-element.224), channel_id=1, source_target_pairs={{0,2},{1,3},{2,0},{3,1},{4,6},{5,7},{6,4},{7,5},{8,10},{9,11},{10,... | collective-permute-start | bytes 589832 | tf_op jit(solution)/shard_map/ppermute | solution.py:549
  55.9 13.9 %collective-permute-start.24 = (bf16[96,1024]{1,0:T(8,128)(2,1)S(1)}, bf16[96,1024]{1,0:T(8,128)(2,1)S(1)}, u32[]{:S(2)}, u32[]{:S(2)}) collective-permute-start(bf16[96,1024]{1,0:T(8,128)(2,1)S(1)} %get-tuple-element.225), channel_id=1, source_target_pairs={{0,3},{1,2},{2,1},{3,0},{4,7},{5,6},{6,5},{7,4},{8,11},{9,10},{10,... | collective-permute-start | bytes 589832 | tf_op jit(solution)/shard_map/ppermute | solution.py:549
  72.2 13.9 %collective-permute-start.26 = (bf16[192,1728]{1,0:T(8,128)(2,1)S(1)}, bf16[192,1728]{1,0:T(8,128)(2,1)S(1)}, u32[]{:S(2)}, u32[]{:S(2)}) collective-permute-start(bf16[192,1728]{1,0:T(8,128)(2,1)S(1)} %get-tuple-element.242), channel_id=1, source_target_pairs={{0,2},{2,0},{1,3},{3,1},{4,6},{6,4},{5,7},{7,5},{8,10},{10,8},{9,1... | collective-permute-start | bytes 1990664 | tf_op jit(solution)/shard_map/ppermute | solution.py:545
  72.4 17.7 %collective-permute-start.27 = (bf16[192,1728]{1,0:T(8,128)(2,1)S(1)}, bf16[192,1728]{1,0:T(8,128)(2,1)S(1)}, u32[]{:S(2)}, u32[]{:S(2)}) collective-permute-start(bf16[192,1728]{1,0:T(8,128)(2,1)S(1)} %add_convert_fusion.1), channel_id=1, source_target_pairs={{0,1},{1,0},{2,3},{3,2},{4,5},{5,4},{6,7},{7,6},{8,9},{9,8},{10,11... | collective-permute-start | bytes 1990664 | tf_op jit(solution)/shard_map/ppermute | solution.py:545
  91.2 25.6 %all-to-all-start = ((bf16[8,24,1728]{2,1,0:T(8,128)(2,1)}), bf16[8,24,1728]{2,1,0:T(8,128)(2,1)}, u32[]{:S(2)}, u32[]{:S(2)}) async-start(bf16[8,24,1728]{2,1,0:T(8,128)(2,1)} %bitcast.33), calls=%async_computation | async-start | bytes 1376256 | tf_op jit(solution)/shard_map/all_to_all | solution.py:575
  99.4 7.7 %collective-permute-start.34 = (bf16[96,1024]{1,0:T(8,128)(2,1)S(1)}, bf16[96,1024]{1,0:T(8,128)(2,1)S(1)}, u32[]{:S(2)}, u32[]{:S(2)}) collective-permute-start(bf16[96,1024]{1,0:T(8,128)(2,1)S(1)} %get-tuple-element.260), channel_id=1, source_target_pairs={{0,1},{1,0},{2,3},{3,2},{4,5},{5,4},{6,7},{7,6},{8,9},{9,8},{10,11... | collective-permute-start | bytes 589832 | tf_op jit(solution)/shard_map/ppermute | solution.py:549
  101.3 8.9 %collective-permute-start.36 = (bf16[96,1024]{1,0:T(8,128)(2,1)S(1)}, bf16[96,1024]{1,0:T(8,128)(2,1)S(1)}, u32[]{:S(2)}, u32[]{:S(2)}) collective-permute-start(bf16[96,1024]{1,0:T(8,128)(2,1)S(1)} %get-tuple-element.262), channel_id=1, source_target_pairs={{0,3},{1,2},{2,1},{3,0},{4,7},{5,6},{6,5},{7,4},{8,11},{9,10},{10,... | collective-permute-start | bytes 589832 | tf_op jit(solution)/shard_map/ppermute | solution.py:549
  102.4 13.5 %collective-permute-start.28 = (bf16[192,576]{1,0:T(8,128)(2,1)S(1)}, bf16[192,576]{1,0:T(8,128)(2,1)S(1)}, u32[]{:S(2)}, u32[]{:S(2)}) collective-permute-start(bf16[192,576]{1,0:T(8,128)(2,1)S(1)} %get-tuple-element.249), channel_id=1, source_target_pairs={{0,2},{2,0},{1,3},{3,1},{4,6},{6,4},{5,7},{7,5},{8,10},{10,8},{9,1... | collective-permute-start | bytes 663560 | tf_op jit(solution)/shard_map/ppermute | solution.py:545
  102.5 13.5 %collective-permute-start.30 = (bf16[192,576]{1,0:T(8,128)(2,1)S(1)}, bf16[192,576]{1,0:T(8,128)(2,1)S(1)}, u32[]{:S(2)}, u32[]{:S(2)}) collective-permute-start(bf16[192,576]{1,0:T(8,128)(2,1)S(1)} %add_convert_fusion.3), channel_id=1, source_target_pairs={{0,1},{1,0},{2,3},{3,2},{4,5},{5,4},{6,7},{7,6},{8,9},{9,8},{10,11... | collective-permute-start | bytes 663560 | tf_op jit(solution)/shard_map/ppermute | solution.py:545
  118.1 10.0 %collective-permute-start.39 = (bf16[24,1728]{1,0:T(8,128)(2,1)S(1)}, bf16[24,1728]{1,0:T(8,128)(2,1)S(1)}, u32[]{:S(2)}, u32[]{:S(2)}) collective-permute-start(bf16[24,1728]{1,0:T(8,128)(2,1)S(1)} %reduce_sum.24), channel_id=1, source_target_pairs={{0,16},{4,20},{8,24},{12,28},{16,0},{20,4},{24,8},{28,12},{1,17},{... | collective-permute-start | bytes 248840 | tf_op jit(solution)/shard_map/ppermute | solution.py:569
  121.0 17.9 %all-to-all-start.1 = ((bf16[8,24,576]{2,1,0:T(8,128)(2,1)}), bf16[8,24,576]{2,1,0:T(8,128)(2,1)S(1)}, u32[]{:S(2)}, u32[]{:S(2)}) async-start(bf16[8,24,576]{2,1,0:T(8,128)(2,1)} %bitcast.6), calls=%async_computation.1 | async-start | bytes 491520 | tf_op jit(solution)/shard_map/all_to_all | solution.py:575
  126.0 10.6 %collective-permute-start.41 = (bf16[2,128,192]{2,1,0:T(8,128)(2,1)S(1)}, bf16[2,128,192]{2,1,0:T(8,128)(2,1)S(1)}, u32[]{:S(2)}, u32[]{:S(2)}) collective-permute-start(bf16[2,128,192]{2,1,0:T(8,128)(2,1)S(1)} %pad_maximum_fusion.5), channel_id=1, source_target_pairs={{0,8},{4,12},{8,0},{12,4},{16,24},{20,28},{24,16},{28,20},{1,9},{5... | collective-permute-start | bytes 294920 | tf_op jit(solution)/shard_map/ppermute | solution.py:569
  128.1 10.7 %collective-permute-start.40 = (bf16[2,24,1728]{2,1,0:T(8,128)(2,1)S(1)}, bf16[2,24,1728]{2,1,0:T(8,128)(2,1)S(1)}, u32[]{:S(2)}, u32[]{:S(2)}) collective-permute-start(bf16[2,24,1728]{2,1,0:T(8,128)(2,1)S(1)} %pad_maximum_fusion.4), channel_id=1, source_target_pairs={{0,8},{4,12},{8,0},{12,4},{16,24},{20,28},{24,16},{28,20},{1,9},{5... | collective-permute-start | bytes 497672 | tf_op jit(solution)/shard_map/ppermute | solution.py:569
  138.9 9.3 %collective-permute-start.42 = (bf16[4,128,192]{2,1,0:T(8,128)(2,1)S(1)}, bf16[4,128,192]{2,1,0:T(8,128)(2,1)S(1)}, u32[]{:S(2)}, u32[]{:S(2)}) collective-permute-start(bf16[4,128,192]{2,1,0:T(8,128)(2,1)S(1)} %pad_maximum_fusion.3), channel_id=1, source_target_pairs={{0,4},{4,0},{8,12},{12,8},{16,20},{20,16},{24,28},{28,24},{1,5},{5... | collective-permute-start | bytes 589832 | tf_op jit(solution)/shard_map/ppermute | solution.py:569
  140.5 15.1 %collective-permute-start.43 = (bf16[2,2,24,1728]{3,2,1,0:T(8,128)(2,1)S(1)}, bf16[2,2,24,1728]{3,2,1,0:T(8,128)(2,1)S(1)}, u32[]{:S(2)}, u32[]{:S(2)}) collective-permute-start(bf16[2,2,24,1728]{3,2,1,0:T(8,128)(2,1)S(1)} %pad_maximum_fusion.2), channel_id=1, source_target_pairs={{0,4},{4,0},{8,12},{12,8},{16,20},{20,16},{24,28},{28,24},{1,5},{5... | collective-permute-start | bytes 995336 | tf_op jit(solution)/shard_map/ppermute | solution.py:569
  142.4 15.2 %all-to-all-start.2 = ((bf16[8,24,576]{2,1,0:T(8,128)(2,1)}), bf16[8,24,576]{2,1,0:T(8,128)(2,1)S(1)}, u32[]{:S(2)}, u32[]{:S(2)}) async-start(bf16[8,24,576]{2,1,0:T(8,128)(2,1)} %broadcast_in_dim.10), calls=%async_computation.2 | async-start | bytes 491520 | tf_op jit(solution)/shard_map/all_to_all | solution.py:751
  (27 other events, 222.7 us)

commit v4 on v3

--- a/solution.py
+++ b/solution.py
@@ -14,7 +14,8 @@
 BF16 = jnp.bfloat16
 F32 = jnp.float32
 GROUP = ("row", "col")
-LIMITS = {"modulation_parts": 60, "attention_forward": 15, "mlp_forward": 16, "mlp_backward": 27, "attention_backward": 20}
+LIMITS = {"modulation_parts": 60, "attention_forward": 18, "mlp_forward": 22, "mlp_backward": 30, "attention_backward": 24}
+TOGETHER = {"attention_forward": 2, "mlp_forward": 2, "mlp_backward": 2, "attention_backward": 2}
 
 
 def dot_nn(left, right):
@@ -36,6 +37,19 @@
 def lane_fold(value):
     parts = [value[:, at : at + 128] for at in range(0, value.shape[1], 128)]
     return sum(parts[1:], parts[0])
+
+
+def latent_columns(mod, width):
+    seq = width // mod.shape[0]
+    return [slice(at * seq, (at + 1) * seq) for at in range(mod.shape[0])]
+
+
+def spread(mod, vector, width):
+    shape = (mod.shape[1], width // mod.shape[0])
+    parts = [
+        jnp.broadcast_to(mod[at, :, vector : vector + 1], shape) for at in range(mod.shape[0])
+    ]
+    return parts[0] if len(parts) == 1 else jnp.concatenate(parts, axis=1)
 
 
 def norm_stats(value):
@@ -147,11 +161,15 @@
 
 
 def join_tokens(pos, x0, x1, x2, x3, out):
+    own = pos[0] * 2 + pos[1]
+    width = x0.shape[1]
+    here = out.shape[1] // width
     for step, piece in enumerate((x0, x1, x2, x3)):
 
-        @pl.when(pl.program_id(0) == step)
+        @pl.when(pl.program_id(0) == step // here)
         def _():
-            out[...] = piece[...].astype(out.dtype)
+            at = pl.multiple_of(((own ^ step) & (here - 1)) * width, width)
+            out[:, pl.ds(at, width)] = piece[...].astype(out.dtype)
 
 
 def group_vectors(pos, pack0, pack1, pack2, pack3, cond, w_ada, everyone, cond_part):
@@ -241,14 +259,18 @@
 
     third = D // GROUPS
     for first, second, who in ((pack0, pack1, pos[0]), (pack2, pack3, 1 - pos[0])):
-        rows = pl.ds(pl.multiple_of(pl.program_id(0) * 8, 8), 8)
         at = pl.multiple_of(who * third, third)
-        mod[0, pl.ds(at, third), :] = (first[rows, :] + second[rows, :]).T
+        for latent in range(mod.shape[0]):
+            rows = pl.multiple_of((pl.program_id(0) * mod.shape[0] + latent) * 8, 8)
+            rows = pl.ds(rows, 8)
+            mod[latent, pl.ds(at, third), :] = (first[rows, :] + second[rows, :]).T
     place_features((x0, x1, x2, x3), x_s, pos)
     x = x_s[...]
     x_out[...] = x.astype(BF16)
     normed, _ = norm_stats(x)
-    mod_one = (normed * (1.0 + mod[0, :, 1:2]) + mod[0, :, 0:1]).astype(BF16)
+    width = x.shape[1]
+    columns = latent_columns(mod, width)
+    mod_one = (normed * (1.0 + spread(mod, 1, width)) + spread(mod, 0, width)).astype(BF16)
     mod_one_out[...] = mod_one
     per_group = HEADS // GROUPS
     heads = []
@@ -264,16 +286,18 @@
         scaled = query * jnp.asarray(HD ** (-0.5), BF16)
         for head in range(per_group):
             rows = slice(head * HD, (head + 1) * HD)
-            heads.append((keys[rows], scaled[rows], values[rows]))
-    scores = [dot_nn(keys.T, query) for keys, query, _ in heads]
+            for latent, tokens in enumerate(columns):
+                place = (latent, part * per_group + head, tokens)
+                heads.append((place, keys[rows, tokens], scaled[rows, tokens], values[rows, tokens]))
+    scores = [dot_nn(keys.T, query) for _, keys, query, _ in heads]
     probs = []
     for score in scores:
         raised = jnp.exp(score - jnp.max(score, axis=0, keepdims=True))
         total = jnp.sum(raised, axis=0, keepdims=True)
         probs.append((raised * (1.0 / total)).astype(BF16))
-    for head, prob in enumerate(probs):
-        probs_out[0, head] = prob
-        attended_out[head * HD : (head + 1) * HD] = dot_nn(heads[head][2], prob).astype(BF16)
+    for ((latent, head, tokens), _, _, values), prob in zip(heads, probs):
+        probs_out[latent, head] = prob
+        attended_out[head * HD : (head + 1) * HD, tokens] = dot_nn(values, prob).astype(BF16)
     attended = attended_out[...]
     for part in range(2):
         rows = slice(part * third, (part + 1) * third)
@@ -299,9 +323,10 @@
         for part in range(GROUPS):
             w1_t[part] = w1_s[part].T
 
-    hidden = x[...].astype(F32) + mod[0, :, 2:3] * branch[...]
+    width = x.shape[1]
+    hidden = x[...].astype(F32) + spread(mod, 2, width) * branch[...]
     normed, _ = norm_stats(hidden)
-    mod_two = (normed * (1.0 + mod[0, :, 4:5]) + mod[0, :, 3:4]).astype(BF16)
+    mod_two = (normed * (1.0 + spread(mod, 4, width)) + spread(mod, 3, width)).astype(BF16)
     mod_two_out[...] = mod_two
     half = FF // GROUPS
     slope = (2.0 / jnp.pi) ** 0.5
@@ -319,8 +344,8 @@
         ).astype(BF16)
     total = dot_nn(w2_s[0], acts[0]) + dot_nn(w2_s[1], acts[1])
     mlp = total + bias_2[...]
-    mlp_out[...] = mlp
-    block_s[...] = hidden + mod[0, :, 5:6] * mlp
+    mlp_out[...] = mlp.astype(BF16)
+    block_s[...] = hidden + spread(mod, 5, width) * mlp
     split_features(block_s, (out0, out1, out2, out3), pos)
 
 
@@ -344,11 +369,18 @@
 
     place_features((g0, g1, g2, g3), g_s, pos)
     grad = g_s[...]
-    gate_one = mod[0, :, 2:3]
-    gate_two = mod[0, :, 5:6]
+    width = x.shape[1]
+    columns = latent_columns(mod, width)
+    gate_one = spread(mod, 2, width)
+    gate_two = spread(mod, 5, width)
+
+    def latent_sums(vector, value):
+        for latent, tokens in enumerate(columns):
+            mod_grad_out[latent, :, vector : vector + 1] = lane_sum(value[:, tokens])
+
     hidden = x[...].astype(F32) + gate_one * branch[...]
     normed, inverse = norm_stats(hidden)
-    mod_grad_out[0, :, 3:4] = lane_sum(grad * mlp[...])
+    latent_sums(3, grad * mlp[...])
     mlp_grad = (gate_two * grad).astype(BF16)
     sum2[...] += lane_fold(mlp_grad.astype(F32))
     half = FF // GROUPS
@@ -364,11 +396,11 @@
     for part, rows in enumerate(parts):
         acc2[part] += dot_nt(mlp_grad, act[rows])
         acc1[part] += dot_nt(mod_two_low, pre_grads[part])
-    mod_grad_out[0, :, 1:2] = lane_sum(back)
-    mod_grad_out[0, :, 2:3] = lane_sum(back * normed)
-    hidden_grad = grad + norm_back(back * (1.0 + mod[0, :, 4:5]), normed, inverse)
-    hidden_grad_out[...] = hidden_grad
-    mod_grad_out[0, :, 0:1] = lane_sum(hidden_grad * branch[...])
+    latent_sums(1, back)
+    latent_sums(2, back * normed)
+    hidden_grad = grad + norm_back(back * (1.0 + spread(mod, 4, width)), normed, inverse)
+    hidden_grad_out[...] = hidden_grad.astype(BF16)
+    latent_sums(0, hidden_grad * branch[...])
     branch_grad = (gate_one * hidden_grad).astype(BF16)
     sump[...] += lane_fold(branch_grad.astype(F32))
     context = None
@@ -414,34 +446,37 @@
     mod_one_low = mod_one[...]
     per_group = HEADS // GROUPS
     heads = []
+    width = x.shape[1]
+    columns = latent_columns(mod, width)
     for head in range(HEADS):
         part, at = head // per_group, head % per_group * HD
-        heads.append(
-            (
-                qkv[part, at : at + HD],
-                qkv[part, third + at : third + at + HD],
-                qkv[part, 2 * third + at : 2 * third + at + HD],
-                context[head * HD : (head + 1) * HD],
-                probs[0, head],
+        for latent, tokens in enumerate(columns):
+            heads.append(
+                (
+                    (part, at, tokens),
+                    qkv[part, at : at + HD, tokens],
+                    qkv[part, third + at : third + at + HD, tokens],
+                    qkv[part, 2 * third + at : 2 * third + at + HD, tokens],
+                    context[head * HD : (head + 1) * HD, tokens],
+                    probs[latent, head],
+                )
             )
-        )
-    prob_grads = [dot_nn(values.T, grad) for _, _, values, grad, _ in heads]
+    prob_grads = [dot_nn(values.T, grad) for _, _, _, values, grad, _ in heads]
     score_grads = []
-    for prob_grad, (_, _, _, _, weight) in zip(prob_grads, heads):
+    for prob_grad, (_, _, _, _, _, weight) in zip(prob_grads, heads):
         wide = weight.astype(F32)
         product = wide * prob_grad
         row_dot = jnp.sum(product, axis=0, keepdims=True)
         score_grads.append((product - wide * row_dot).astype(BF16))
-    for head, (query, keys, _, grad, weight) in enumerate(heads):
-        part, at = head // per_group, head % per_group * HD
+    for ((part, at, tokens), query, keys, _, grad, weight), score_grad in zip(heads, score_grads):
         parts = (
-            dot_nn(keys, score_grads[head]) * scale,
-            dot_nt(query, score_grads[head]) * scale,
+            dot_nn(keys, score_grad) * scale,
+            dot_nt(query, score_grad) * scale,
             dot_nt(grad, weight),
         )
         for which, value in enumerate(parts):
             start = which * third + at
-            grad_s[part, start : start + HD] = value.astype(BF16)
+            grad_s[part, start : start + HD, tokens] = value.astype(BF16)
     back = dot_nn(wq_s[0], grad_s[0]) + dot_nn(wq_s[1], grad_s[1])
     for part in range(GROUPS):
         base = part * third
@@ -450,21 +485,25 @@
         sumv[base : base + third] += lane_fold(qkv_grad[2 * third :].astype(F32))
         acc[part] += dot_nt(mod_one_low, qkv_grad)
     normed, inverse = norm_stats(x[...].astype(F32))
-    mod_s[...] = jnp.zeros_like(mod_s)
-    mod_s[:, 0:1] = lane_sum(back)
-    mod_s[:, 1:2] = lane_sum(back * normed)
-    mod_s[:, 2:6] = mod_grad[0]
+    scaled = back * normed
     packs = (pack0, pack1, pack2, pack3)
-    rows = pl.ds(pl.multiple_of(step * 8, 8), 8)
     mine = pl.multiple_of(pos[0] * third, third)
     other = pl.multiple_of((1 - pos[0]) * third, third)
-    vectors = mod_s[pl.ds(mine, third), :].T
-    pack0[rows, :] = vectors
-    pack1[rows, :] = vectors
-    vectors = mod_s[pl.ds(other, third), :].T
-    pack2[rows, :] = vectors
-    pack3[rows, :] = vectors
-    block_s[...] = hidden_grad[...] + norm_back(back * (1.0 + mod[0, :, 1:2]), normed, inverse)
+    for latent, tokens in enumerate(columns):
+        mod_s[latent] = jnp.zeros_like(mod_s[latent])
+        mod_s[latent, :, 0:1] = lane_sum(back[:, tokens])
+        mod_s[latent, :, 1:2] = lane_sum(scaled[:, tokens])
+        mod_s[latent, :, 2:6] = mod_grad[latent]
+        rows = pl.ds(pl.multiple_of((step * mod.shape[0] + latent) * 8, 8), 8)
+        vectors = mod_s[latent, pl.ds(mine, third), :].T
+        pack0[rows, :] = vectors
+        pack1[rows, :] = vectors
+        vectors = mod_s[latent, pl.ds(other, third), :].T
+        pack2[rows, :] = vectors
+        pack3[rows, :] = vectors
+    block_s[...] = hidden_grad[...] + norm_back(
+        back * (1.0 + spread(mod, 1, width)), normed, inverse
+    )
     split_features(block_s, (out0, out1, out2, out3), pos)
     join_tokens(pos, left0, left1, left2, left3, joined)
 
@@ -495,6 +534,9 @@
 
 
 def call(kernel, pos, steps, seq, inputs, outputs, scratch, micros, name):
+    together = TOGETHER.get(name, 1)
+    steps, seq = steps // together, seq * together
+
     def spec(kind, shape):
         kind = kind[0]
         rank = len(shape)
@@ -507,11 +549,12 @@
             )
         if kind == "j":
             return pl.BlockSpec(
-                shape[:-1] + (shape[-1] // 4,), lambda i, p: (0, (p[0] * 2 + p[1]) ^ i)
+                shape[:-1] + (shape[-1] // 4 * together,),
+                lambda i, p: (0, (p[0] * 2 + p[1]) // together ^ i),
             )
         if kind == "l":
             tail = (0,) * (rank - 1)
-            return pl.BlockSpec((1,) + shape[1:], lambda i, p: (i,) + tail)
+            return pl.BlockSpec((together,) + shape[1:], lambda i, p: (i,) + tail)
         zeros = (0,) * rank
         if steps > 1:
             return pl.BlockSpec(shape, lambda i, p: zeros, pipeline_mode=pl.Buffered(1))
@@ -651,8 +694,8 @@
         [("tv", t_low), ("tv", t_low), ("tv", shape((2, 3 * third, width), BF16)),
          ("lv", shape((steps, HEADS, seq, seq), BF16)), ("tv", t_low), ("tv", t_wide),
          ("lv", shape((steps, D, 8), F32))],
-        [pltpu.VMEM((D, seq), F32), pltpu.VMEM((2, D, 3 * third), BF16),
-         pltpu.VMEM((2, 3 * third, D), BF16), pltpu.VMEM((2, D, third), BF16),
+        [pltpu.VMEM((D, seq * TOGETHER.get("attention_forward", 1)), F32),
+         pltpu.VMEM((2, D, 3 * third), BF16), pltpu.VMEM((2, 3 * third, D), BF16), pltpu.VMEM((2, D, third), BF16),
          pltpu.VMEM((2, third, D), BF16), pltpu.VMEM((D, 1), F32), pltpu.VMEM((D, 1), F32),
          pltpu.VMEM((D, 1), F32)],
         16, "attention_forward",
@@ -668,9 +711,10 @@
         mlp_forward, pos, steps, seq,
         [("t", x), ("t", branch), ("l", mod)] + [("w", a) for a in w1 + w2]
         + [("w", a) for a in (*packs, *b_fc1)],
-        [("t", t_piece)] * 4 + [("tv", t_low), ("tv", t_ff), ("tv", t_ff), ("tv", t_wide)],
+        [("t", t_piece)] * 4 + [("tv", t_low), ("tv", t_ff), ("tv", t_ff), ("tv", t_low)],
         [pltpu.VMEM((2, D, half), BF16), pltpu.VMEM((2, half, D), BF16),
-         pltpu.VMEM((2, D, half), BF16), pltpu.VMEM((D, seq), F32), pltpu.VMEM((FF, 1), F32),
+         pltpu.VMEM((2, D, half), BF16),
+         pltpu.VMEM((D, seq * TOGETHER.get("mlp_forward", 1)), F32), pltpu.VMEM((FF, 1), F32),
          pltpu.VMEM((D, 1), F32)],
         12, "mlp_forward",
     )
@@ -685,9 +729,10 @@
         + [("t", x), ("t", branch), ("l", mod), ("t", mod_two), ("t", act), ("t", slope),
            ("t", mlp), ("t", attended)]
         + [("w", a) for a in w1 + w2 + wp],
-        [("tv", t_wide), ("tv", t_low), ("lv", shape((steps, D, 4), F32))] + blocks(fc_block)
+        [("tv", t_low), ("tv", t_low), ("lv", shape((steps, D, 4), F32))] + blocks(fc_block)
         + [("w", shape((FF, 1), F32)), ("w", shape((D, 1), F32)), ("w", shape((D, 1), F32))],
-        [pltpu.VMEM((D, seq), F32), pltpu.VMEM((2, D, half), BF16), pltpu.VMEM((2, D, half), BF16),
+        [pltpu.VMEM((D, seq * TOGETHER.get("mlp_backward", 1)), F32),
+         pltpu.VMEM((2, D, half), BF16), pltpu.VMEM((2, D, half), BF16),
          pltpu.VMEM((2, half, D), BF16), pltpu.VMEM((2, D, third), BF16),
          pltpu.VMEM((2, D, half), F32), pltpu.VMEM((2, D, half), F32),
          pltpu.VMEM((2, D, third), F32), pltpu.VMEM((FF, 128), F32),
@@ -708,7 +753,9 @@
         + [("j", shape((quarter, tokens), F32))],
         [pltpu.VMEM((2, D, 3 * third), BF16), pltpu.VMEM((2, D, 3 * third), F32),
          pltpu.VMEM((D, 128), F32), pltpu.VMEM((D, 128), F32),
-         pltpu.VMEM((2, 3 * third, seq), BF16), pltpu.VMEM((D, seq), F32), pltpu.VMEM((D, 8), F32),
+         pltpu.VMEM((2, 3 * third, seq * TOGETHER.get("attention_backward", 1)), BF16),
+         pltpu.VMEM((D, seq * TOGETHER.get("attention_backward", 1)), F32),
+         pltpu.VMEM((TOGETHER.get("attention_backward", 1), D, 8), F32),
          pltpu.VMEM((third, 8), F32)],
         16, "attention_backward",
     )

time: 159 us -> 156 us (0.981)
  Pallas kernels: 57.3 us -> 49.3 us
  waiting for transfers between devices: 40.1 us -> 44 us
    pallas_call x9, Pallas kernels: 57.3 us -> 49.3 us  [call(): pl.pallas_call(kernel, grid_spec=pltpu.PrefetchScalarGridSpec(num_scalar_...]
    ppermute x20, waiting for transfers between devices: 12.7 us -> 16.7 us  [swap(): return lax.ppermute(value, axis, [(0, 1), (1, 0)])]
  transfers between devices with their start and end apart: 47 -> 47, of which waited for: 18 -> 18; matrix products, arithmetic and copies ran while one was open for 4% -> 4% of each run, Pallas kernels for 36% -> 32%
where the time goes in v4:
time: 156 us
  starting transfers between devices  50.9 us (33%)
  Pallas kernels  49.3 us (32%)
  waiting for transfers between devices  44 us (28%)
  other arithmetic  5.93 us (4%)
  local copies, waits for them, and re-layouts  4.64 us (3%)
    pallas_call x9, Pallas kernels, call(): pl.pallas_call(kernel, grid_spec=pltpu.PrefetchScalarGridSpec(num_scalar_...  49.3 us
    ppermute x20, waiting for transfers between devices, swap(): return lax.ppermute(value, axis, [(0, 1), (1, 0)])  16.7 us
    ppermute x6, waiting for transfers between devices, dp_step(): return lax.ppermute(value, 'dp', [(at, at ^ bit) for at in range(count)])  14.5 us
    ppermute x18, waiting for transfers between devices, group_step(): return lax.ppermute(value, GROUP, [(at, at ^ step) for at in range(4)])  12.8 us
    ppermute x20, starting transfers between devices, swap(): return lax.ppermute(value, axis, [(0, 1), (1, 0)])  12.7 us
    ppermute x18, starting transfers between devices, group_step(): return lax.ppermute(value, GROUP, [(at, at ^ step) for at in range(4)])  12.6 us
    all_to_all x2, starting transfers between devices, scatter_terms(): lax.all_to_all(value.reshape(count, rows // count, columns), 'dp', 0, 0)  11 us
    ppermute x6, starting transfers between devices, dp_step(): return lax.ppermute(value, 'dp', [(at, at ^ bit) for at in range(count)])  9.98 us
  transfers between devices with their start and end apart: 47, of which 18 were waited for; matrix products, arithmetic and copies ran while one was open for 4% of the time, Pallas kernels for 32%

profile of v4, /device:TPU:0, one launch (start us, length us, event | category | flops | bytes accessed | tf_op | source)
XLA Modules:
  0.0 155.9 jit_solution(1118845215728696784)
XLA Ops:
  0.6 3.0 %collective-permute-start = (bf16[192,576]{1,0:T(8,128)(2,1)}, bf16[192,576]{1,0:T(8,128)(2,1)S(1)}, u32[]{:S(2)}, u32[]{:S(2)}) collective-permute-start(bf16[192,576]{1,0:T(8,128)(2,1)} %wq0.1), channel_id=1, source_target_pairs={{0,1},{1,0},{2,3},{3,2},{4,5},{5,4},{6,7},{7,6},{8,9},{9,8},{10,11... | collective-permute-start | bytes 663560 | tf_op jit(solution)/shard_map/ppermute | solution.py:588
  4.8 5.3 %modulation_parts.1 = (bf16[96,1024]{1,0:T(8,128)(2,1)}, bf16[96,1024]{1,0:T(8,128)(2,1)}, bf16[96,1024]{1,0:T(8,128)(2,1)}, f32[40,192]{1,0:T(8,128)}, f32[40,1...) custom-call(s32[2]{0:T(128)} %pad_add_fusion.pos, ...), custom_call_target="tpu_custom_call" | custom-call | flops 6000000000 | bytes 2404608 | tf_op jit(solution)/shard_map/modulation_parts/pallas_call | solution.py:565
  10.0 1.9 %collective-permute-done.1.wp1 = bf16[192,192]{1,0:T(8,128)(2,1)S(1)} collective-permute-done((bf16[192,192]{1,0:T(8,128)(2,1)}, bf16[192,192]{1,0:T(8,128)(2,1)S(1)}, u32[]{:S(2)}, u32[]{:S(2)}) %collective-permute-start.1) | collective-permute-done | bytes 73760 | tf_op jit(solution)/shard_map/ppermute | solution.py:588
  12.0 1.8 %collective-permute-start.9 = (f32[40,192]{1,0:T(8,128)}, f32[40,192]{1,0:T(8,128)S(1)}, u32[]{:S(2)}, u32[]{:S(2)}) collective-permute-start(f32[40,192]{1,0:T(8,128)} %get-tuple-element.163), channel_id=1, source_target_pairs={{0,1},{1,0},{2,3},{3,2},{4,5},{5,4},{6,7},{7,6},{8,9},{9,8},{10,11... | collective-permute-start | bytes 92168 | tf_op jit(solution)/shard_map/ppermute | solution.py:592
  14.2 1.7 %collective-permute-start.2 = (bf16[96,1024]{1,0:T(8,128)(2,1)}, bf16[96,1024]{1,0:T(8,128)(2,1)S(1)}, u32[]{:S(2)}, u32[]{:S(2)}) collective-permute-start(bf16[96,1024]{1,0:T(8,128)(2,1)} %get-tuple-element.157), channel_id=1, source_target_pairs={{0,1},{1,0},{2,3},{3,2},{4,5},{5,4},{6,7},{7,6},{8,9},{9,8},{10,11... | collective-permute-start | bytes 589832 | tf_op jit(solution)/shard_map/ppermute | solution.py:592
  16.3 2.0 %collective-permute-start.6 = (bf16[192,576]{1,0:T(8,128)(2,1)S(1)}, bf16[192,576]{1,0:T(8,128)(2,1)S(1)}, u32[]{:S(2)}, u32[]{:S(2)}) collective-permute-start(bf16[192,576]{1,0:T(8,128)(2,1)S(1)} %collective-permute-done.wq1), channel_id=1, source_target_pairs={{0,2},{2,0},{1,3},{3,1},{4,6},{6,4},{5,7},{7,5},{8,10},{10,8},{9,1... | collective-permute-start | bytes 663560 | tf_op jit(solution)/shard_map/ppermute | solution.py:588
  19.7 3.0 %collective-permute-done.2.x1 = bf16[96,1024]{1,0:T(8,128)(2,1)S(1)} collective-permute-done((bf16[96,1024]{1,0:T(8,128)(2,1)}, bf16[96,1024]{1,0:T(8,128)(2,1)S(1)}, u32[]{:S(2)}, u32[]{:S(2)}) %collective-permute-start.2) | collective-permute-done | bytes 196640 | tf_op jit(solution)/shard_map/ppermute | solution.py:592
  22.7 2.9 %collective-permute-done.4.x3 = bf16[96,1024]{1,0:T(8,128)(2,1)S(1)} collective-permute-done((bf16[96,1024]{1,0:T(8,128)(2,1)}, bf16[96,1024]{1,0:T(8,128)(2,1)S(1)}, u32[]{:S(2)}, u32[]{:S(2)}) %collective-permute-start.4) | collective-permute-done | bytes 196640 | tf_op jit(solution)/shard_map/ppermute | solution.py:592
  28.8 7.4 %attention_forward.1 = (bf16[384,1024]{1,0:T(8,128)(2,1)S(1)}, bf16[384,1024]{1,0:T(8,128)(2,1)S(1)}, bf16[2,576,1024]{2,1,0:T(8,128)(2,1)S(1)}, bf16[4,6,256,25...) custom-call(s32[2]{0:T(128)S(1)} %copy-done.6, ...), custom_call_target="tpu_custom_call" | custom-call | flops 16000000000 | bytes 12165120 | tf_op jit(solution)/shard_map/attention_forward/pallas_call | solution.py:565
  36.2 5.2 %collective-permute-done.16.b11 = bf16[1,768]{1,0:T(2,128)(2,1)S(1)} collective-permute-done((bf16[1,768]{1,0:T(2,128)(2,1)S(1)}, bf16[1,768]{1,0:T(2,128)(2,1)S(1)}, u32[]{:S(2)}, u32[]{:S(2)}) %collective-permute-start.16) | collective-permute-done | bytes 1568 | tf_op jit(solution)/shard_map/ppermute | solution.py:588
  44.2 8.4 %mlp_forward.1 = (bf16[96,1024]{1,0:T(8,128)(2,1)S(1)}, bf16[96,1024]{1,0:T(8,128)(2,1)S(1)}, bf16[96,1024]{1,0:T(8,128)(2,1)S(1)}, bf16[96,1024]{1,0:T(8,128)(2...) custom-call(s32[2]{0:T(128)S(1)} %copy-done.6, ...), custom_call_target="tpu_custom_call" | custom-call | flops 12000000000 | bytes 13544448 | tf_op jit(solution)/shard_map/mlp_forward/pallas_call | solution.py:565
  53.6 1.3 collective-permute-start.24
  54.8 1.4 copy-done.9
  56.2 10.9 %mlp_backward.1 = (bf16[384,1024]{1,0:T(8,128)(2,1)S(1)}, bf16[384,1024]{1,0:T(8,128)(2,1)S(1)}, f32[4,384,4]{2,1,0:T(8,128)S(1)}, bf16[192,1728]{1,0:T(8,128)(2...) custom-call(s32[2]{0:T(128)S(1)} %copy-done.6, ...), custom_call_target="tpu_custom_call" | custom-call | flops 20000000000 | bytes 19350528 | tf_op jit(solution)/shard_map/mlp_backward/pallas_call | solution.py:565
  67.3 2.1 %collective-permute-done.25 = bf16[192,1728]{1,0:T(8,128)(2,1)S(1)} collective-permute-done((bf16[192,1728]{1,0:T(8,128)(2,1)S(1)}, bf16[192,1728]{1,0:T(8,128)(2,1)S(1)}, u32[]{:S(2)}, u32[]{:S(2)}) %collective-permute-start.25) | collective-permute-done | bytes 663584 | tf_op jit(solution)/shard_map/ppermute | solution.py:588
  70.7 11.0 %attention_backward.1 = (bf16[96,1024]{1,0:T(8,128)(2,1)S(1)}, bf16[96,1024]{1,0:T(8,128)(2,1)S(1)}, bf16[96,1024]{1,0:T(8,128)(2,1)S(1)}, bf16[96,1024]{1,0:T(8...) custom-call(s32[2]{0:T(128)S(1)} %copy-done.6, ...), custom_call_target="tpu_custom_call" | custom-call | flops 16000000000 | bytes 13771776 | tf_op jit(solution)/shard_map/attention_backward/pallas_call | solution.py:565
  81.7 5.8 %collective-permute-done.27 = bf16[192,1728]{1,0:T(8,128)(2,1)S(1)} collective-permute-done((bf16[192,1728]{1,0:T(8,128)(2,1)S(1)}, bf16[192,1728]{1,0:T(8,128)(2,1)S(1)}, u32[]{:S(2)}, u32[]{:S(2)}) %collective-permute-start.27) | collective-permute-done | bytes 663584 | tf_op jit(solution)/shard_map/ppermute | solution.py:588
  88.6 6.0 %all-to-all-start = ((bf16[8,24,1728]{2,1,0:T(8,128)(2,1)}), bf16[8,24,1728]{2,1,0:T(8,128)(2,1)}, u32[]{:S(2)}, u32[]{:S(2)}) async-start(bf16[8,24,1728]{2,1,0:T(8,128)(2,1)} %bitcast.33), calls=%async_computation | async-start | bytes 1376256 | tf_op jit(solution)/shard_map/all_to_all | solution.py:618
  101.9 2.6 %collective-permute-done.34.x1 = bf16[96,1024]{1,0:T(8,128)(2,1)S(1)} collective-permute-done((bf16[96,1024]{1,0:T(8,128)(2,1)S(1)}, bf16[96,1024]{1,0:T(8,128)(2,1)S(1)}, u32[]{:S(2)}, u32[]{:S(2)}) %collective-permute-start.34) | collective-permute-done | bytes 196640 | tf_op jit(solution)/shard_map/ppermute | solution.py:592
  104.6 3.0 %collective-permute-done.36.x3 = bf16[96,1024]{1,0:T(8,128)(2,1)S(1)} collective-permute-done((bf16[96,1024]{1,0:T(8,128)(2,1)S(1)}, bf16[96,1024]{1,0:T(8,128)(2,1)S(1)}, u32[]{:S(2)}, u32[]{:S(2)}) %collective-permute-start.36) | collective-permute-done | bytes 196640 | tf_op jit(solution)/shard_map/ppermute | solution.py:592
  107.6 2.9 %collective-permute-start.37 = (bf16[1,128,192]{2,1,0:T(8,128)(2,1)S(1)}, bf16[1,128,192]{2,1,0:T(8,128)(2,1)S(1)}, u32[]{:S(2)}, u32[]{:S(2)}) collective-permute-start(bf16[1,128,192]{2,1,0:T(8,128)(2,1)S(1)} %bitcast.31), channel_id=1, source_target_pairs={{0,16},{4,20},{8,24},{12,28},{16,0},{20,4},{24,8},{28,12},{1,17},{... | collective-permute-start | bytes 147464 | tf_op jit(solution)/shard_map/ppermute | solution.py:612
  115.4 2.9 %collective-permute-start.39 = (bf16[24,1728]{1,0:T(8,128)(2,1)S(1)}, bf16[24,1728]{1,0:T(8,128)(2,1)S(1)}, u32[]{:S(2)}, u32[]{:S(2)}) collective-permute-start(bf16[24,1728]{1,0:T(8,128)(2,1)S(1)} %reduce_sum.24), channel_id=1, source_target_pairs={{0,16},{4,20},{8,24},{12,28},{16,0},{20,4},{24,8},{28,12},{1,17},{... | collective-permute-start | bytes 248840 | tf_op jit(solution)/shard_map/ppermute | solution.py:612
  118.4 5.1 %all-to-all-start.1 = ((bf16[8,24,576]{2,1,0:T(8,128)(2,1)}), bf16[8,24,576]{2,1,0:T(8,128)(2,1)S(1)}, u32[]{:S(2)}, u32[]{:S(2)}) async-start(bf16[8,24,576]{2,1,0:T(8,128)(2,1)} %bitcast.6), calls=%async_computation.1 | async-start | bytes 491520 | tf_op jit(solution)/shard_map/all_to_all | solution.py:618
  123.4 2.0 %collective-permute-start.41 = (bf16[2,128,192]{2,1,0:T(8,128)(2,1)S(1)}, bf16[2,128,192]{2,1,0:T(8,128)(2,1)S(1)}, u32[]{:S(2)}, u32[]{:S(2)}) collective-permute-start(bf16[2,128,192]{2,1,0:T(8,128)(2,1)S(1)} %pad_maximum_fusion.5), channel_id=1, source_target_pairs={{0,8},{4,12},{8,0},{12,4},{16,24},{20,28},{24,16},{28,20},{1,9},{5... | collective-permute-start | bytes 294920 | tf_op jit(solution)/shard_map/ppermute | solution.py:612
  125.6 2.3 %join_tokens.1 = f32[96,4096]{1,0:T(8,128)} custom-call(s32[2]{0:T(128)S(1)} %copy-done.6, bf16[96,1024]{1,0:T(8,128)(2,1)S(1)} %get-tuple-element.272.x0, bf16[96,1024]{1,0:T(8,128)(2,1)S(1)} %collective-permute-done.34.x1, bf16[96,1024]{1,0:T(8,128)(2,1)S(1)} %collective-permute-done.35.x2, bf16[96,1024]{1,0:T(8,128)(2,1)S(1)} %collective-permute-done.36.x3), custom_call_target="tpu_custom_call" | custom-call | flops 2000000000 | bytes 2359296 | tf_op jit(solution)/shard_map/join_tokens/pallas_call | solution.py:565
  127.9 6.1 %collective-permute-done.41 = bf16[2,128,192]{2,1,0:T(8,128)(2,1)S(1)} collective-permute-done((bf16[2,128,192]{2,1,0:T(8,128)(2,1)S(1)}, bf16[2,128,192]{2,1,0:T(8,128)(2,1)S(1)}, u32[]{:S(2)}, u32[]{:S(2)}) %collective-permute-start.41) | collective-permute-done | bytes 98336 | tf_op jit(solution)/shard_map/ppermute | solution.py:612
  134.1 2.2 %collective-permute-done.40 = bf16[2,24,1728]{2,1,0:T(8,128)(2,1)S(1)} collective-permute-done((bf16[2,24,1728]{2,1,0:T(8,128)(2,1)S(1)}, bf16[2,24,1728]{2,1,0:T(8,128)(2,1)S(1)}, u32[]{:S(2)}, u32[]{:S(2)}) %collective-permute-start.40) | collective-permute-done | bytes 165920 | tf_op jit(solution)/shard_map/ppermute | solution.py:612
  136.3 1.5 collective-permute-start.42
  139.8 4.5 %all-to-all-start.2 = ((bf16[8,24,576]{2,1,0:T(8,128)(2,1)}), bf16[8,24,576]{2,1,0:T(8,128)(2,1)S(1)}, u32[]{:S(2)}, u32[]{:S(2)}) async-start(bf16[8,24,576]{2,1,0:T(8,128)(2,1)} %broadcast_in_dim.10), calls=%async_computation.2 | async-start | bytes 491520 | tf_op jit(solution)/shard_map/all_to_all | solution.py:798
  144.3 1.3 collective-permute-done.42
  145.7 2.6 %modulation_grads.1 = (f32[192,1152]{1,0:T(8,128)}, f32[6,96]{1,0:T(8,128)}, f32[4,192]{1,0:T(4,128)S(1)}, f32[2,192]{1,0:T(2,128)}, f32[1,96]{1,0:T(1,128)}, /*index=5*/f32[1,96]{1,0:T(1,128)}) custom-call(s32[2]{0:T(128)S(1)} %copy-done.6, bf16[8,128,192]{2,1,0:T(8,128)(2,1)S(1)} %pad_maximum_fusion.1.refs_0_), custom_call_target="tpu_custom_call" | custom-call | flops 2000000000 | bytes 1285632 | tf_op jit(solution)/shard_map/modulation_grads/pallas_call | solution.py:565
  149.0 4.0 %collective-permute-done.43 = bf16[2,2,24,1728]{3,2,1,0:T(8,128)(2,1)S(1)} collective-permute-done((bf16[2,2,24,1728]{3,2,1,0:T(8,128)(2,1)S(1)}, bf16[2,2,24,1728]{3,2,1,0:T(8,128)(2,1)S(1)}, u32[]{:S(2)}, u32[]{:S(2)}) %collective-permute-start.43) | collective-permute-done | bytes 331808 | tf_op jit(solution)/shard_map/ppermute | solution.py:612
  (128 shorter events, 30.6 us)
Async XLA Ops:
  0.6 11.3 %collective-permute-start = (bf16[192,576]{1,0:T(8,128)(2,1)}, bf16[192,576]{1,0:T(8,128)(2,1)S(1)}, u32[]{:S(2)}, u32[]{:S(2)}) collective-permute-start(bf16[192,576]{1,0:T(8,128)(2,1)} %wq0.1), channel_id=1, source_target_pairs={{0,1},{1,0},{2,3},{3,2},{4,5},{5,4},{6,7},{7,6},{8,9},{9,8},{10,11... | collective-permute-start | bytes 663560 | tf_op jit(solution)/shard_map/ppermute | solution.py:588
  3.6 12.3 %collective-permute-start.5 = (bf16[192,576]{1,0:T(8,128)(2,1)}, bf16[192,576]{1,0:T(8,128)(2,1)S(1)}, u32[]{:S(2)}, u32[]{:S(2)}) collective-permute-start(bf16[192,576]{1,0:T(8,128)(2,1)} %wq0.1), channel_id=1, source_target_pairs={{0,2},{2,0},{1,3},{3,1},{4,6},{6,4},{5,7},{7,5},{8,10},{10,8},{9,1... | collective-permute-start | bytes 663560 | tf_op jit(solution)/shard_map/ppermute | solution.py:588
  3.6 8.3 %collective-permute-start.1 = (bf16[192,192]{1,0:T(8,128)(2,1)}, bf16[192,192]{1,0:T(8,128)(2,1)S(1)}, u32[]{:S(2)}, u32[]{:S(2)}) collective-permute-start(bf16[192,192]{1,0:T(8,128)(2,1)} %wp0.1), channel_id=1, source_target_pairs={{0,1},{1,0},{2,3},{3,2},{4,5},{5,4},{6,7},{7,6},{8,9},{9,8},{10,11... | collective-permute-start | bytes 221192 | tf_op jit(solution)/shard_map/ppermute | solution.py:588
  3.8 10.4 %collective-permute-start.7 = (bf16[192,192]{1,0:T(8,128)(2,1)}, bf16[192,192]{1,0:T(8,128)(2,1)S(1)}, u32[]{:S(2)}, u32[]{:S(2)}) collective-permute-start(bf16[192,192]{1,0:T(8,128)(2,1)} %wp0.1), channel_id=1, source_target_pairs={{0,2},{2,0},{1,3},{3,1},{4,6},{6,4},{5,7},{7,5},{8,10},{10,8},{9,1... | collective-permute-start | bytes 221192 | tf_op jit(solution)/shard_map/ppermute | solution.py:588
  14.2 8.5 %collective-permute-start.2 = (bf16[96,1024]{1,0:T(8,128)(2,1)}, bf16[96,1024]{1,0:T(8,128)(2,1)S(1)}, u32[]{:S(2)}, u32[]{:S(2)}) collective-permute-start(bf16[96,1024]{1,0:T(8,128)(2,1)} %get-tuple-element.157), channel_id=1, source_target_pairs={{0,1},{1,0},{2,3},{3,2},{4,5},{5,4},{6,7},{7,6},{8,9},{9,8},{10,11... | collective-permute-start | bytes 589832 | tf_op jit(solution)/shard_map/ppermute | solution.py:592
  16.3 9.4 %collective-permute-start.4 = (bf16[96,1024]{1,0:T(8,128)(2,1)}, bf16[96,1024]{1,0:T(8,128)(2,1)S(1)}, u32[]{:S(2)}, u32[]{:S(2)}) collective-permute-start(bf16[96,1024]{1,0:T(8,128)(2,1)} %get-tuple-element.159), channel_id=1, source_target_pairs={{0,3},{1,2},{2,1},{3,0},{4,7},{5,6},{6,5},{7,4},{8,11},{9,10},{10,... | collective-permute-start | bytes 589832 | tf_op jit(solution)/shard_map/ppermute | solution.py:592
  16.3 9.3 %collective-permute-start.6 = (bf16[192,576]{1,0:T(8,128)(2,1)S(1)}, bf16[192,576]{1,0:T(8,128)(2,1)S(1)}, u32[]{:S(2)}, u32[]{:S(2)}) collective-permute-start(bf16[192,576]{1,0:T(8,128)(2,1)S(1)} %collective-permute-done.wq1), channel_id=1, source_target_pairs={{0,2},{2,0},{1,3},{3,1},{4,6},{6,4},{5,7},{7,5},{8,10},{10,8},{9,1... | collective-permute-start | bytes 663560 | tf_op jit(solution)/shard_map/ppermute | solution.py:588
  25.7 15.8 %collective-permute-start.12 = (bf16[192,768]{1,0:T(8,128)(2,1)S(1)}, bf16[192,768]{1,0:T(8,128)(2,1)S(1)}, u32[]{:S(2)}, u32[]{:S(2)}) collective-permute-start(bf16[192,768]{1,0:T(8,128)(2,1)S(1)} %copy-done.2), channel_id=1, source_target_pairs={{0,1},{1,0},{2,3},{3,2},{4,5},{5,4},{6,7},{7,6},{8,9},{9,8},{10,11... | collective-permute-start | bytes 884744 | tf_op jit(solution)/shard_map/ppermute | solution.py:588
  26.2 15.2 %collective-permute-start.14 = (bf16[192,768]{1,0:T(8,128)(2,1)S(1)}, bf16[192,768]{1,0:T(8,128)(2,1)S(1)}, u32[]{:S(2)}, u32[]{:S(2)}) collective-permute-start(bf16[192,768]{1,0:T(8,128)(2,1)S(1)} %copy-done.2), channel_id=1, source_target_pairs={{0,2},{2,0},{1,3},{3,1},{4,6},{6,4},{5,7},{7,5},{8,10},{10,8},{9,1... | collective-permute-start | bytes 884744 | tf_op jit(solution)/shard_map/ppermute | solution.py:588
  26.7 14.7 %collective-permute-start.13 = (bf16[192,768]{1,0:T(8,128)(2,1)S(1)}, bf16[192,768]{1,0:T(8,128)(2,1)S(1)}, u32[]{:S(2)}, u32[]{:S(2)}) collective-permute-start(bf16[192,768]{1,0:T(8,128)(2,1)S(1)} %copy-done.3), channel_id=1, source_target_pairs={{0,1},{1,0},{2,3},{3,2},{4,5},{5,4},{6,7},{7,6},{8,9},{9,8},{10,11... | collective-permute-start | bytes 884744 | tf_op jit(solution)/shard_map/ppermute | solution.py:588
  27.9 13.6 %collective-permute-start.15 = (bf16[192,768]{1,0:T(8,128)(2,1)S(1)}, bf16[192,768]{1,0:T(8,128)(2,1)S(1)}, u32[]{:S(2)}, u32[]{:S(2)}) collective-permute-start(bf16[192,768]{1,0:T(8,128)(2,1)S(1)} %copy-done.3), channel_id=1, source_target_pairs={{0,2},{2,0},{1,3},{3,1},{4,6},{6,4},{5,7},{7,5},{8,10},{10,8},{9,1... | collective-permute-start | bytes 884744 | tf_op jit(solution)/shard_map/ppermute | solution.py:588
  27.9 13.5 %collective-permute-start.16 = (bf16[1,768]{1,0:T(2,128)(2,1)S(1)}, bf16[1,768]{1,0:T(2,128)(2,1)S(1)}, u32[]{:S(2)}, u32[]{:S(2)}) collective-permute-start(bf16[1,768]{1,0:T(2,128)(2,1)S(1)} %reshape.59.b10), channel_id=1, source_target_pairs={{0,1},{1,0},{2,3},{3,2},{4,5},{5,4},{6,7},{7,6},{8,9},{9,8},{10,11... | collective-permute-start | bytes 4616 | tf_op jit(solution)/shard_map/ppermute | solution.py:588
  42.0 10.6 %collective-permute-start.19 = (bf16[96,1024]{1,0:T(8,128)(2,1)S(1)}, bf16[96,1024]{1,0:T(8,128)(2,1)S(1)}, u32[]{:S(2)}, u32[]{:S(2)}) collective-permute-start(bf16[96,1024]{1,0:T(8,128)(2,1)S(1)} %get-tuple-element.209), channel_id=1, source_target_pairs={{0,1},{1,0},{2,3},{3,2},{4,5},{5,4},{6,7},{7,6},{8,9},{9,8},{10,11... | collective-permute-start | bytes 589832 | tf_op jit(solution)/shard_map/ppermute | solution.py:592
  42.9 9.7 %collective-permute-start.20 = (bf16[96,1024]{1,0:T(8,128)(2,1)S(1)}, bf16[96,1024]{1,0:T(8,128)(2,1)S(1)}, u32[]{:S(2)}, u32[]{:S(2)}) collective-permute-start(bf16[96,1024]{1,0:T(8,128)(2,1)S(1)} %get-tuple-element.210), channel_id=1, source_target_pairs={{0,2},{1,3},{2,0},{3,1},{4,6},{5,7},{6,4},{7,5},{8,10},{9,11},{10,... | collective-permute-start | bytes 589832 | tf_op jit(solution)/shard_map/ppermute | solution.py:592
  42.9 9.7 %collective-permute-start.21 = (bf16[96,1024]{1,0:T(8,128)(2,1)S(1)}, bf16[96,1024]{1,0:T(8,128)(2,1)S(1)}, u32[]{:S(2)}, u32[]{:S(2)}) collective-permute-start(bf16[96,1024]{1,0:T(8,128)(2,1)S(1)} %get-tuple-element.211), channel_id=1, source_target_pairs={{0,3},{1,2},{2,1},{3,0},{4,7},{5,6},{6,5},{7,4},{8,11},{9,10},{10,... | collective-permute-start | bytes 589832 | tf_op jit(solution)/shard_map/ppermute | solution.py:592
  52.6 14.6 %collective-permute-start.22 = (bf16[96,1024]{1,0:T(8,128)(2,1)S(1)}, bf16[96,1024]{1,0:T(8,128)(2,1)S(1)}, u32[]{:S(2)}, u32[]{:S(2)}) collective-permute-start(bf16[96,1024]{1,0:T(8,128)(2,1)S(1)} %get-tuple-element.223), channel_id=1, source_target_pairs={{0,1},{1,0},{2,3},{3,2},{4,5},{5,4},{6,7},{7,6},{8,9},{9,8},{10,11... | collective-permute-start | bytes 589832 | tf_op jit(solution)/shard_map/ppermute | solution.py:592
  53.6 13.7 %collective-permute-start.23 = (bf16[96,1024]{1,0:T(8,128)(2,1)S(1)}, bf16[96,1024]{1,0:T(8,128)(2,1)S(1)}, u32[]{:S(2)}, u32[]{:S(2)}) collective-permute-start(bf16[96,1024]{1,0:T(8,128)(2,1)S(1)} %get-tuple-element.224), channel_id=1, source_target_pairs={{0,2},{1,3},{2,0},{3,1},{4,6},{5,7},{6,4},{7,5},{8,10},{9,11},{10,... | collective-permute-start | bytes 589832 | tf_op jit(solution)/shard_map/ppermute | solution.py:592
  53.6 13.7 %collective-permute-start.24 = (bf16[96,1024]{1,0:T(8,128)(2,1)S(1)}, bf16[96,1024]{1,0:T(8,128)(2,1)S(1)}, u32[]{:S(2)}, u32[]{:S(2)}) collective-permute-start(bf16[96,1024]{1,0:T(8,128)(2,1)S(1)} %get-tuple-element.225), channel_id=1, source_target_pairs={{0,3},{1,2},{2,1},{3,0},{4,7},{5,6},{6,5},{7,4},{8,11},{9,10},{10,... | collective-permute-start | bytes 589832 | tf_op jit(solution)/shard_map/ppermute | solution.py:592
  69.6 12.1 %collective-permute-start.26 = (bf16[192,1728]{1,0:T(8,128)(2,1)S(1)}, bf16[192,1728]{1,0:T(8,128)(2,1)S(1)}, u32[]{:S(2)}, u32[]{:S(2)}) collective-permute-start(bf16[192,1728]{1,0:T(8,128)(2,1)S(1)} %get-tuple-element.242), channel_id=1, source_target_pairs={{0,2},{2,0},{1,3},{3,1},{4,6},{6,4},{5,7},{7,5},{8,10},{10,8},{9,1... | collective-permute-start | bytes 1990664 | tf_op jit(solution)/shard_map/ppermute | solution.py:588
  69.8 17.7 %collective-permute-start.27 = (bf16[192,1728]{1,0:T(8,128)(2,1)S(1)}, bf16[192,1728]{1,0:T(8,128)(2,1)S(1)}, u32[]{:S(2)}, u32[]{:S(2)}) collective-permute-start(bf16[192,1728]{1,0:T(8,128)(2,1)S(1)} %add_convert_fusion.1), channel_id=1, source_target_pairs={{0,1},{1,0},{2,3},{3,2},{4,5},{5,4},{6,7},{7,6},{8,9},{9,8},{10,11... | collective-permute-start | bytes 1990664 | tf_op jit(solution)/shard_map/ppermute | solution.py:588
  88.6 25.6 %all-to-all-start = ((bf16[8,24,1728]{2,1,0:T(8,128)(2,1)}), bf16[8,24,1728]{2,1,0:T(8,128)(2,1)}, u32[]{:S(2)}, u32[]{:S(2)}) async-start(bf16[8,24,1728]{2,1,0:T(8,128)(2,1)} %bitcast.33), calls=%async_computation | async-start | bytes 1376256 | tf_op jit(solution)/shard_map/all_to_all | solution.py:618
  96.8 7.7 %collective-permute-start.34 = (bf16[96,1024]{1,0:T(8,128)(2,1)S(1)}, bf16[96,1024]{1,0:T(8,128)(2,1)S(1)}, u32[]{:S(2)}, u32[]{:S(2)}) collective-permute-start(bf16[96,1024]{1,0:T(8,128)(2,1)S(1)} %get-tuple-element.260), channel_id=1, source_target_pairs={{0,1},{1,0},{2,3},{3,2},{4,5},{5,4},{6,7},{7,6},{8,9},{9,8},{10,11... | collective-permute-start | bytes 589832 | tf_op jit(solution)/shard_map/ppermute | solution.py:592
  98.7 8.9 %collective-permute-start.36 = (bf16[96,1024]{1,0:T(8,128)(2,1)S(1)}, bf16[96,1024]{1,0:T(8,128)(2,1)S(1)}, u32[]{:S(2)}, u32[]{:S(2)}) collective-permute-start(bf16[96,1024]{1,0:T(8,128)(2,1)S(1)} %get-tuple-element.262), channel_id=1, source_target_pairs={{0,3},{1,2},{2,1},{3,0},{4,7},{5,6},{6,5},{7,4},{8,11},{9,10},{10,... | collective-permute-start | bytes 589832 | tf_op jit(solution)/shard_map/ppermute | solution.py:592
  99.8 13.5 %collective-permute-start.28 = (bf16[192,576]{1,0:T(8,128)(2,1)S(1)}, bf16[192,576]{1,0:T(8,128)(2,1)S(1)}, u32[]{:S(2)}, u32[]{:S(2)}) collective-permute-start(bf16[192,576]{1,0:T(8,128)(2,1)S(1)} %get-tuple-element.249), channel_id=1, source_target_pairs={{0,2},{2,0},{1,3},{3,1},{4,6},{6,4},{5,7},{7,5},{8,10},{10,8},{9,1... | collective-permute-start | bytes 663560 | tf_op jit(solution)/shard_map/ppermute | solution.py:588
  99.9 13.5 %collective-permute-start.30 = (bf16[192,576]{1,0:T(8,128)(2,1)S(1)}, bf16[192,576]{1,0:T(8,128)(2,1)S(1)}, u32[]{:S(2)}, u32[]{:S(2)}) collective-permute-start(bf16[192,576]{1,0:T(8,128)(2,1)S(1)} %add_convert_fusion.3), channel_id=1, source_target_pairs={{0,1},{1,0},{2,3},{3,2},{4,5},{5,4},{6,7},{7,6},{8,9},{9,8},{10,11... | collective-permute-start | bytes 663560 | tf_op jit(solution)/shard_map/ppermute | solution.py:588
  115.4 10.0 %collective-permute-start.39 = (bf16[24,1728]{1,0:T(8,128)(2,1)S(1)}, bf16[24,1728]{1,0:T(8,128)(2,1)S(1)}, u32[]{:S(2)}, u32[]{:S(2)}) collective-permute-start(bf16[24,1728]{1,0:T(8,128)(2,1)S(1)} %reduce_sum.24), channel_id=1, source_target_pairs={{0,16},{4,20},{8,24},{12,28},{16,0},{20,4},{24,8},{28,12},{1,17},{... | collective-permute-start | bytes 248840 | tf_op jit(solution)/shard_map/ppermute | solution.py:612
  118.4 17.9 %all-to-all-start.1 = ((bf16[8,24,576]{2,1,0:T(8,128)(2,1)}), bf16[8,24,576]{2,1,0:T(8,128)(2,1)S(1)}, u32[]{:S(2)}, u32[]{:S(2)}) async-start(bf16[8,24,576]{2,1,0:T(8,128)(2,1)} %bitcast.6), calls=%async_computation.1 | async-start | bytes 491520 | tf_op jit(solution)/shard_map/all_to_all | solution.py:618
  123.4 10.6 %collective-permute-start.41 = (bf16[2,128,192]{2,1,0:T(8,128)(2,1)S(1)}, bf16[2,128,192]{2,1,0:T(8,128)(2,1)S(1)}, u32[]{:S(2)}, u32[]{:S(2)}) collective-permute-start(bf16[2,128,192]{2,1,0:T(8,128)(2,1)S(1)} %pad_maximum_fusion.5), channel_id=1, source_target_pairs={{0,8},{4,12},{8,0},{12,4},{16,24},{20,28},{24,16},{28,20},{1,9},{5... | collective-permute-start | bytes 294920 | tf_op jit(solution)/shard_map/ppermute | solution.py:612
  125.5 10.7 %collective-permute-start.40 = (bf16[2,24,1728]{2,1,0:T(8,128)(2,1)S(1)}, bf16[2,24,1728]{2,1,0:T(8,128)(2,1)S(1)}, u32[]{:S(2)}, u32[]{:S(2)}) collective-permute-start(bf16[2,24,1728]{2,1,0:T(8,128)(2,1)S(1)} %pad_maximum_fusion.4), channel_id=1, source_target_pairs={{0,8},{4,12},{8,0},{12,4},{16,24},{20,28},{24,16},{28,20},{1,9},{5... | collective-permute-start | bytes 497672 | tf_op jit(solution)/shard_map/ppermute | solution.py:612
  136.3 9.3 %collective-permute-start.42 = (bf16[4,128,192]{2,1,0:T(8,128)(2,1)S(1)}, bf16[4,128,192]{2,1,0:T(8,128)(2,1)S(1)}, u32[]{:S(2)}, u32[]{:S(2)}) collective-permute-start(bf16[4,128,192]{2,1,0:T(8,128)(2,1)S(1)} %pad_maximum_fusion.3), channel_id=1, source_target_pairs={{0,4},{4,0},{8,12},{12,8},{16,20},{20,16},{24,28},{28,24},{1,5},{5... | collective-permute-start | bytes 589832 | tf_op jit(solution)/shard_map/ppermute | solution.py:612
  137.8 15.1 %collective-permute-start.43 = (bf16[2,2,24,1728]{3,2,1,0:T(8,128)(2,1)S(1)}, bf16[2,2,24,1728]{3,2,1,0:T(8,128)(2,1)S(1)}, u32[]{:S(2)}, u32[]{:S(2)}) collective-permute-start(bf16[2,2,24,1728]{3,2,1,0:T(8,128)(2,1)S(1)} %pad_maximum_fusion.2), channel_id=1, source_target_pairs={{0,4},{4,0},{8,12},{12,8},{16,20},{20,16},{24,28},{28,24},{1,5},{5... | collective-permute-start | bytes 995336 | tf_op jit(solution)/shard_map/ppermute | solution.py:612
  139.8 15.2 %all-to-all-start.2 = ((bf16[8,24,576]{2,1,0:T(8,128)(2,1)}), bf16[8,24,576]{2,1,0:T(8,128)(2,1)S(1)}, u32[]{:S(2)}, u32[]{:S(2)}) async-start(bf16[8,24,576]{2,1,0:T(8,128)(2,1)} %broadcast_in_dim.10), calls=%async_computation.2 | async-start | bytes 491520 | tf_op jit(solution)/shard_map/all_to_all | solution.py:798
  (31 other events, 260.5 us)

commit v5 on v4

--- a/solution.py
+++ b/solution.py
@@ -783,7 +783,7 @@
     )
     qkv_parts = scatter_terms(qkv)
     fc = jnp.sum(fc_parts.astype(F32), axis=0).astype(BF16)
-    for bit in bits[:-1]:
+    for bit in bits[:-2]:
         fc = double(fc, bit)
     for bit in bits[-2:-1]:
         everyone = jnp.concatenate([everyone, dp_step(everyone, bit)])
@@ -791,12 +791,13 @@
         join_tokens, pos, 4, seq, [("w", a) for a in ins],
         [("j", shape((quarter, tokens), F32))], [], 2, "join_tokens",
     )[0]
-    qkv_parts, fc, everyone, input_grad = lax.optimization_barrier(
-        (qkv_parts, fc, everyone, input_grad)
+    cond_grad = jax.vjp(jax.nn.silu, condition)[1](cond_part)[0]
+    qkv_parts, fc, everyone, input_grad, cond_grad = lax.optimization_barrier(
+        (qkv_parts, fc, everyone, input_grad, cond_grad)
     )
     qkv = jnp.sum(qkv_parts.astype(F32), axis=0).astype(BF16)
     qkv = lax.all_to_all(jnp.broadcast_to(qkv[None], (count,) + qkv.shape), "dp", 0, 0)
-    for bit in bits[-1:]:
+    for bit in bits[-2:]:
         fc = double(fc, bit)
     for bit in bits[-1:]:
         everyone = jnp.concatenate([everyone, dp_step(everyone, bit)])
@@ -809,8 +810,6 @@
         "modulation_grads",
     )
     grads_qkv = qkv.reshape(qkv_block).astype(F32)
-    silu_back = jax.vjp(jax.nn.silu, condition)[1]
-    cond_grad = silu_back(cond_part)[0]
     return (
         block_output,
         input_grad,

time: 156 us -> 154 us (0.987)
  waiting for transfers between devices: 44 us -> 39.2 us
  starting transfers between devices: 50.9 us -> 53.4 us
    ppermute x6, waiting for transfers between devices: 14.5 us -> 7.03 us  [dp_step(): return lax.ppermute(value, 'dp', [(at, at ^ bit) for at in range(count)])]
    all_to_all x1, waiting for transfers between devices: 0.01 us -> 2.71 us  [local(): lax.all_to_all(jnp.broadcast_to(qkv[None], (count,) + qkv.shape), 'dp', 0...]
    all_to_all x2, starting transfers between devices: 11 us -> 13.3 us  [scatter_terms(): lax.all_to_all(value.reshape(count, rows // count, columns), 'dp', 0, 0)]
  transfers between devices with their start and end apart: 47 -> 47, of which waited for: 18 -> 17; matrix products, arithmetic and copies ran while one was open for 4% -> 4% of each run, Pallas kernels for 32% -> 32%
where the time goes in v5:
time: 154 us
  starting transfers between devices  53.4 us (35%)
  Pallas kernels  49.4 us (32%)
  waiting for transfers between devices  39.2 us (25%)
  other arithmetic  5.93 us (4%)
  local copies, waits for them, and re-layouts  4.64 us (3%)
    pallas_call x9, Pallas kernels, call(): pl.pallas_call(kernel, grid_spec=pltpu.PrefetchScalarGridSpec(num_scalar_...  49.4 us
    ppermute x20, waiting for transfers between devices, swap(): return lax.ppermute(value, axis, [(0, 1), (1, 0)])  16.7 us
    all_to_all x2, starting transfers between devices, scatter_terms(): lax.all_to_all(value.reshape(count, rows // count, columns), 'dp', 0, 0)  13.3 us
    ppermute x18, waiting for transfers between devices, group_step(): return lax.ppermute(value, GROUP, [(at, at ^ step) for at in range(4)])  12.8 us
    ppermute x20, starting transfers between devices, swap(): return lax.ppermute(value, axis, [(0, 1), (1, 0)])  12.7 us
    ppermute x18, starting transfers between devices, group_step(): return lax.ppermute(value, GROUP, [(at, at ^ step) for at in range(4)])  12.6 us
    ppermute x6, starting transfers between devices, dp_step(): return lax.ppermute(value, 'dp', [(at, at ^ bit) for at in range(count)])  11 us
    ppermute x6, waiting for transfers between devices, dp_step(): return lax.ppermute(value, 'dp', [(at, at ^ bit) for at in range(count)])  7.03 us
  transfers between devices with their start and end apart: 47, of which 17 were waited for; matrix products, arithmetic and copies ran while one was open for 4% of the time, Pallas kernels for 32%

profile of v5, /device:TPU:0, one launch (start us, length us, event | category | flops | bytes accessed | tf_op | source)
XLA Modules:
  0.0 153.6 jit_solution(4721262057091196614)
XLA Ops:
  0.6 3.0 %collective-permute-start = (bf16[192,576]{1,0:T(8,128)(2,1)}, bf16[192,576]{1,0:T(8,128)(2,1)S(1)}, u32[]{:S(2)}, u32[]{:S(2)}) collective-permute-start(bf16[192,576]{1,0:T(8,128)(2,1)} %wq0.1), channel_id=1, source_target_pairs={{0,1},{1,0},{2,3},{3,2},{4,5},{5,4},{6,7},{7,6},{8,9},{9,8},{10,11... | collective-permute-start | bytes 663560 | tf_op jit(solution)/shard_map/ppermute | solution.py:588
  4.8 5.3 %modulation_parts.1 = (bf16[96,1024]{1,0:T(8,128)(2,1)}, bf16[96,1024]{1,0:T(8,128)(2,1)}, bf16[96,1024]{1,0:T(8,128)(2,1)}, f32[40,192]{1,0:T(8,128)}, f32[40,1...) custom-call(s32[2]{0:T(128)} %pad_add_fusion.pos, ...), custom_call_target="tpu_custom_call" | custom-call | flops 6000000000 | bytes 2404608 | tf_op jit(solution)/shard_map/modulation_parts/pallas_call | solution.py:565
  10.0 1.9 %collective-permute-done.1.wp1 = bf16[192,192]{1,0:T(8,128)(2,1)S(1)} collective-permute-done((bf16[192,192]{1,0:T(8,128)(2,1)}, bf16[192,192]{1,0:T(8,128)(2,1)S(1)}, u32[]{:S(2)}, u32[]{:S(2)}) %collective-permute-start.1) | collective-permute-done | bytes 73760 | tf_op jit(solution)/shard_map/ppermute | solution.py:588
  12.0 1.8 %collective-permute-start.9 = (f32[40,192]{1,0:T(8,128)}, f32[40,192]{1,0:T(8,128)S(1)}, u32[]{:S(2)}, u32[]{:S(2)}) collective-permute-start(f32[40,192]{1,0:T(8,128)} %get-tuple-element.164), channel_id=1, source_target_pairs={{0,1},{1,0},{2,3},{3,2},{4,5},{5,4},{6,7},{7,6},{8,9},{9,8},{10,11... | collective-permute-start | bytes 92168 | tf_op jit(solution)/shard_map/ppermute | solution.py:592
  14.2 1.7 %collective-permute-start.2 = (bf16[96,1024]{1,0:T(8,128)(2,1)}, bf16[96,1024]{1,0:T(8,128)(2,1)S(1)}, u32[]{:S(2)}, u32[]{:S(2)}) collective-permute-start(bf16[96,1024]{1,0:T(8,128)(2,1)} %get-tuple-element.158), channel_id=1, source_target_pairs={{0,1},{1,0},{2,3},{3,2},{4,5},{5,4},{6,7},{7,6},{8,9},{9,8},{10,11... | collective-permute-start | bytes 589832 | tf_op jit(solution)/shard_map/ppermute | solution.py:592
  16.3 2.0 %collective-permute-start.6 = (bf16[192,576]{1,0:T(8,128)(2,1)S(1)}, bf16[192,576]{1,0:T(8,128)(2,1)S(1)}, u32[]{:S(2)}, u32[]{:S(2)}) collective-permute-start(bf16[192,576]{1,0:T(8,128)(2,1)S(1)} %collective-permute-done.wq1), channel_id=1, source_target_pairs={{0,2},{2,0},{1,3},{3,1},{4,6},{6,4},{5,7},{7,5},{8,10},{10,8},{9,1... | collective-permute-start | bytes 663560 | tf_op jit(solution)/shard_map/ppermute | solution.py:588
  19.7 3.0 %collective-permute-done.2.x1 = bf16[96,1024]{1,0:T(8,128)(2,1)S(1)} collective-permute-done((bf16[96,1024]{1,0:T(8,128)(2,1)}, bf16[96,1024]{1,0:T(8,128)(2,1)S(1)}, u32[]{:S(2)}, u32[]{:S(2)}) %collective-permute-start.2) | collective-permute-done | bytes 196640 | tf_op jit(solution)/shard_map/ppermute | solution.py:592
  22.7 2.9 %collective-permute-done.4.x3 = bf16[96,1024]{1,0:T(8,128)(2,1)S(1)} collective-permute-done((bf16[96,1024]{1,0:T(8,128)(2,1)}, bf16[96,1024]{1,0:T(8,128)(2,1)S(1)}, u32[]{:S(2)}, u32[]{:S(2)}) %collective-permute-start.4) | collective-permute-done | bytes 196640 | tf_op jit(solution)/shard_map/ppermute | solution.py:592
  28.8 7.4 %attention_forward.1 = (bf16[384,1024]{1,0:T(8,128)(2,1)S(1)}, bf16[384,1024]{1,0:T(8,128)(2,1)S(1)}, bf16[2,576,1024]{2,1,0:T(8,128)(2,1)S(1)}, bf16[4,6,256,25...) custom-call(s32[2]{0:T(128)S(1)} %copy-done.6, ...), custom_call_target="tpu_custom_call" | custom-call | flops 16000000000 | bytes 12165120 | tf_op jit(solution)/shard_map/attention_forward/pallas_call | solution.py:565
  36.2 5.2 %collective-permute-done.16.b11 = bf16[1,768]{1,0:T(2,128)(2,1)S(1)} collective-permute-done((bf16[1,768]{1,0:T(2,128)(2,1)S(1)}, bf16[1,768]{1,0:T(2,128)(2,1)S(1)}, u32[]{:S(2)}, u32[]{:S(2)}) %collective-permute-start.16) | collective-permute-done | bytes 1568 | tf_op jit(solution)/shard_map/ppermute | solution.py:588
  44.2 8.4 %mlp_forward.1 = (bf16[96,1024]{1,0:T(8,128)(2,1)S(1)}, bf16[96,1024]{1,0:T(8,128)(2,1)S(1)}, bf16[96,1024]{1,0:T(8,128)(2,1)S(1)}, bf16[96,1024]{1,0:T(8,128)(2...) custom-call(s32[2]{0:T(128)S(1)} %copy-done.6, ...), custom_call_target="tpu_custom_call" | custom-call | flops 12000000000 | bytes 13544448 | tf_op jit(solution)/shard_map/mlp_forward/pallas_call | solution.py:565
  53.6 1.3 collective-permute-start.24
  54.8 1.4 copy-done.9
  56.2 10.9 %mlp_backward.1 = (bf16[384,1024]{1,0:T(8,128)(2,1)S(1)}, bf16[384,1024]{1,0:T(8,128)(2,1)S(1)}, f32[4,384,4]{2,1,0:T(8,128)S(1)}, bf16[192,1728]{1,0:T(8,128)(2...) custom-call(s32[2]{0:T(128)S(1)} %copy-done.6, ...), custom_call_target="tpu_custom_call" | custom-call | flops 20000000000 | bytes 19350528 | tf_op jit(solution)/shard_map/mlp_backward/pallas_call | solution.py:565
  67.3 2.1 %collective-permute-done.25 = bf16[192,1728]{1,0:T(8,128)(2,1)S(1)} collective-permute-done((bf16[192,1728]{1,0:T(8,128)(2,1)S(1)}, bf16[192,1728]{1,0:T(8,128)(2,1)S(1)}, u32[]{:S(2)}, u32[]{:S(2)}) %collective-permute-start.25) | collective-permute-done | bytes 663584 | tf_op jit(solution)/shard_map/ppermute | solution.py:588
  70.7 11.0 %attention_backward.1 = (bf16[96,1024]{1,0:T(8,128)(2,1)S(1)}, bf16[96,1024]{1,0:T(8,128)(2,1)S(1)}, bf16[96,1024]{1,0:T(8,128)(2,1)S(1)}, bf16[96,1024]{1,0:T(8...) custom-call(s32[2]{0:T(128)S(1)} %copy-done.6, ...), custom_call_target="tpu_custom_call" | custom-call | flops 16000000000 | bytes 13771776 | tf_op jit(solution)/shard_map/attention_backward/pallas_call | solution.py:565
  81.7 5.8 %collective-permute-done.27 = bf16[192,1728]{1,0:T(8,128)(2,1)S(1)} collective-permute-done((bf16[192,1728]{1,0:T(8,128)(2,1)S(1)}, bf16[192,1728]{1,0:T(8,128)(2,1)S(1)}, u32[]{:S(2)}, u32[]{:S(2)}) %collective-permute-start.27) | collective-permute-done | bytes 663584 | tf_op jit(solution)/shard_map/ppermute | solution.py:588
  88.6 6.0 %all-to-all-start = ((bf16[8,24,1728]{2,1,0:T(8,128)(2,1)}), bf16[8,24,1728]{2,1,0:T(8,128)(2,1)}, u32[]{:S(2)}, u32[]{:S(2)}) async-start(bf16[8,24,1728]{2,1,0:T(8,128)(2,1)} %bitcast.33), calls=%async_computation | async-start | bytes 1376256 | tf_op jit(solution)/shard_map/all_to_all | solution.py:618
  101.9 2.6 %collective-permute-done.34.x1 = bf16[96,1024]{1,0:T(8,128)(2,1)S(1)} collective-permute-done((bf16[96,1024]{1,0:T(8,128)(2,1)S(1)}, bf16[96,1024]{1,0:T(8,128)(2,1)S(1)}, u32[]{:S(2)}, u32[]{:S(2)}) %collective-permute-start.34) | collective-permute-done | bytes 196640 | tf_op jit(solution)/shard_map/ppermute | solution.py:592
  104.6 3.0 %collective-permute-done.36.x3 = bf16[96,1024]{1,0:T(8,128)(2,1)S(1)} collective-permute-done((bf16[96,1024]{1,0:T(8,128)(2,1)S(1)}, bf16[96,1024]{1,0:T(8,128)(2,1)S(1)}, u32[]{:S(2)}, u32[]{:S(2)}) %collective-permute-start.36) | collective-permute-done | bytes 196640 | tf_op jit(solution)/shard_map/ppermute | solution.py:592
  107.6 2.9 %collective-permute-start.37 = (bf16[1,128,192]{2,1,0:T(8,128)(2,1)S(1)}, bf16[1,128,192]{2,1,0:T(8,128)(2,1)S(1)}, u32[]{:S(2)}, u32[]{:S(2)}) collective-permute-start(bf16[1,128,192]{2,1,0:T(8,128)(2,1)S(1)} %bitcast.31), channel_id=1, source_target_pairs={{0,16},{4,20},{8,24},{12,28},{16,0},{20,4},{24,8},{28,12},{1,17},{... | collective-permute-start | bytes 147464 | tf_op jit(solution)/shard_map/ppermute | solution.py:612
  114.2 7.4 %all-to-all-start.1 = ((bf16[8,24,576]{2,1,0:T(8,128)(2,1)}), bf16[8,24,576]{2,1,0:T(8,128)(2,1)S(1)}, u32[]{:S(2)}, u32[]{:S(2)}) async-start(bf16[8,24,576]{2,1,0:T(8,128)(2,1)} %bitcast.6), calls=%async_computation.1 | async-start | bytes 491520 | tf_op jit(solution)/shard_map/all_to_all | solution.py:618
  122.8 3.0 %collective-permute-start.39 = (bf16[24,1728]{1,0:T(8,128)(2,1)S(1)}, bf16[24,1728]{1,0:T(8,128)(2,1)S(1)}, u32[]{:S(2)}, u32[]{:S(2)}) collective-permute-start(bf16[24,1728]{1,0:T(8,128)(2,1)S(1)} %reduce_sum.24), channel_id=1, source_target_pairs={{0,16},{4,20},{8,24},{12,28},{16,0},{20,4},{24,8},{28,12},{1,17},{... | collective-permute-start | bytes 248840 | tf_op jit(solution)/shard_map/ppermute | solution.py:612
  125.8 1.5 collective-permute-start.40
  127.9 2.3 %join_tokens.1 = f32[96,4096]{1,0:T(8,128)} custom-call(s32[2]{0:T(128)S(1)} %copy-done.6, bf16[96,1024]{1,0:T(8,128)(2,1)S(1)} %get-tuple-element.273.x0, bf16[96,1024]{1,0:T(8,128)(2,1)S(1)} %collective-permute-done.34.x1, bf16[96,1024]{1,0:T(8,128)(2,1)S(1)} %collective-permute-done.35.x2, bf16[96,1024]{1,0:T(8,128)(2,1)S(1)} %collective-permute-done.36.x3), custom_call_target="tpu_custom_call" | custom-call | flops 2000000000 | bytes 2359296 | tf_op jit(solution)/shard_map/join_tokens/pallas_call | solution.py:565
  130.1 3.9 %collective-permute-done.39 = bf16[24,1728]{1,0:T(8,128)(2,1)S(1)} collective-permute-done((bf16[24,1728]{1,0:T(8,128)(2,1)S(1)}, bf16[24,1728]{1,0:T(8,128)(2,1)S(1)}, u32[]{:S(2)}, u32[]{:S(2)}) %collective-permute-start.39) | collective-permute-done | bytes 82976 | tf_op jit(solution)/shard_map/ppermute | solution.py:612
  134.3 1.5 collective-permute-start.41
  136.6 3.7 %all-to-all-start.2 = ((bf16[8,24,576]{2,1,0:T(8,128)(2,1)}), bf16[8,24,576]{2,1,0:T(8,128)(2,1)S(1)}, u32[]{:S(2)}, u32[]{:S(2)}) async-start(bf16[8,24,576]{2,1,0:T(8,128)(2,1)} %broadcast_in_dim.10), calls=%async_computation.2 | async-start | bytes 491520 | tf_op jit(solution)/shard_map/all_to_all | solution.py:799
  140.4 2.1 %collective-permute-start.43 = (bf16[2,2,24,1728]{3,2,1,0:T(8,128)(2,1)S(1)}, bf16[2,2,24,1728]{3,2,1,0:T(8,128)(2,1)S(1)}, u32[]{:S(2)}, u32[]{:S(2)}) collective-permute-start(bf16[2,2,24,1728]{3,2,1,0:T(8,128)(2,1)S(1)} %pad_maximum_fusion.2), channel_id=1, source_target_pairs={{0,4},{4,0},{8,12},{12,8},{16,20},{20,16},{24,28},{28,24},{1,5},{5... | collective-permute-start | bytes 995336 | tf_op jit(solution)/shard_map/ppermute | solution.py:612
  142.5 2.6 %modulation_grads.1 = (f32[192,1152]{1,0:T(8,128)}, f32[6,96]{1,0:T(8,128)}, f32[4,192]{1,0:T(4,128)S(1)}, f32[2,192]{1,0:T(2,128)}, f32[1,96]{1,0:T(1,128)}, /*index=5*/f32[1,96]{1,0:T(1,128)}) custom-call(s32[2]{0:T(128)S(1)} %copy-done.6, bf16[8,128,192]{2,1,0:T(8,128)(2,1)S(1)} %pad_maximum_fusion.1.refs_0_), custom_call_target="tpu_custom_call" | custom-call | flops 2000000000 | bytes 1285632 | tf_op jit(solution)/shard_map/modulation_grads/pallas_call | solution.py:565
  145.8 2.7 %all-to-all-done.2 = bf16[8,24,576]{2,1,0:T(8,128)(2,1)S(1)} async-done(((bf16[8,24,576]{2,1,0:T(8,128)(2,1)}), bf16[8,24,576]{2,1,0:T(8,128)(2,1)S(1)}, u32[]{:S(2)}, u32[]{:S(2)}) %all-to-all-start.2) | async-done | bytes 221216 | tf_op jit(solution)/shard_map/all_to_all | solution.py:799
  149.3 2.2 %collective-permute-done.43 = bf16[2,2,24,1728]{3,2,1,0:T(8,128)(2,1)S(1)} collective-permute-done((bf16[2,2,24,1728]{3,2,1,0:T(8,128)(2,1)S(1)}, bf16[2,2,24,1728]{3,2,1,0:T(8,128)(2,1)S(1)}, u32[]{:S(2)}, u32[]{:S(2)}) %collective-permute-start.43) | collective-permute-done | bytes 331808 | tf_op jit(solution)/shard_map/ppermute | solution.py:612
  (128 shorter events, 30.0 us)
Async XLA Ops:
  0.6 11.3 %collective-permute-start = (bf16[192,576]{1,0:T(8,128)(2,1)}, bf16[192,576]{1,0:T(8,128)(2,1)S(1)}, u32[]{:S(2)}, u32[]{:S(2)}) collective-permute-start(bf16[192,576]{1,0:T(8,128)(2,1)} %wq0.1), channel_id=1, source_target_pairs={{0,1},{1,0},{2,3},{3,2},{4,5},{5,4},{6,7},{7,6},{8,9},{9,8},{10,11... | collective-permute-start | bytes 663560 | tf_op jit(solution)/shard_map/ppermute | solution.py:588
  3.6 12.3 %collective-permute-start.5 = (bf16[192,576]{1,0:T(8,128)(2,1)}, bf16[192,576]{1,0:T(8,128)(2,1)S(1)}, u32[]{:S(2)}, u32[]{:S(2)}) collective-permute-start(bf16[192,576]{1,0:T(8,128)(2,1)} %wq0.1), channel_id=1, source_target_pairs={{0,2},{2,0},{1,3},{3,1},{4,6},{6,4},{5,7},{7,5},{8,10},{10,8},{9,1... | collective-permute-start | bytes 663560 | tf_op jit(solution)/shard_map/ppermute | solution.py:588
  3.6 8.3 %collective-permute-start.1 = (bf16[192,192]{1,0:T(8,128)(2,1)}, bf16[192,192]{1,0:T(8,128)(2,1)S(1)}, u32[]{:S(2)}, u32[]{:S(2)}) collective-permute-start(bf16[192,192]{1,0:T(8,128)(2,1)} %wp0.1), channel_id=1, source_target_pairs={{0,1},{1,0},{2,3},{3,2},{4,5},{5,4},{6,7},{7,6},{8,9},{9,8},{10,11... | collective-permute-start | bytes 221192 | tf_op jit(solution)/shard_map/ppermute | solution.py:588
  3.8 10.4 %collective-permute-start.7 = (bf16[192,192]{1,0:T(8,128)(2,1)}, bf16[192,192]{1,0:T(8,128)(2,1)S(1)}, u32[]{:S(2)}, u32[]{:S(2)}) collective-permute-start(bf16[192,192]{1,0:T(8,128)(2,1)} %wp0.1), channel_id=1, source_target_pairs={{0,2},{2,0},{1,3},{3,1},{4,6},{6,4},{5,7},{7,5},{8,10},{10,8},{9,1... | collective-permute-start | bytes 221192 | tf_op jit(solution)/shard_map/ppermute | solution.py:588
  14.2 8.5 %collective-permute-start.2 = (bf16[96,1024]{1,0:T(8,128)(2,1)}, bf16[96,1024]{1,0:T(8,128)(2,1)S(1)}, u32[]{:S(2)}, u32[]{:S(2)}) collective-permute-start(bf16[96,1024]{1,0:T(8,128)(2,1)} %get-tuple-element.158), channel_id=1, source_target_pairs={{0,1},{1,0},{2,3},{3,2},{4,5},{5,4},{6,7},{7,6},{8,9},{9,8},{10,11... | collective-permute-start | bytes 589832 | tf_op jit(solution)/shard_map/ppermute | solution.py:592
  15.9 6.8 %collective-permute-start.3 = (bf16[96,1024]{1,0:T(8,128)(2,1)}, bf16[96,1024]{1,0:T(8,128)(2,1)S(1)}, u32[]{:S(2)}, u32[]{:S(2)}) collective-permute-start(bf16[96,1024]{1,0:T(8,128)(2,1)} %get-tuple-element.159), channel_id=1, source_target_pairs={{0,2},{1,3},{2,0},{3,1},{4,6},{5,7},{6,4},{7,5},{8,10},{9,11},{10,... | collective-permute-start | bytes 589832 | tf_op jit(solution)/shard_map/ppermute | solution.py:592
  16.3 9.4 %collective-permute-start.4 = (bf16[96,1024]{1,0:T(8,128)(2,1)}, bf16[96,1024]{1,0:T(8,128)(2,1)S(1)}, u32[]{:S(2)}, u32[]{:S(2)}) collective-permute-start(bf16[96,1024]{1,0:T(8,128)(2,1)} %get-tuple-element.160), channel_id=1, source_target_pairs={{0,3},{1,2},{2,1},{3,0},{4,7},{5,6},{6,5},{7,4},{8,11},{9,10},{10,... | collective-permute-start | bytes 589832 | tf_op jit(solution)/shard_map/ppermute | solution.py:592
  16.3 9.3 %collective-permute-start.6 = (bf16[192,576]{1,0:T(8,128)(2,1)S(1)}, bf16[192,576]{1,0:T(8,128)(2,1)S(1)}, u32[]{:S(2)}, u32[]{:S(2)}) collective-permute-start(bf16[192,576]{1,0:T(8,128)(2,1)S(1)} %collective-permute-done.wq1), channel_id=1, source_target_pairs={{0,2},{2,0},{1,3},{3,1},{4,6},{6,4},{5,7},{7,5},{8,10},{10,8},{9,1... | collective-permute-start | bytes 663560 | tf_op jit(solution)/shard_map/ppermute | solution.py:588
  25.7 15.8 %collective-permute-start.12 = (bf16[192,768]{1,0:T(8,128)(2,1)S(1)}, bf16[192,768]{1,0:T(8,128)(2,1)S(1)}, u32[]{:S(2)}, u32[]{:S(2)}) collective-permute-start(bf16[192,768]{1,0:T(8,128)(2,1)S(1)} %copy-done.2), channel_id=1, source_target_pairs={{0,1},{1,0},{2,3},{3,2},{4,5},{5,4},{6,7},{7,6},{8,9},{9,8},{10,11... | collective-permute-start | bytes 884744 | tf_op jit(solution)/shard_map/ppermute | solution.py:588
  26.2 15.2 %collective-permute-start.14 = (bf16[192,768]{1,0:T(8,128)(2,1)S(1)}, bf16[192,768]{1,0:T(8,128)(2,1)S(1)}, u32[]{:S(2)}, u32[]{:S(2)}) collective-permute-start(bf16[192,768]{1,0:T(8,128)(2,1)S(1)} %copy-done.2), channel_id=1, source_target_pairs={{0,2},{2,0},{1,3},{3,1},{4,6},{6,4},{5,7},{7,5},{8,10},{10,8},{9,1... | collective-permute-start | bytes 884744 | tf_op jit(solution)/shard_map/ppermute | solution.py:588
  26.7 14.7 %collective-permute-start.13 = (bf16[192,768]{1,0:T(8,128)(2,1)S(1)}, bf16[192,768]{1,0:T(8,128)(2,1)S(1)}, u32[]{:S(2)}, u32[]{:S(2)}) collective-permute-start(bf16[192,768]{1,0:T(8,128)(2,1)S(1)} %copy-done.3), channel_id=1, source_target_pairs={{0,1},{1,0},{2,3},{3,2},{4,5},{5,4},{6,7},{7,6},{8,9},{9,8},{10,11... | collective-permute-start | bytes 884744 | tf_op jit(solution)/shard_map/ppermute | solution.py:588
  27.9 13.6 %collective-permute-start.15 = (bf16[192,768]{1,0:T(8,128)(2,1)S(1)}, bf16[192,768]{1,0:T(8,128)(2,1)S(1)}, u32[]{:S(2)}, u32[]{:S(2)}) collective-permute-start(bf16[192,768]{1,0:T(8,128)(2,1)S(1)} %copy-done.3), channel_id=1, source_target_pairs={{0,2},{2,0},{1,3},{3,1},{4,6},{6,4},{5,7},{7,5},{8,10},{10,8},{9,1... | collective-permute-start | bytes 884744 | tf_op jit(solution)/shard_map/ppermute | solution.py:588
  27.9 13.5 %collective-permute-start.16 = (bf16[1,768]{1,0:T(2,128)(2,1)S(1)}, bf16[1,768]{1,0:T(2,128)(2,1)S(1)}, u32[]{:S(2)}, u32[]{:S(2)}) collective-permute-start(bf16[1,768]{1,0:T(2,128)(2,1)S(1)} %reshape.59.b10), channel_id=1, source_target_pairs={{0,1},{1,0},{2,3},{3,2},{4,5},{5,4},{6,7},{7,6},{8,9},{9,8},{10,11... | collective-permute-start | bytes 4616 | tf_op jit(solution)/shard_map/ppermute | solution.py:588
  42.0 10.6 %collective-permute-start.19 = (bf16[96,1024]{1,0:T(8,128)(2,1)S(1)}, bf16[96,1024]{1,0:T(8,128)(2,1)S(1)}, u32[]{:S(2)}, u32[]{:S(2)}) collective-permute-start(bf16[96,1024]{1,0:T(8,128)(2,1)S(1)} %get-tuple-element.210), channel_id=1, source_target_pairs={{0,1},{1,0},{2,3},{3,2},{4,5},{5,4},{6,7},{7,6},{8,9},{9,8},{10,11... | collective-permute-start | bytes 589832 | tf_op jit(solution)/shard_map/ppermute | solution.py:592
  42.9 9.7 %collective-permute-start.20 = (bf16[96,1024]{1,0:T(8,128)(2,1)S(1)}, bf16[96,1024]{1,0:T(8,128)(2,1)S(1)}, u32[]{:S(2)}, u32[]{:S(2)}) collective-permute-start(bf16[96,1024]{1,0:T(8,128)(2,1)S(1)} %get-tuple-element.211), channel_id=1, source_target_pairs={{0,2},{1,3},{2,0},{3,1},{4,6},{5,7},{6,4},{7,5},{8,10},{9,11},{10,... | collective-permute-start | bytes 589832 | tf_op jit(solution)/shard_map/ppermute | solution.py:592
  42.9 9.7 %collective-permute-start.21 = (bf16[96,1024]{1,0:T(8,128)(2,1)S(1)}, bf16[96,1024]{1,0:T(8,128)(2,1)S(1)}, u32[]{:S(2)}, u32[]{:S(2)}) collective-permute-start(bf16[96,1024]{1,0:T(8,128)(2,1)S(1)} %get-tuple-element.212), channel_id=1, source_target_pairs={{0,3},{1,2},{2,1},{3,0},{4,7},{5,6},{6,5},{7,4},{8,11},{9,10},{10,... | collective-permute-start | bytes 589832 | tf_op jit(solution)/shard_map/ppermute | solution.py:592
  52.6 14.6 %collective-permute-start.22 = (bf16[96,1024]{1,0:T(8,128)(2,1)S(1)}, bf16[96,1024]{1,0:T(8,128)(2,1)S(1)}, u32[]{:S(2)}, u32[]{:S(2)}) collective-permute-start(bf16[96,1024]{1,0:T(8,128)(2,1)S(1)} %get-tuple-element.224), channel_id=1, source_target_pairs={{0,1},{1,0},{2,3},{3,2},{4,5},{5,4},{6,7},{7,6},{8,9},{9,8},{10,11... | collective-permute-start | bytes 589832 | tf_op jit(solution)/shard_map/ppermute | solution.py:592
  53.6 13.7 %collective-permute-start.23 = (bf16[96,1024]{1,0:T(8,128)(2,1)S(1)}, bf16[96,1024]{1,0:T(8,128)(2,1)S(1)}, u32[]{:S(2)}, u32[]{:S(2)}) collective-permute-start(bf16[96,1024]{1,0:T(8,128)(2,1)S(1)} %get-tuple-element.225), channel_id=1, source_target_pairs={{0,2},{1,3},{2,0},{3,1},{4,6},{5,7},{6,4},{7,5},{8,10},{9,11},{10,... | collective-permute-start | bytes 589832 | tf_op jit(solution)/shard_map/ppermute | solution.py:592
  53.6 13.7 %collective-permute-start.24 = (bf16[96,1024]{1,0:T(8,128)(2,1)S(1)}, bf16[96,1024]{1,0:T(8,128)(2,1)S(1)}, u32[]{:S(2)}, u32[]{:S(2)}) collective-permute-start(bf16[96,1024]{1,0:T(8,128)(2,1)S(1)} %get-tuple-element.226), channel_id=1, source_target_pairs={{0,3},{1,2},{2,1},{3,0},{4,7},{5,6},{6,5},{7,4},{8,11},{9,10},{10,... | collective-permute-start | bytes 589832 | tf_op jit(solution)/shard_map/ppermute | solution.py:592
  69.6 12.1 %collective-permute-start.26 = (bf16[192,1728]{1,0:T(8,128)(2,1)S(1)}, bf16[192,1728]{1,0:T(8,128)(2,1)S(1)}, u32[]{:S(2)}, u32[]{:S(2)}) collective-permute-start(bf16[192,1728]{1,0:T(8,128)(2,1)S(1)} %get-tuple-element.243), channel_id=1, source_target_pairs={{0,2},{2,0},{1,3},{3,1},{4,6},{6,4},{5,7},{7,5},{8,10},{10,8},{9,1... | collective-permute-start | bytes 1990664 | tf_op jit(solution)/shard_map/ppermute | solution.py:588
  69.8 17.7 %collective-permute-start.27 = (bf16[192,1728]{1,0:T(8,128)(2,1)S(1)}, bf16[192,1728]{1,0:T(8,128)(2,1)S(1)}, u32[]{:S(2)}, u32[]{:S(2)}) collective-permute-start(bf16[192,1728]{1,0:T(8,128)(2,1)S(1)} %add_convert_fusion.1), channel_id=1, source_target_pairs={{0,1},{1,0},{2,3},{3,2},{4,5},{5,4},{6,7},{7,6},{8,9},{9,8},{10,11... | collective-permute-start | bytes 1990664 | tf_op jit(solution)/shard_map/ppermute | solution.py:588
  88.6 25.6 %all-to-all-start = ((bf16[8,24,1728]{2,1,0:T(8,128)(2,1)}), bf16[8,24,1728]{2,1,0:T(8,128)(2,1)}, u32[]{:S(2)}, u32[]{:S(2)}) async-start(bf16[8,24,1728]{2,1,0:T(8,128)(2,1)} %bitcast.33), calls=%async_computation | async-start | bytes 1376256 | tf_op jit(solution)/shard_map/all_to_all | solution.py:618
  96.8 7.7 %collective-permute-start.34 = (bf16[96,1024]{1,0:T(8,128)(2,1)S(1)}, bf16[96,1024]{1,0:T(8,128)(2,1)S(1)}, u32[]{:S(2)}, u32[]{:S(2)}) collective-permute-start(bf16[96,1024]{1,0:T(8,128)(2,1)S(1)} %get-tuple-element.261), channel_id=1, source_target_pairs={{0,1},{1,0},{2,3},{3,2},{4,5},{5,4},{6,7},{7,6},{8,9},{9,8},{10,11... | collective-permute-start | bytes 589832 | tf_op jit(solution)/shard_map/ppermute | solution.py:592
  98.7 8.9 %collective-permute-start.36 = (bf16[96,1024]{1,0:T(8,128)(2,1)S(1)}, bf16[96,1024]{1,0:T(8,128)(2,1)S(1)}, u32[]{:S(2)}, u32[]{:S(2)}) collective-permute-start(bf16[96,1024]{1,0:T(8,128)(2,1)S(1)} %get-tuple-element.263), channel_id=1, source_target_pairs={{0,3},{1,2},{2,1},{3,0},{4,7},{5,6},{6,5},{7,4},{8,11},{9,10},{10,... | collective-permute-start | bytes 589832 | tf_op jit(solution)/shard_map/ppermute | solution.py:592
  99.8 13.5 %collective-permute-start.28 = (bf16[192,576]{1,0:T(8,128)(2,1)S(1)}, bf16[192,576]{1,0:T(8,128)(2,1)S(1)}, u32[]{:S(2)}, u32[]{:S(2)}) collective-permute-start(bf16[192,576]{1,0:T(8,128)(2,1)S(1)} %get-tuple-element.250), channel_id=1, source_target_pairs={{0,2},{2,0},{1,3},{3,1},{4,6},{6,4},{5,7},{7,5},{8,10},{10,8},{9,1... | collective-permute-start | bytes 663560 | tf_op jit(solution)/shard_map/ppermute | solution.py:588
  99.9 13.5 %collective-permute-start.30 = (bf16[192,576]{1,0:T(8,128)(2,1)S(1)}, bf16[192,576]{1,0:T(8,128)(2,1)S(1)}, u32[]{:S(2)}, u32[]{:S(2)}) collective-permute-start(bf16[192,576]{1,0:T(8,128)(2,1)S(1)} %add_convert_fusion.3), channel_id=1, source_target_pairs={{0,1},{1,0},{2,3},{3,2},{4,5},{5,4},{6,7},{7,6},{8,9},{9,8},{10,11... | collective-permute-start | bytes 663560 | tf_op jit(solution)/shard_map/ppermute | solution.py:588
  114.2 20.0 %all-to-all-start.1 = ((bf16[8,24,576]{2,1,0:T(8,128)(2,1)}), bf16[8,24,576]{2,1,0:T(8,128)(2,1)S(1)}, u32[]{:S(2)}, u32[]{:S(2)}) async-start(bf16[8,24,576]{2,1,0:T(8,128)(2,1)} %bitcast.6), calls=%async_computation.1 | async-start | bytes 491520 | tf_op jit(solution)/shard_map/all_to_all | solution.py:618
  122.8 11.3 %collective-permute-start.39 = (bf16[24,1728]{1,0:T(8,128)(2,1)S(1)}, bf16[24,1728]{1,0:T(8,128)(2,1)S(1)}, u32[]{:S(2)}, u32[]{:S(2)}) collective-permute-start(bf16[24,1728]{1,0:T(8,128)(2,1)S(1)} %reduce_sum.24), channel_id=1, source_target_pairs={{0,16},{4,20},{8,24},{12,28},{16,0},{20,4},{24,8},{28,12},{1,17},{... | collective-permute-start | bytes 248840 | tf_op jit(solution)/shard_map/ppermute | solution.py:612
  125.8 8.3 %collective-permute-start.40 = (bf16[2,128,192]{2,1,0:T(8,128)(2,1)S(1)}, bf16[2,128,192]{2,1,0:T(8,128)(2,1)S(1)}, u32[]{:S(2)}, u32[]{:S(2)}) collective-permute-start(bf16[2,128,192]{2,1,0:T(8,128)(2,1)S(1)} %pad_maximum_fusion.5), channel_id=1, source_target_pairs={{0,8},{4,12},{8,0},{12,4},{16,24},{20,28},{24,16},{28,20},{1,9},{5... | collective-permute-start | bytes 294920 | tf_op jit(solution)/shard_map/ppermute | solution.py:612
  134.3 8.1 %collective-permute-start.41 = (bf16[4,128,192]{2,1,0:T(8,128)(2,1)S(1)}, bf16[4,128,192]{2,1,0:T(8,128)(2,1)S(1)}, u32[]{:S(2)}, u32[]{:S(2)}) collective-permute-start(bf16[4,128,192]{2,1,0:T(8,128)(2,1)S(1)} %pad_maximum_fusion.3), channel_id=1, source_target_pairs={{0,4},{4,0},{8,12},{12,8},{16,20},{20,16},{24,28},{28,24},{1,5},{5... | collective-permute-start | bytes 589832 | tf_op jit(solution)/shard_map/ppermute | solution.py:612
  136.6 11.9 %all-to-all-start.2 = ((bf16[8,24,576]{2,1,0:T(8,128)(2,1)}), bf16[8,24,576]{2,1,0:T(8,128)(2,1)S(1)}, u32[]{:S(2)}, u32[]{:S(2)}) async-start(bf16[8,24,576]{2,1,0:T(8,128)(2,1)} %broadcast_in_dim.10), calls=%async_computation.2 | async-start | bytes 491520 | tf_op jit(solution)/shard_map/all_to_all | solution.py:799
  140.4 11.2 %collective-permute-start.43 = (bf16[2,2,24,1728]{3,2,1,0:T(8,128)(2,1)S(1)}, bf16[2,2,24,1728]{3,2,1,0:T(8,128)(2,1)S(1)}, u32[]{:S(2)}, u32[]{:S(2)}) collective-permute-start(bf16[2,2,24,1728]{3,2,1,0:T(8,128)(2,1)S(1)} %pad_maximum_fusion.2), channel_id=1, source_target_pairs={{0,4},{4,0},{8,12},{12,8},{16,20},{20,16},{24,28},{28,24},{1,5},{5... | collective-permute-start | bytes 995336 | tf_op jit(solution)/shard_map/ppermute | solution.py:612
  (31 other events, 274.5 us)

commit v6 on v5

--- a/solution.py
+++ b/solution.py
@@ -301,7 +301,7 @@
     attended = attended_out[...]
     for part in range(2):
         rows = slice(part * third, (part + 1) * third)
-        branch_out[rows] = dot_nn(wp_t[part], attended) + bias_p[rows]
+        branch_out[rows] = (dot_nn(wp_t[part], attended) + bias_p[rows]).astype(BF16)
 
 
 def mlp_forward(
@@ -692,7 +692,7 @@
         [("o", block_input)] + [("t", a) for a in x_moved]
         + [("w", a) for a in (*wq, *wp, *packs)],
         [("tv", t_low), ("tv", t_low), ("tv", shape((2, 3 * third, width), BF16)),
-         ("lv", shape((steps, HEADS, seq, seq), BF16)), ("tv", t_low), ("tv", t_wide),
+         ("lv", shape((steps, HEADS, seq, seq), BF16)), ("tv", t_low), ("tv", t_low),
          ("lv", shape((steps, D, 8), F32))],
         [pltpu.VMEM((D, seq * TOGETHER.get("attention_forward", 1)), F32),
          pltpu.VMEM((2, D, 3 * third), BF16), pltpu.VMEM((2, 3 * third, D), BF16), pltpu.VMEM((2, D, third), BF16),

time: 154 us -> 152 us (0.987)
  no operation moved by 1% of the time
where the time goes in v6:
time: 152 us
  starting transfers between devices  53.4 us (35%)
  Pallas kernels  49.1 us (32%)
  waiting for transfers between devices  39.2 us (26%)
  other arithmetic  5.93 us (4%)
  local copies, waits for them, and re-layouts  3.22 us (2%)
    pallas_call x9, Pallas kernels, call(): pl.pallas_call(kernel, grid_spec=pltpu.PrefetchScalarGridSpec(num_scalar_...  49.1 us
    ppermute x20, waiting for transfers between devices, swap(): return lax.ppermute(value, axis, [(0, 1), (1, 0)])  16.7 us
    all_to_all x2, starting transfers between devices, scatter_terms(): lax.all_to_all(value.reshape(count, rows // count, columns), 'dp', 0, 0)  13.3 us
    ppermute x18, waiting for transfers between devices, group_step(): return lax.ppermute(value, GROUP, [(at, at ^ step) for at in range(4)])  12.8 us
    ppermute x20, starting transfers between devices, swap(): return lax.ppermute(value, axis, [(0, 1), (1, 0)])  12.8 us
    ppermute x18, starting transfers between devices, group_step(): return lax.ppermute(value, GROUP, [(at, at ^ step) for at in range(4)])  12.6 us
    ppermute x6, starting transfers between devices, dp_step(): return lax.ppermute(value, 'dp', [(at, at ^ bit) for at in range(count)])  11 us
    ppermute x6, waiting for transfers between devices, dp_step(): return lax.ppermute(value, 'dp', [(at, at ^ bit) for at in range(count)])  7.03 us
  transfers between devices with their start and end apart: 47, of which 17 were waited for; matrix products, arithmetic and copies ran while one was open for 4% of the time, Pallas kernels for 32%

profile of v6, /device:TPU:0, one launch (start us, length us, event | category | flops | bytes accessed | tf_op | source)
XLA Modules:
  0.0 151.9 jit_solution(2066012520064355581)
XLA Ops:
  0.6 3.0 %collective-permute-start = (bf16[192,576]{1,0:T(8,128)(2,1)}, bf16[192,576]{1,0:T(8,128)(2,1)S(1)}, u32[]{:S(2)}, u32[]{:S(2)}) collective-permute-start(bf16[192,576]{1,0:T(8,128)(2,1)} %wq0.1), channel_id=1, source_target_pairs={{0,1},{1,0},{2,3},{3,2},{4,5},{5,4},{6,7},{7,6},{8,9},{9,8},{10,11... | collective-permute-start | bytes 663560 | tf_op jit(solution)/shard_map/ppermute | solution.py:588
  4.8 5.3 %modulation_parts.1 = (bf16[96,1024]{1,0:T(8,128)(2,1)}, bf16[96,1024]{1,0:T(8,128)(2,1)}, bf16[96,1024]{1,0:T(8,128)(2,1)}, f32[40,192]{1,0:T(8,128)}, f32[40,1...) custom-call(s32[2]{0:T(128)} %pad_add_fusion.pos, ...), custom_call_target="tpu_custom_call" | custom-call | flops 6000000000 | bytes 2404608 | tf_op jit(solution)/shard_map/modulation_parts/pallas_call | solution.py:565
  10.0 1.9 %collective-permute-done.1.wp1 = bf16[192,192]{1,0:T(8,128)(2,1)S(1)} collective-permute-done((bf16[192,192]{1,0:T(8,128)(2,1)}, bf16[192,192]{1,0:T(8,128)(2,1)S(1)}, u32[]{:S(2)}, u32[]{:S(2)}) %collective-permute-start.1) | collective-permute-done | bytes 73760 | tf_op jit(solution)/shard_map/ppermute | solution.py:588
  12.0 1.8 %collective-permute-start.9 = (f32[40,192]{1,0:T(8,128)}, f32[40,192]{1,0:T(8,128)S(1)}, u32[]{:S(2)}, u32[]{:S(2)}) collective-permute-start(f32[40,192]{1,0:T(8,128)} %get-tuple-element.164), channel_id=1, source_target_pairs={{0,1},{1,0},{2,3},{3,2},{4,5},{5,4},{6,7},{7,6},{8,9},{9,8},{10,11... | collective-permute-start | bytes 92168 | tf_op jit(solution)/shard_map/ppermute | solution.py:592
  14.2 1.7 %collective-permute-start.2 = (bf16[96,1024]{1,0:T(8,128)(2,1)}, bf16[96,1024]{1,0:T(8,128)(2,1)S(1)}, u32[]{:S(2)}, u32[]{:S(2)}) collective-permute-start(bf16[96,1024]{1,0:T(8,128)(2,1)} %get-tuple-element.158), channel_id=1, source_target_pairs={{0,1},{1,0},{2,3},{3,2},{4,5},{5,4},{6,7},{7,6},{8,9},{9,8},{10,11... | collective-permute-start | bytes 589832 | tf_op jit(solution)/shard_map/ppermute | solution.py:592
  16.3 2.0 %collective-permute-start.6 = (bf16[192,576]{1,0:T(8,128)(2,1)S(1)}, bf16[192,576]{1,0:T(8,128)(2,1)S(1)}, u32[]{:S(2)}, u32[]{:S(2)}) collective-permute-start(bf16[192,576]{1,0:T(8,128)(2,1)S(1)} %collective-permute-done.wq1), channel_id=1, source_target_pairs={{0,2},{2,0},{1,3},{3,1},{4,6},{6,4},{5,7},{7,5},{8,10},{10,8},{9,1... | collective-permute-start | bytes 663560 | tf_op jit(solution)/shard_map/ppermute | solution.py:588
  19.7 3.0 %collective-permute-done.2.x1 = bf16[96,1024]{1,0:T(8,128)(2,1)S(1)} collective-permute-done((bf16[96,1024]{1,0:T(8,128)(2,1)}, bf16[96,1024]{1,0:T(8,128)(2,1)S(1)}, u32[]{:S(2)}, u32[]{:S(2)}) %collective-permute-start.2) | collective-permute-done | bytes 196640 | tf_op jit(solution)/shard_map/ppermute | solution.py:592
  22.7 2.9 %collective-permute-done.4.x3 = bf16[96,1024]{1,0:T(8,128)(2,1)S(1)} collective-permute-done((bf16[96,1024]{1,0:T(8,128)(2,1)}, bf16[96,1024]{1,0:T(8,128)(2,1)S(1)}, u32[]{:S(2)}, u32[]{:S(2)}) %collective-permute-start.4) | collective-permute-done | bytes 196640 | tf_op jit(solution)/shard_map/ppermute | solution.py:592
  28.8 7.4 %attention_forward.1 = (bf16[384,1024]{1,0:T(8,128)(2,1)S(1)}, bf16[384,1024]{1,0:T(8,128)(2,1)S(1)}, bf16[2,576,1024]{2,1,0:T(8,128)(2,1)S(1)}, bf16[4,6,256,25...) custom-call(s32[2]{0:T(128)S(1)} %copy-done.6, ...), custom_call_target="tpu_custom_call" | custom-call | flops 16000000000 | bytes 11378688 | tf_op jit(solution)/shard_map/attention_forward/pallas_call | solution.py:565
  36.2 5.3 %collective-permute-done.16.b11 = bf16[1,768]{1,0:T(2,128)(2,1)S(1)} collective-permute-done((bf16[1,768]{1,0:T(2,128)(2,1)S(1)}, bf16[1,768]{1,0:T(2,128)(2,1)S(1)}, u32[]{:S(2)}, u32[]{:S(2)}) %collective-permute-start.16) | collective-permute-done | bytes 1568 | tf_op jit(solution)/shard_map/ppermute | solution.py:588
  42.9 1.3 collective-permute-start.21
  44.2 8.3 %mlp_forward.1 = (bf16[96,1024]{1,0:T(8,128)(2,1)S(1)}, bf16[96,1024]{1,0:T(8,128)(2,1)S(1)}, bf16[96,1024]{1,0:T(8,128)(2,1)S(1)}, bf16[96,1024]{1,0:T(8,128)(2...) custom-call(s32[2]{0:T(128)S(1)} %copy-done.6, ...), custom_call_target="tpu_custom_call" | custom-call | flops 12000000000 | bytes 12758016 | tf_op jit(solution)/shard_map/mlp_forward/pallas_call | solution.py:565
  53.5 1.2 collective-permute-start.24
  54.7 10.8 %mlp_backward.1 = (bf16[384,1024]{1,0:T(8,128)(2,1)S(1)}, bf16[384,1024]{1,0:T(8,128)(2,1)S(1)}, f32[4,384,4]{2,1,0:T(8,128)S(1)}, bf16[192,1728]{1,0:T(8,128)(2...) custom-call(s32[2]{0:T(128)S(1)} %copy-done.6, ...), custom_call_target="tpu_custom_call" | custom-call | flops 20000000000 | bytes 18564096 | tf_op jit(solution)/shard_map/mlp_backward/pallas_call | solution.py:565
  65.7 2.1 %collective-permute-done.25 = bf16[192,1728]{1,0:T(8,128)(2,1)S(1)} collective-permute-done((bf16[192,1728]{1,0:T(8,128)(2,1)S(1)}, bf16[192,1728]{1,0:T(8,128)(2,1)S(1)}, u32[]{:S(2)}, u32[]{:S(2)}) %collective-permute-start.25) | collective-permute-done | bytes 663584 | tf_op jit(solution)/shard_map/ppermute | solution.py:588
  69.0 11.0 %attention_backward.1 = (bf16[96,1024]{1,0:T(8,128)(2,1)S(1)}, bf16[96,1024]{1,0:T(8,128)(2,1)S(1)}, bf16[96,1024]{1,0:T(8,128)(2,1)S(1)}, bf16[96,1024]{1,0:T(8...) custom-call(s32[2]{0:T(128)S(1)} %copy-done.6, ...), custom_call_target="tpu_custom_call" | custom-call | flops 16000000000 | bytes 13771776 | tf_op jit(solution)/shard_map/attention_backward/pallas_call | solution.py:565
  80.0 5.8 %collective-permute-done.27 = bf16[192,1728]{1,0:T(8,128)(2,1)S(1)} collective-permute-done((bf16[192,1728]{1,0:T(8,128)(2,1)S(1)}, bf16[192,1728]{1,0:T(8,128)(2,1)S(1)}, u32[]{:S(2)}, u32[]{:S(2)}) %collective-permute-start.27) | collective-permute-done | bytes 663584 | tf_op jit(solution)/shard_map/ppermute | solution.py:588
  86.9 6.0 %all-to-all-start = ((bf16[8,24,1728]{2,1,0:T(8,128)(2,1)}), bf16[8,24,1728]{2,1,0:T(8,128)(2,1)}, u32[]{:S(2)}, u32[]{:S(2)}) async-start(bf16[8,24,1728]{2,1,0:T(8,128)(2,1)} %bitcast.33), calls=%async_computation | async-start | bytes 1376256 | tf_op jit(solution)/shard_map/all_to_all | solution.py:618
  100.3 2.6 %collective-permute-done.34.x1 = bf16[96,1024]{1,0:T(8,128)(2,1)S(1)} collective-permute-done((bf16[96,1024]{1,0:T(8,128)(2,1)S(1)}, bf16[96,1024]{1,0:T(8,128)(2,1)S(1)}, u32[]{:S(2)}, u32[]{:S(2)}) %collective-permute-start.34) | collective-permute-done | bytes 196640 | tf_op jit(solution)/shard_map/ppermute | solution.py:592
  102.9 3.0 %collective-permute-done.36.x3 = bf16[96,1024]{1,0:T(8,128)(2,1)S(1)} collective-permute-done((bf16[96,1024]{1,0:T(8,128)(2,1)S(1)}, bf16[96,1024]{1,0:T(8,128)(2,1)S(1)}, u32[]{:S(2)}, u32[]{:S(2)}) %collective-permute-start.36) | collective-permute-done | bytes 196640 | tf_op jit(solution)/shard_map/ppermute | solution.py:592
  105.9 2.9 %collective-permute-start.37 = (bf16[1,128,192]{2,1,0:T(8,128)(2,1)S(1)}, bf16[1,128,192]{2,1,0:T(8,128)(2,1)S(1)}, u32[]{:S(2)}, u32[]{:S(2)}) collective-permute-start(bf16[1,128,192]{2,1,0:T(8,128)(2,1)S(1)} %bitcast.31), channel_id=1, source_target_pairs={{0,16},{4,20},{8,24},{12,28},{16,0},{20,4},{24,8},{28,12},{1,17},{... | collective-permute-start | bytes 147464 | tf_op jit(solution)/shard_map/ppermute | solution.py:612
  112.6 7.4 %all-to-all-start.1 = ((bf16[8,24,576]{2,1,0:T(8,128)(2,1)}), bf16[8,24,576]{2,1,0:T(8,128)(2,1)S(1)}, u32[]{:S(2)}, u32[]{:S(2)}) async-start(bf16[8,24,576]{2,1,0:T(8,128)(2,1)} %bitcast.6), calls=%async_computation.1 | async-start | bytes 491520 | tf_op jit(solution)/shard_map/all_to_all | solution.py:618
  121.1 3.0 %collective-permute-start.39 = (bf16[24,1728]{1,0:T(8,128)(2,1)S(1)}, bf16[24,1728]{1,0:T(8,128)(2,1)S(1)}, u32[]{:S(2)}, u32[]{:S(2)}) collective-permute-start(bf16[24,1728]{1,0:T(8,128)(2,1)S(1)} %reduce_sum.24), channel_id=1, source_target_pairs={{0,16},{4,20},{8,24},{12,28},{16,0},{20,4},{24,8},{28,12},{1,17},{... | collective-permute-start | bytes 248840 | tf_op jit(solution)/shard_map/ppermute | solution.py:612
  124.1 1.5 collective-permute-start.40
  126.2 2.3 %join_tokens.1 = f32[96,4096]{1,0:T(8,128)} custom-call(s32[2]{0:T(128)S(1)} %copy-done.6, bf16[96,1024]{1,0:T(8,128)(2,1)S(1)} %get-tuple-element.273.x0, bf16[96,1024]{1,0:T(8,128)(2,1)S(1)} %collective-permute-done.34.x1, bf16[96,1024]{1,0:T(8,128)(2,1)S(1)} %collective-permute-done.35.x2, bf16[96,1024]{1,0:T(8,128)(2,1)S(1)} %collective-permute-done.36.x3), custom_call_target="tpu_custom_call" | custom-call | flops 2000000000 | bytes 2359296 | tf_op jit(solution)/shard_map/join_tokens/pallas_call | solution.py:565
  128.5 3.9 %collective-permute-done.39 = bf16[24,1728]{1,0:T(8,128)(2,1)S(1)} collective-permute-done((bf16[24,1728]{1,0:T(8,128)(2,1)S(1)}, bf16[24,1728]{1,0:T(8,128)(2,1)S(1)}, u32[]{:S(2)}, u32[]{:S(2)}) %collective-permute-start.39) | collective-permute-done | bytes 82976 | tf_op jit(solution)/shard_map/ppermute | solution.py:612
  132.6 1.5 %collective-permute-start.41 = (bf16[4,128,192]{2,1,0:T(8,128)(2,1)S(1)}, bf16[4,128,192]{2,1,0:T(8,128)(2,1)S(1)}, u32[]{:S(2)}, u32[]{:S(2)}) collective-permute-start(bf16[4,128,192]{2,1,0:T(8,128)(2,1)S(1)} %pad_maximum_fusion.3), channel_id=1, source_target_pairs={{0,4},{4,0},{8,12},{12,8},{16,20},{20,16},{24,28},{28,24},{1,5},{5... | collective-permute-start | bytes 589832 | tf_op jit(solution)/shard_map/ppermute | solution.py:612
  134.9 3.7 %all-to-all-start.2 = ((bf16[8,24,576]{2,1,0:T(8,128)(2,1)}), bf16[8,24,576]{2,1,0:T(8,128)(2,1)S(1)}, u32[]{:S(2)}, u32[]{:S(2)}) async-start(bf16[8,24,576]{2,1,0:T(8,128)(2,1)} %broadcast_in_dim.10), calls=%async_computation.2 | async-start | bytes 491520 | tf_op jit(solution)/shard_map/all_to_all | solution.py:799
  138.7 2.1 %collective-permute-start.43 = (bf16[2,2,24,1728]{3,2,1,0:T(8,128)(2,1)S(1)}, bf16[2,2,24,1728]{3,2,1,0:T(8,128)(2,1)S(1)}, u32[]{:S(2)}, u32[]{:S(2)}) collective-permute-start(bf16[2,2,24,1728]{3,2,1,0:T(8,128)(2,1)S(1)} %pad_maximum_fusion.2), channel_id=1, source_target_pairs={{0,4},{4,0},{8,12},{12,8},{16,20},{20,16},{24,28},{28,24},{1,5},{5... | collective-permute-start | bytes 995336 | tf_op jit(solution)/shard_map/ppermute | solution.py:612
  140.9 2.6 %modulation_grads.1 = (f32[192,1152]{1,0:T(8,128)}, f32[6,96]{1,0:T(8,128)}, f32[4,192]{1,0:T(4,128)S(1)}, f32[2,192]{1,0:T(2,128)}, f32[1,96]{1,0:T(1,128)}, /*index=5*/f32[1,96]{1,0:T(1,128)}) custom-call(s32[2]{0:T(128)S(1)} %copy-done.6, bf16[8,128,192]{2,1,0:T(8,128)(2,1)S(1)} %pad_maximum_fusion.1.refs_0_), custom_call_target="tpu_custom_call" | custom-call | flops 2000000000 | bytes 1285632 | tf_op jit(solution)/shard_map/modulation_grads/pallas_call | solution.py:565
  144.1 2.7 %all-to-all-done.2 = bf16[8,24,576]{2,1,0:T(8,128)(2,1)S(1)} async-done(((bf16[8,24,576]{2,1,0:T(8,128)(2,1)}), bf16[8,24,576]{2,1,0:T(8,128)(2,1)S(1)}, u32[]{:S(2)}, u32[]{:S(2)}) %all-to-all-start.2) | async-done | bytes 221216 | tf_op jit(solution)/shard_map/all_to_all | solution.py:799
  147.7 2.2 %collective-permute-done.43 = bf16[2,2,24,1728]{3,2,1,0:T(8,128)(2,1)S(1)} collective-permute-done((bf16[2,2,24,1728]{3,2,1,0:T(8,128)(2,1)S(1)}, bf16[2,2,24,1728]{3,2,1,0:T(8,128)(2,1)S(1)}, u32[]{:S(2)}, u32[]{:S(2)}) %collective-permute-start.43) | collective-permute-done | bytes 331808 | tf_op jit(solution)/shard_map/ppermute | solution.py:612
  (120 shorter events, 28.8 us)
Async XLA Ops:
  0.6 11.3 %collective-permute-start = (bf16[192,576]{1,0:T(8,128)(2,1)}, bf16[192,576]{1,0:T(8,128)(2,1)S(1)}, u32[]{:S(2)}, u32[]{:S(2)}) collective-permute-start(bf16[192,576]{1,0:T(8,128)(2,1)} %wq0.1), channel_id=1, source_target_pairs={{0,1},{1,0},{2,3},{3,2},{4,5},{5,4},{6,7},{7,6},{8,9},{9,8},{10,11... | collective-permute-start | bytes 663560 | tf_op jit(solution)/shard_map/ppermute | solution.py:588
  3.6 12.3 %collective-permute-start.5 = (bf16[192,576]{1,0:T(8,128)(2,1)}, bf16[192,576]{1,0:T(8,128)(2,1)S(1)}, u32[]{:S(2)}, u32[]{:S(2)}) collective-permute-start(bf16[192,576]{1,0:T(8,128)(2,1)} %wq0.1), channel_id=1, source_target_pairs={{0,2},{2,0},{1,3},{3,1},{4,6},{6,4},{5,7},{7,5},{8,10},{10,8},{9,1... | collective-permute-start | bytes 663560 | tf_op jit(solution)/shard_map/ppermute | solution.py:588
  3.6 8.3 %collective-permute-start.1 = (bf16[192,192]{1,0:T(8,128)(2,1)}, bf16[192,192]{1,0:T(8,128)(2,1)S(1)}, u32[]{:S(2)}, u32[]{:S(2)}) collective-permute-start(bf16[192,192]{1,0:T(8,128)(2,1)} %wp0.1), channel_id=1, source_target_pairs={{0,1},{1,0},{2,3},{3,2},{4,5},{5,4},{6,7},{7,6},{8,9},{9,8},{10,11... | collective-permute-start | bytes 221192 | tf_op jit(solution)/shard_map/ppermute | solution.py:588
  3.8 10.4 %collective-permute-start.7 = (bf16[192,192]{1,0:T(8,128)(2,1)}, bf16[192,192]{1,0:T(8,128)(2,1)S(1)}, u32[]{:S(2)}, u32[]{:S(2)}) collective-permute-start(bf16[192,192]{1,0:T(8,128)(2,1)} %wp0.1), channel_id=1, source_target_pairs={{0,2},{2,0},{1,3},{3,1},{4,6},{6,4},{5,7},{7,5},{8,10},{10,8},{9,1... | collective-permute-start | bytes 221192 | tf_op jit(solution)/shard_map/ppermute | solution.py:588
  14.2 8.5 %collective-permute-start.2 = (bf16[96,1024]{1,0:T(8,128)(2,1)}, bf16[96,1024]{1,0:T(8,128)(2,1)S(1)}, u32[]{:S(2)}, u32[]{:S(2)}) collective-permute-start(bf16[96,1024]{1,0:T(8,128)(2,1)} %get-tuple-element.158), channel_id=1, source_target_pairs={{0,1},{1,0},{2,3},{3,2},{4,5},{5,4},{6,7},{7,6},{8,9},{9,8},{10,11... | collective-permute-start | bytes 589832 | tf_op jit(solution)/shard_map/ppermute | solution.py:592
  15.9 6.8 %collective-permute-start.3 = (bf16[96,1024]{1,0:T(8,128)(2,1)}, bf16[96,1024]{1,0:T(8,128)(2,1)S(1)}, u32[]{:S(2)}, u32[]{:S(2)}) collective-permute-start(bf16[96,1024]{1,0:T(8,128)(2,1)} %get-tuple-element.159), channel_id=1, source_target_pairs={{0,2},{1,3},{2,0},{3,1},{4,6},{5,7},{6,4},{7,5},{8,10},{9,11},{10,... | collective-permute-start | bytes 589832 | tf_op jit(solution)/shard_map/ppermute | solution.py:592
  16.3 9.4 %collective-permute-start.4 = (bf16[96,1024]{1,0:T(8,128)(2,1)}, bf16[96,1024]{1,0:T(8,128)(2,1)S(1)}, u32[]{:S(2)}, u32[]{:S(2)}) collective-permute-start(bf16[96,1024]{1,0:T(8,128)(2,1)} %get-tuple-element.160), channel_id=1, source_target_pairs={{0,3},{1,2},{2,1},{3,0},{4,7},{5,6},{6,5},{7,4},{8,11},{9,10},{10,... | collective-permute-start | bytes 589832 | tf_op jit(solution)/shard_map/ppermute | solution.py:592
  16.3 9.3 %collective-permute-start.6 = (bf16[192,576]{1,0:T(8,128)(2,1)S(1)}, bf16[192,576]{1,0:T(8,128)(2,1)S(1)}, u32[]{:S(2)}, u32[]{:S(2)}) collective-permute-start(bf16[192,576]{1,0:T(8,128)(2,1)S(1)} %collective-permute-done.wq1), channel_id=1, source_target_pairs={{0,2},{2,0},{1,3},{3,1},{4,6},{6,4},{5,7},{7,5},{8,10},{10,8},{9,1... | collective-permute-start | bytes 663560 | tf_op jit(solution)/shard_map/ppermute | solution.py:588
  25.7 15.8 %collective-permute-start.12 = (bf16[192,768]{1,0:T(8,128)(2,1)S(1)}, bf16[192,768]{1,0:T(8,128)(2,1)S(1)}, u32[]{:S(2)}, u32[]{:S(2)}) collective-permute-start(bf16[192,768]{1,0:T(8,128)(2,1)S(1)} %copy-done.2), channel_id=1, source_target_pairs={{0,1},{1,0},{2,3},{3,2},{4,5},{5,4},{6,7},{7,6},{8,9},{9,8},{10,11... | collective-permute-start | bytes 884744 | tf_op jit(solution)/shard_map/ppermute | solution.py:588
  26.2 15.2 %collective-permute-start.14 = (bf16[192,768]{1,0:T(8,128)(2,1)S(1)}, bf16[192,768]{1,0:T(8,128)(2,1)S(1)}, u32[]{:S(2)}, u32[]{:S(2)}) collective-permute-start(bf16[192,768]{1,0:T(8,128)(2,1)S(1)} %copy-done.2), channel_id=1, source_target_pairs={{0,2},{2,0},{1,3},{3,1},{4,6},{6,4},{5,7},{7,5},{8,10},{10,8},{9,1... | collective-permute-start | bytes 884744 | tf_op jit(solution)/shard_map/ppermute | solution.py:588
  26.7 14.7 %collective-permute-start.13 = (bf16[192,768]{1,0:T(8,128)(2,1)S(1)}, bf16[192,768]{1,0:T(8,128)(2,1)S(1)}, u32[]{:S(2)}, u32[]{:S(2)}) collective-permute-start(bf16[192,768]{1,0:T(8,128)(2,1)S(1)} %copy-done.3), channel_id=1, source_target_pairs={{0,1},{1,0},{2,3},{3,2},{4,5},{5,4},{6,7},{7,6},{8,9},{9,8},{10,11... | collective-permute-start | bytes 884744 | tf_op jit(solution)/shard_map/ppermute | solution.py:588
  27.9 13.6 %collective-permute-start.15 = (bf16[192,768]{1,0:T(8,128)(2,1)S(1)}, bf16[192,768]{1,0:T(8,128)(2,1)S(1)}, u32[]{:S(2)}, u32[]{:S(2)}) collective-permute-start(bf16[192,768]{1,0:T(8,128)(2,1)S(1)} %copy-done.3), channel_id=1, source_target_pairs={{0,2},{2,0},{1,3},{3,1},{4,6},{6,4},{5,7},{7,5},{8,10},{10,8},{9,1... | collective-permute-start | bytes 884744 | tf_op jit(solution)/shard_map/ppermute | solution.py:588
  27.9 13.5 %collective-permute-start.16 = (bf16[1,768]{1,0:T(2,128)(2,1)S(1)}, bf16[1,768]{1,0:T(2,128)(2,1)S(1)}, u32[]{:S(2)}, u32[]{:S(2)}) collective-permute-start(bf16[1,768]{1,0:T(2,128)(2,1)S(1)} %reshape.59.b10), channel_id=1, source_target_pairs={{0,1},{1,0},{2,3},{3,2},{4,5},{5,4},{6,7},{7,6},{8,9},{9,8},{10,11... | collective-permute-start | bytes 4616 | tf_op jit(solution)/shard_map/ppermute | solution.py:588
  42.0 10.5 %collective-permute-start.19 = (bf16[96,1024]{1,0:T(8,128)(2,1)S(1)}, bf16[96,1024]{1,0:T(8,128)(2,1)S(1)}, u32[]{:S(2)}, u32[]{:S(2)}) collective-permute-start(bf16[96,1024]{1,0:T(8,128)(2,1)S(1)} %get-tuple-element.210), channel_id=1, source_target_pairs={{0,1},{1,0},{2,3},{3,2},{4,5},{5,4},{6,7},{7,6},{8,9},{9,8},{10,11... | collective-permute-start | bytes 589832 | tf_op jit(solution)/shard_map/ppermute | solution.py:592
  42.9 9.6 %collective-permute-start.20 = (bf16[96,1024]{1,0:T(8,128)(2,1)S(1)}, bf16[96,1024]{1,0:T(8,128)(2,1)S(1)}, u32[]{:S(2)}, u32[]{:S(2)}) collective-permute-start(bf16[96,1024]{1,0:T(8,128)(2,1)S(1)} %get-tuple-element.211), channel_id=1, source_target_pairs={{0,2},{1,3},{2,0},{3,1},{4,6},{5,7},{6,4},{7,5},{8,10},{9,11},{10,... | collective-permute-start | bytes 589832 | tf_op jit(solution)/shard_map/ppermute | solution.py:592
  42.9 9.6 %collective-permute-start.21 = (bf16[96,1024]{1,0:T(8,128)(2,1)S(1)}, bf16[96,1024]{1,0:T(8,128)(2,1)S(1)}, u32[]{:S(2)}, u32[]{:S(2)}) collective-permute-start(bf16[96,1024]{1,0:T(8,128)(2,1)S(1)} %get-tuple-element.212), channel_id=1, source_target_pairs={{0,3},{1,2},{2,1},{3,0},{4,7},{5,6},{6,5},{7,4},{8,11},{9,10},{10,... | collective-permute-start | bytes 589832 | tf_op jit(solution)/shard_map/ppermute | solution.py:592
  52.5 13.0 %collective-permute-start.22 = (bf16[96,1024]{1,0:T(8,128)(2,1)S(1)}, bf16[96,1024]{1,0:T(8,128)(2,1)S(1)}, u32[]{:S(2)}, u32[]{:S(2)}) collective-permute-start(bf16[96,1024]{1,0:T(8,128)(2,1)S(1)} %get-tuple-element.224), channel_id=1, source_target_pairs={{0,1},{1,0},{2,3},{3,2},{4,5},{5,4},{6,7},{7,6},{8,9},{9,8},{10,11... | collective-permute-start | bytes 589832 | tf_op jit(solution)/shard_map/ppermute | solution.py:592
  53.5 12.0 %collective-permute-start.23 = (bf16[96,1024]{1,0:T(8,128)(2,1)S(1)}, bf16[96,1024]{1,0:T(8,128)(2,1)S(1)}, u32[]{:S(2)}, u32[]{:S(2)}) collective-permute-start(bf16[96,1024]{1,0:T(8,128)(2,1)S(1)} %get-tuple-element.225), channel_id=1, source_target_pairs={{0,2},{1,3},{2,0},{3,1},{4,6},{5,7},{6,4},{7,5},{8,10},{9,11},{10,... | collective-permute-start | bytes 589832 | tf_op jit(solution)/shard_map/ppermute | solution.py:592
  53.5 12.0 %collective-permute-start.24 = (bf16[96,1024]{1,0:T(8,128)(2,1)S(1)}, bf16[96,1024]{1,0:T(8,128)(2,1)S(1)}, u32[]{:S(2)}, u32[]{:S(2)}) collective-permute-start(bf16[96,1024]{1,0:T(8,128)(2,1)S(1)} %get-tuple-element.226), channel_id=1, source_target_pairs={{0,3},{1,2},{2,1},{3,0},{4,7},{5,6},{6,5},{7,4},{8,11},{9,10},{10,... | collective-permute-start | bytes 589832 | tf_op jit(solution)/shard_map/ppermute | solution.py:592
  67.9 12.1 %collective-permute-start.26 = (bf16[192,1728]{1,0:T(8,128)(2,1)S(1)}, bf16[192,1728]{1,0:T(8,128)(2,1)S(1)}, u32[]{:S(2)}, u32[]{:S(2)}) collective-permute-start(bf16[192,1728]{1,0:T(8,128)(2,1)S(1)} %get-tuple-element.243), channel_id=1, source_target_pairs={{0,2},{2,0},{1,3},{3,1},{4,6},{6,4},{5,7},{7,5},{8,10},{10,8},{9,1... | collective-permute-start | bytes 1990664 | tf_op jit(solution)/shard_map/ppermute | solution.py:588
  68.1 17.7 %collective-permute-start.27 = (bf16[192,1728]{1,0:T(8,128)(2,1)S(1)}, bf16[192,1728]{1,0:T(8,128)(2,1)S(1)}, u32[]{:S(2)}, u32[]{:S(2)}) collective-permute-start(bf16[192,1728]{1,0:T(8,128)(2,1)S(1)} %add_convert_fusion.1), channel_id=1, source_target_pairs={{0,1},{1,0},{2,3},{3,2},{4,5},{5,4},{6,7},{7,6},{8,9},{9,8},{10,11... | collective-permute-start | bytes 1990664 | tf_op jit(solution)/shard_map/ppermute | solution.py:588
  86.9 25.6 %all-to-all-start = ((bf16[8,24,1728]{2,1,0:T(8,128)(2,1)}), bf16[8,24,1728]{2,1,0:T(8,128)(2,1)}, u32[]{:S(2)}, u32[]{:S(2)}) async-start(bf16[8,24,1728]{2,1,0:T(8,128)(2,1)} %bitcast.33), calls=%async_computation | async-start | bytes 1376256 | tf_op jit(solution)/shard_map/all_to_all | solution.py:618
  95.1 7.7 %collective-permute-start.34 = (bf16[96,1024]{1,0:T(8,128)(2,1)S(1)}, bf16[96,1024]{1,0:T(8,128)(2,1)S(1)}, u32[]{:S(2)}, u32[]{:S(2)}) collective-permute-start(bf16[96,1024]{1,0:T(8,128)(2,1)S(1)} %get-tuple-element.261), channel_id=1, source_target_pairs={{0,1},{1,0},{2,3},{3,2},{4,5},{5,4},{6,7},{7,6},{8,9},{9,8},{10,11... | collective-permute-start | bytes 589832 | tf_op jit(solution)/shard_map/ppermute | solution.py:592
  97.0 8.9 %collective-permute-start.36 = (bf16[96,1024]{1,0:T(8,128)(2,1)S(1)}, bf16[96,1024]{1,0:T(8,128)(2,1)S(1)}, u32[]{:S(2)}, u32[]{:S(2)}) collective-permute-start(bf16[96,1024]{1,0:T(8,128)(2,1)S(1)} %get-tuple-element.263), channel_id=1, source_target_pairs={{0,3},{1,2},{2,1},{3,0},{4,7},{5,6},{6,5},{7,4},{8,11},{9,10},{10,... | collective-permute-start | bytes 589832 | tf_op jit(solution)/shard_map/ppermute | solution.py:592
  98.2 13.5 %collective-permute-start.28 = (bf16[192,576]{1,0:T(8,128)(2,1)S(1)}, bf16[192,576]{1,0:T(8,128)(2,1)S(1)}, u32[]{:S(2)}, u32[]{:S(2)}) collective-permute-start(bf16[192,576]{1,0:T(8,128)(2,1)S(1)} %get-tuple-element.250), channel_id=1, source_target_pairs={{0,2},{2,0},{1,3},{3,1},{4,6},{6,4},{5,7},{7,5},{8,10},{10,8},{9,1... | collective-permute-start | bytes 663560 | tf_op jit(solution)/shard_map/ppermute | solution.py:588
  98.2 13.5 %collective-permute-start.30 = (bf16[192,576]{1,0:T(8,128)(2,1)S(1)}, bf16[192,576]{1,0:T(8,128)(2,1)S(1)}, u32[]{:S(2)}, u32[]{:S(2)}) collective-permute-start(bf16[192,576]{1,0:T(8,128)(2,1)S(1)} %add_convert_fusion.3), channel_id=1, source_target_pairs={{0,1},{1,0},{2,3},{3,2},{4,5},{5,4},{6,7},{7,6},{8,9},{9,8},{10,11... | collective-permute-start | bytes 663560 | tf_op jit(solution)/shard_map/ppermute | solution.py:588
  112.6 20.0 %all-to-all-start.1 = ((bf16[8,24,576]{2,1,0:T(8,128)(2,1)}), bf16[8,24,576]{2,1,0:T(8,128)(2,1)S(1)}, u32[]{:S(2)}, u32[]{:S(2)}) async-start(bf16[8,24,576]{2,1,0:T(8,128)(2,1)} %bitcast.6), calls=%async_computation.1 | async-start | bytes 491520 | tf_op jit(solution)/shard_map/all_to_all | solution.py:618
  121.1 11.3 %collective-permute-start.39 = (bf16[24,1728]{1,0:T(8,128)(2,1)S(1)}, bf16[24,1728]{1,0:T(8,128)(2,1)S(1)}, u32[]{:S(2)}, u32[]{:S(2)}) collective-permute-start(bf16[24,1728]{1,0:T(8,128)(2,1)S(1)} %reduce_sum.24), channel_id=1, source_target_pairs={{0,16},{4,20},{8,24},{12,28},{16,0},{20,4},{24,8},{28,12},{1,17},{... | collective-permute-start | bytes 248840 | tf_op jit(solution)/shard_map/ppermute | solution.py:612
  124.1 8.3 %collective-permute-start.40 = (bf16[2,128,192]{2,1,0:T(8,128)(2,1)S(1)}, bf16[2,128,192]{2,1,0:T(8,128)(2,1)S(1)}, u32[]{:S(2)}, u32[]{:S(2)}) collective-permute-start(bf16[2,128,192]{2,1,0:T(8,128)(2,1)S(1)} %pad_maximum_fusion.5), channel_id=1, source_target_pairs={{0,8},{4,12},{8,0},{12,4},{16,24},{20,28},{24,16},{28,20},{1,9},{5... | collective-permute-start | bytes 294920 | tf_op jit(solution)/shard_map/ppermute | solution.py:612
  132.6 8.1 %collective-permute-start.41 = (bf16[4,128,192]{2,1,0:T(8,128)(2,1)S(1)}, bf16[4,128,192]{2,1,0:T(8,128)(2,1)S(1)}, u32[]{:S(2)}, u32[]{:S(2)}) collective-permute-start(bf16[4,128,192]{2,1,0:T(8,128)(2,1)S(1)} %pad_maximum_fusion.3), channel_id=1, source_target_pairs={{0,4},{4,0},{8,12},{12,8},{16,20},{20,16},{24,28},{28,24},{1,5},{5... | collective-permute-start | bytes 589832 | tf_op jit(solution)/shard_map/ppermute | solution.py:612
  134.9 11.9 %all-to-all-start.2 = ((bf16[8,24,576]{2,1,0:T(8,128)(2,1)}), bf16[8,24,576]{2,1,0:T(8,128)(2,1)S(1)}, u32[]{:S(2)}, u32[]{:S(2)}) async-start(bf16[8,24,576]{2,1,0:T(8,128)(2,1)} %broadcast_in_dim.10), calls=%async_computation.2 | async-start | bytes 491520 | tf_op jit(solution)/shard_map/all_to_all | solution.py:799
  138.7 11.2 %collective-permute-start.43 = (bf16[2,2,24,1728]{3,2,1,0:T(8,128)(2,1)S(1)}, bf16[2,2,24,1728]{3,2,1,0:T(8,128)(2,1)S(1)}, u32[]{:S(2)}, u32[]{:S(2)}) collective-permute-start(bf16[2,2,24,1728]{3,2,1,0:T(8,128)(2,1)S(1)} %pad_maximum_fusion.2), channel_id=1, source_target_pairs={{0,4},{4,0},{8,12},{12,8},{16,20},{20,16},{24,28},{28,24},{1,5},{5... | collective-permute-start | bytes 995336 | tf_op jit(solution)/shard_map/ppermute | solution.py:612
  (27 other events, 236.9 us)
